TPU v7x, 128 devices: a whole 4x4x4 slice. The times are simulated.
128 devices in a mesh: row: 16 (over y, z), col: 8 (over x, core).
Axes of the slice: x: 4, y: 4, z: 4, core: 2. Of those that a mesh axis runs over, the one named last changes fastest.
Arguments:
- clips: bfloat16 [8192, 768], P('row', 'col'), may hold values from -512 to 512
- captions: bfloat16 [16384, 768], P('col', 'row'), may hold values from -32 to 32
- caption_owner: int32 [16384], P('col'), may hold values from 0 to 8191, as said below
Outputs:
- loss: float32 [], replicated
- clip_grad: float32 [8192, 768], P(('row', 'col'))
- caption_grad: float32 [16384, 768], P(('col', 'row'))
Inputs may be any that keep to these rules, and one draw needn't show every extreme that they name: `caption_owner`: each clip index is named by exactly two captions.
All inputs are finite; a program needn't handle non-finite values.
Results may differ from a plain program's by a relative error of at most 0.00105.
The roundings to bfloat16 on the way count: a program that leaves them out, or rounds other values in their place, can miss the bound.
Values may be sent and summed in bfloat16 or wider, within the bound.
No kernel may reach another device: no remote copies, remote signals or barrier semaphores. Data moves between devices by JAX's collectives and lax.ppermute only.
A program may use at most 64 MiB of HBM per device.

v0:
```python
import math

import jax
import jax.numpy as jnp
from jax import lax
from jax.sharding import PartitionSpec as P

ROUNDS = 3


diagonal_increment = 4.0
midway_portion = math.log(0.5)


def pair_logits(clip_side, caption_side):
    return lax.dot_general(
        clip_side, caption_side, (((1,), (1,)), ((), ())), preferred_element_type=jnp.float32
    )


def across_col(maxima, totals):
    larger = lax.pmax(maxima, "col")
    totals = lax.psum(totals * jnp.exp(maxima - larger), "col")
    maxima = larger
    return maxima + jnp.log(totals)


def across_row(maxima, totals):
    larger = lax.pmax(maxima, "row")
    totals = lax.psum(totals * jnp.exp(maxima - larger), "row")
    maxima = larger
    return maxima + jnp.log(totals)


def body(clips, captions, caption_owner):
    clip_count = clips.shape[0]
    caption_count = captions.shape[0]
    total_clips = clip_count * lax.axis_size("row")
    total_captions = caption_count * lax.axis_size("col")
    clip_full = lax.all_gather(clips, "col", axis=1, tiled=True)
    caption_full = lax.all_gather(captions, "row", axis=1, tiled=True)
    logit_scale = 1.0 / math.sqrt(caption_full.shape[1])
    video_index_list = lax.axis_index("row") * clip_count + jnp.arange(clip_count, dtype=jnp.int32)
    block_cols = min(512, caption_count)
    block_count = caption_count // block_cols

    def fetch_submatrix(iteration_counter):
        displacement = iteration_counter * block_cols
        caption_block = lax.dynamic_slice_in_dim(caption_full, displacement, block_cols, 0)
        caption_holders = lax.dynamic_slice_in_dim(caption_owner, displacement, block_cols, 0)
        cosine_affinity = pair_logits(clip_full, caption_block) * logit_scale
        raised_affinity = cosine_affinity + diagonal_increment * (
            caption_holders[None, :] == video_index_list[:, None]
        ).astype(jnp.float32)
        return (displacement, cosine_affinity, raised_affinity)

    def row_pass(vertical_dual_potential, with_plain):
        stat_count = 2 if with_plain else 1

        def row_advance(iteration_counter, accumulating_state):
            maxima, totals = accumulating_state
            displacement, cosine_affinity, raised_affinity = fetch_submatrix(iteration_counter)
            potential_piece = lax.dynamic_slice_in_dim(
                vertical_dual_potential, displacement, block_cols, 0
            )
            entries_array = [raised_affinity + potential_piece[None, :]]
            if with_plain:
                entries_array.append(cosine_affinity)
            block_max = jnp.stack([jnp.max(member, axis=1) for member in entries_array])
            larger = jnp.maximum(maxima, block_max)
            block_sum = jnp.stack(
                [
                    jnp.sum(jnp.exp(member - larger[position][:, None]), axis=1)
                    for position, member in enumerate(entries_array)
                ]
            )
            return (larger, totals * jnp.exp(maxima - larger) + block_sum)

        start_state = (
            jnp.full((stat_count, clip_count), -jnp.inf, dtype=jnp.float32),
            jnp.zeros((stat_count, clip_count), dtype=jnp.float32),
        )
        maxima, totals = lax.fori_loop(0, block_count, row_advance, start_state)
        return across_col(maxima, totals)

    def col_pass(horizontal_dual_potential, with_plain):
        stat_count = 2 if with_plain else 1

        def col_advance(iteration_counter, accumulating_state):
            maxima, totals = accumulating_state
            displacement, cosine_affinity, raised_affinity = fetch_submatrix(iteration_counter)
            entries_array = [raised_affinity + horizontal_dual_potential[:, None]]
            if with_plain:
                entries_array.append(cosine_affinity)
            block_max = jnp.stack([jnp.max(member, axis=0) for member in entries_array])
            block_sum = jnp.stack(
                [
                    jnp.sum(jnp.exp(member - block_max[position][None, :]), axis=0)
                    for position, member in enumerate(entries_array)
                ]
            )
            maxima = lax.dynamic_update_slice_in_dim(maxima, block_max, displacement, 1)
            totals = lax.dynamic_update_slice_in_dim(totals, block_sum, displacement, 1)
            return (maxima, totals)

        start_state = (
            jnp.zeros((stat_count, caption_count), dtype=jnp.float32),
            jnp.zeros((stat_count, caption_count), dtype=jnp.float32),
        )
        maxima, totals = lax.fori_loop(0, block_count, col_advance, start_state)
        return across_row(maxima, totals)

    vertical_dual_potential = jnp.zeros((caption_count,), dtype=jnp.float32)
    horizontal_dual_potential = jnp.zeros((clip_count,), dtype=jnp.float32)
    col_lse = jnp.zeros((caption_count,), dtype=jnp.float32)
    for sweep_index in range(ROUNDS):
        horizontal_dual_potential = -row_pass(vertical_dual_potential, False)[0]
        column_stats = col_pass(horizontal_dual_potential, sweep_index == 0)
        if sweep_index == 0:
            col_lse = column_stats[1]
        vertical_dual_potential = midway_portion - column_stats[0]
    final_stats = row_pass(vertical_dual_potential, True)
    horizontal_normalizer = final_stats[0]
    row_lse = final_stats[1]

    def gradient_block(iteration_counter, accumulating_state):
        slope_all, loss_acc = accumulating_state
        displacement, cosine_affinity, raised_affinity = fetch_submatrix(iteration_counter)
        potential_piece = lax.dynamic_slice_in_dim(
            vertical_dual_potential, displacement, block_cols, 0
        )
        lse_block = lax.dynamic_slice_in_dim(col_lse, displacement, block_cols, 0)
        horizontal_marginal = jnp.exp(
            raised_affinity + potential_piece[None, :] - horizontal_normalizer[:, None]
        )
        vertical_marginal = jnp.exp(
            raised_affinity
            + horizontal_dual_potential[:, None]
            + (potential_piece - midway_portion)[None, :]
        )
        loss_part = jnp.sum(horizontal_marginal * (row_lse[:, None] - cosine_affinity)) / (
            2.0 * total_clips
        )
        loss_part = loss_part + jnp.sum(
            vertical_marginal * (lse_block[None, :] - cosine_affinity)
        ) / (2.0 * total_captions)
        slope_bfloat_copy = (
            jnp.exp(cosine_affinity - row_lse[:, None])
            - horizontal_marginal
            + 0.5 * (jnp.exp(cosine_affinity - lse_block[None, :]) - vertical_marginal)
        ).astype(jnp.bfloat16)
        slope_all = lax.dynamic_update_slice_in_dim(slope_all, slope_bfloat_copy, displacement, 1)
        return (slope_all, loss_acc + loss_part)

    start_state = (
        jnp.zeros((clip_count, caption_count), dtype=jnp.bfloat16),
        jnp.zeros((), dtype=jnp.float32),
    )
    slope_all, loss_local = lax.fori_loop(0, block_count, gradient_block, start_state)
    loss = lax.psum(loss_local, ("row", "col"))
    clip_share = clip_count // lax.axis_size("col")
    caption_share = caption_count // lax.axis_size("row")
    clip_term = jnp.dot(slope_all, caption_full, preferred_element_type=jnp.float32)
    clip_summed = lax.psum(clip_term, "col")
    clip_grad = lax.dynamic_slice_in_dim(
        clip_summed, lax.axis_index("col") * clip_share, clip_share, 0
    )
    caption_term = lax.dot_general(
        slope_all, clip_full, (((0,), (0,)), ((), ())), preferred_element_type=jnp.float32
    )
    caption_summed = lax.psum(caption_term, "row")
    caption_grad = lax.dynamic_slice_in_dim(
        caption_summed, lax.axis_index("row") * caption_share, caption_share, 0
    )
    return (loss, clip_grad, caption_grad)


def solution(mesh):
    in_specs = (P("row", "col"), P("col", "row"), P("col"))
    out_specs = (P(), P(("row", "col"), None), P(("col", "row"), None))
    return jax.shard_map(body, mesh=mesh, in_specs=in_specs, out_specs=out_specs, check_vma=False)
```

profile of v0, /device:TPU:8, one launch (start us, length us, event | category | flops | bytes accessed | tf_op | source)
XLA Modules:
  0.0 739.9 jit_solution(1269792395015277316)
XLA Ops:
  8.0 13.9 %all_gather.7 = bf16[512,768]{0,1:T(8,128)(2,1)S(1)} all-gather(bf16[512,96]{0,1:T(8,128)(2,1)} %param.19), channel_id=1, replica_groups=mesh['row'=16,'col'=8] {'col'}, dimensions={1}, use_global_device_ids=true | all-gather | bytes 884736 | tf_op jit(solution)/shard_map/all_gather | solution.py:40
  22.3 37.6 %all-gather.2.cloned.1.call-done = bf16[2048,768]{0,1:T(8,128)(2,1)} async-done(((bf16[2048,48]{0,1:T(8,128)(2,1)}), bf16[2048,768]{0,1:T(8,128)(2,1)}) %all-gather.2.cloned.1.call-update) | async-done | bytes 3145744 | tf_op jit(solution)/shard_map/all_gather | solution.py:41
  59.9 4.7 copy.22
  64.6 8.4 %while.134 = (s32[]{:T(128)}, f32[1,512]{1,0:T(1,128)S(1)}, f32[1,512]{1,0:T(1,128)S(1)}, bf16[2048,768]{1,0:T(8,128)(2,1)}, bf16[512,768]{1,0:T(8,128)(2,1)S(1)...) while((s32[]{:T(128)}, f32[1,512]{1,0:T(1,128)S(1)}, ...), condition=%wide.region_3.0_spmd.clone, body=%wide.region_0.0_spmd.clone.sunk | while | flops 404491264 | bytes 3707066 | solution.py:83
  72.9 14.1 %pmax.49 = f32[1,512]{1,0:T(1,128)S(1)} all-reduce(f32[1,512]{1,0:T(1,128)S(1)} %get-tuple-element.1255), channel_id=1, replica_groups=mesh['row'=16,'col'=8] {'col'}, use_global_device_ids=true, to_apply=%region_4.0 | all-reduce | flops 512 | bytes 4096 | tf_op jit(solution)/shard_map/pmax | solution.py:22
  87.1 12.4 %psum.70 = f32[1,512]{1,0:T(1,128)S(1)} all-reduce(f32[1,512]{1,0:T(1,128)S(1)} %exponential_multiply_fusion.6), channel_id=1, replica_groups=mesh['row'=16,'col'=8] {'col'}, use_global_device_ids=true, to_apply=%region_5.0 | all-reduce | flops 512 | bytes 4096 | tf_op jit(solution)/shard_map/psum | solution.py:23
  99.6 10.4 %while.130 = (s32[]{:T(128)}, f32[2,2048]{1,0:T(2,128)S(1)}, f32[2,2048]{1,0:T(2,128)S(1)}, bf16[2048,768]{1,0:T(8,128)(2,1)}, bf16[512,768]{1,0:T(8,128)(2,1)S(...) while((s32[]{:T(128)}, f32[2,2048]{1,0:T(2,128)S(1)}, ...), condition=%wide.region_11.0_spmd.clone, body=%wide.region_6.0_spmd.clone.sunk | while | flops 406585856 | bytes 4765875 | solution.py:110
  110.0 66.9 %pmax.50 = f32[2,2048]{1,0:T(2,128)S(1)} all-reduce(f32[2,2048]{1,0:T(2,128)S(1)} %get-tuple-element.1257), channel_id=1, replica_groups=mesh['row'=16,'col'=8] {'row'}, use_global_device_ids=true, to_apply=%region_12.0 | all-reduce | flops 4096 | bytes 32768 | tf_op jit(solution)/shard_map/pmax | solution.py:29
  176.9 69.5 %psum.71 = f32[2,2048]{1,0:T(2,128)S(1)} all-reduce(f32[2,2048]{1,0:T(2,128)S(1)} %exponential_multiply_fusion), channel_id=1, replica_groups=mesh['row'=16,'col'=8] {'row'}, use_global_device_ids=true, to_apply=%region_13.0 | all-reduce | flops 4096 | bytes 32768 | tf_op jit(solution)/shard_map/psum | solution.py:30
  246.5 8.8 %while.135 = (s32[]{:T(128)}, f32[1,512]{1,0:T(1,128)S(1)}, f32[1,512]{1,0:T(1,128)S(1)}, bf16[2048,768]{1,0:T(8,128)(2,1)}, bf16[512,768]{1,0:T(8,128)(2,1)S(1)...) while((s32[]{:T(128)}, f32[1,512]{1,0:T(1,128)S(1)}, ...), condition=%wide.region_17.0_spmd.clone, body=%wide.region_14.0_spmd.clone.sunk | while | flops 404753408 | bytes 3713222 | solution.py:83
  255.3 12.4 %pmax.51 = f32[1,512]{1,0:T(1,128)S(1)} all-reduce(f32[1,512]{1,0:T(1,128)S(1)} %get-tuple-element.1259), channel_id=1, replica_groups=mesh['row'=16,'col'=8] {'col'}, use_global_device_ids=true, to_apply=%region_18.0 | all-reduce | flops 512 | bytes 4096 | tf_op jit(solution)/shard_map/pmax | solution.py:22
  267.7 12.4 %psum.72 = f32[1,512]{1,0:T(1,128)S(1)} all-reduce(f32[1,512]{1,0:T(1,128)S(1)} %exponential_multiply_fusion.5), channel_id=1, replica_groups=mesh['row'=16,'col'=8] {'col'}, use_global_device_ids=true, to_apply=%region_19.0 | all-reduce | flops 512 | bytes 4096 | tf_op jit(solution)/shard_map/psum | solution.py:23
  280.2 8.4 %while.131 = (s32[]{:T(128)}, f32[1,2048]{1,0:T(1,128)S(1)}, f32[1,2048]{1,0:T(1,128)S(1)}, bf16[2048,768]{1,0:T(8,128)(2,1)}, bf16[512,768]{1,0:T(8,128)(2,1)S(...) while((s32[]{:T(128)}, f32[1,2048]{1,0:T(1,128)S(1)}, ...), condition=%wide.region_23.0_spmd.clone, body=%wide.region_20.0_spmd.clone.sunk | while | flops 404749824 | bytes 3696819 | solution.py:110
  288.6 36.0 %pmax.52 = f32[1,2048]{1,0:T(1,128)S(1)} all-reduce(f32[1,2048]{1,0:T(1,128)S(1)} %get-tuple-element.1261), channel_id=1, replica_groups=mesh['row'=16,'col'=8] {'row'}, use_global_device_ids=true, to_apply=%region_24.0 | all-reduce | flops 2048 | bytes 16384 | tf_op jit(solution)/shard_map/pmax | solution.py:29
  324.6 38.0 %psum.73 = f32[1,2048]{1,0:T(1,128)S(1)} all-reduce(f32[1,2048]{1,0:T(1,128)S(1)} %exponential_multiply_fusion.2), channel_id=1, replica_groups=mesh['row'=16,'col'=8] {'row'}, use_global_device_ids=true, to_apply=%region_25.0 | all-reduce | flops 2048 | bytes 16384 | tf_op jit(solution)/shard_map/psum | solution.py:30
  362.6 8.8 %while.136 = (s32[]{:T(128)}, f32[1,512]{1,0:T(1,128)S(1)}, f32[1,512]{1,0:T(1,128)S(1)}, bf16[2048,768]{1,0:T(8,128)(2,1)}, bf16[512,768]{1,0:T(8,128)(2,1)S(1)...) while((s32[]{:T(128)}, f32[1,512]{1,0:T(1,128)S(1)}, ...), condition=%wide.region_29.0_spmd.clone, body=%wide.region_26.0_spmd.clone.sunk | while | flops 404753408 | bytes 3713222 | solution.py:83
  371.5 12.4 %pmax.53 = f32[1,512]{1,0:T(1,128)S(1)} all-reduce(f32[1,512]{1,0:T(1,128)S(1)} %get-tuple-element.1263), channel_id=1, replica_groups=mesh['row'=16,'col'=8] {'col'}, use_global_device_ids=true, to_apply=%region_30.0 | all-reduce | flops 512 | bytes 4096 | tf_op jit(solution)/shard_map/pmax | solution.py:22
  383.9 12.4 %psum.74 = f32[1,512]{1,0:T(1,128)S(1)} all-reduce(f32[1,512]{1,0:T(1,128)S(1)} %exponential_multiply_fusion.4), channel_id=1, replica_groups=mesh['row'=16,'col'=8] {'col'}, use_global_device_ids=true, to_apply=%region_31.0 | all-reduce | flops 512 | bytes 4096 | tf_op jit(solution)/shard_map/psum | solution.py:23
  396.4 8.4 %while.132 = (s32[]{:T(128)}, f32[1,2048]{1,0:T(1,128)S(1)}, f32[1,2048]{1,0:T(1,128)S(1)}, bf16[2048,768]{1,0:T(8,128)(2,1)}, bf16[512,768]{1,0:T(8,128)(2,1)S(...) while((s32[]{:T(128)}, f32[1,2048]{1,0:T(1,128)S(1)}, ...), condition=%wide.region_35.0_spmd.clone, body=%wide.region_32.0_spmd.clone.sunk | while | flops 404749824 | bytes 3696819 | solution.py:110
  404.8 36.0 %pmax.54 = f32[1,2048]{1,0:T(1,128)S(1)} all-reduce(f32[1,2048]{1,0:T(1,128)S(1)} %get-tuple-element.1265), channel_id=1, replica_groups=mesh['row'=16,'col'=8] {'row'}, use_global_device_ids=true, to_apply=%region_36.0 | all-reduce | flops 2048 | bytes 16384 | tf_op jit(solution)/shard_map/pmax | solution.py:29
  440.8 38.0 %psum.75 = f32[1,2048]{1,0:T(1,128)S(1)} all-reduce(f32[1,2048]{1,0:T(1,128)S(1)} %exponential_multiply_fusion.1), channel_id=1, replica_groups=mesh['row'=16,'col'=8] {'row'}, use_global_device_ids=true, to_apply=%region_37.0 | all-reduce | flops 2048 | bytes 16384 | tf_op jit(solution)/shard_map/psum | solution.py:30
  478.8 10.9 %while.137 = (s32[]{:T(128)}, f32[2,512]{1,0:T(2,128)S(1)}, f32[2,512]{1,0:T(2,128)S(1)}, bf16[2048,768]{1,0:T(8,128)(2,1)}, bf16[512,768]{1,0:T(8,128)(2,1)S(1)...) while((s32[]{:T(128)}, f32[2,512]{1,0:T(2,128)S(1)}, ...), condition=%wide.region_43.0_spmd.clone, body=%wide.region_38.0_spmd.clone.sunk | while | flops 406595072 | bytes 4802758 | solution.py:83
  489.7 12.4 %pmax.55 = f32[2,512]{1,0:T(2,128)S(1)} all-reduce(f32[2,512]{1,0:T(2,128)S(1)} %get-tuple-element.1267), channel_id=1, replica_groups=mesh['row'=16,'col'=8] {'col'}, use_global_device_ids=true, to_apply=%region_44.0 | all-reduce | flops 1024 | bytes 8192 | tf_op jit(solution)/shard_map/pmax | solution.py:22
  502.2 12.6 %psum.76 = f32[2,512]{1,0:T(2,128)S(1)} all-reduce(f32[2,512]{1,0:T(2,128)S(1)} %exponential_multiply_fusion.3), channel_id=1, replica_groups=mesh['row'=16,'col'=8] {'col'}, use_global_device_ids=true, to_apply=%region_45.0 | all-reduce | flops 1024 | bytes 8192 | tf_op jit(solution)/shard_map/psum | solution.py:23
  514.9 22.6 %while.133 = (s32[]{:T(128)}, bf16[512,2048]{0,1:T(8,128)(2,1)S(1)}, f32[]{:T(128)}, bf16[2048,768]{1,0:T(8,128)(2,1)}, bf16[512,768]{1,0:T(8,128)(2,1)}, /*inde...) while((s32[]{:T(128)}, bf16[512,2048]{0,1:T(8,128)(2,1)S(1)}, ...), condition=%wide.region_49.0_spmd.clone, body=%wide.region_46.0_spmd.clone.sunk | while | flops 409994240 | bytes 4244763 | solution.py:159
  515.2 2.6 fusion.122
  520.8 2.6 fusion.122
  532.1 2.6 fusion.122
  537.5 4.9 fusion.75
  542.5 4.5 fusion.76
  547.0 69.6 %psum.77 = f32[]{:T(128)} all-reduce(f32[]{:T(128)} %get-tuple-element.1269), channel_id=1, replica_groups=mesh['row'=16,'col'=8] {'row','col'}, use_global_device_ids=true, to_apply=%region_50.0 | all-reduce | flops 1 | bytes 8 | tf_op jit(solution)/shard_map/psum | solution.py:160
  618.3 113.2 %all-reduce.5.cloned.1.call-done = f32[2048,768]{1,0:T(8,128)} async-done(((f32[2048,768]{1,0:T(8,128)}), f32[2048,768]{1,0:T(8,128)}) %all-reduce.5.cloned.1.call-update) | async-done | bytes 6291472 | tf_op jit(solution)/shard_map/psum | solution.py:171
  (262 shorter events, 77.6 us)
Async XLA Ops:
  7.2 52.7 %all-gather.2.cloned.1.call-start = ((), (), s32[]{:S(2)}) async-start(), calls=%async_computation | async-start | bytes 3342336 | tf_op jit(solution)/shard_map/all_gather | solution.py:41
  7.9 608.7 %all-reduce.3.cloned.1.call-start = ((), (), s32[]{:S(2)}) async-start(), calls=%async_computation.1 | async-start | bytes 3145728 | tf_op jit(solution)/shard_map/psum | solution.py:164
  22.3 42.3 %copy-start = (s32[2048]{0:T(1024)S(1)}, s32[2048]{0:T(1024)}, u32[]{:S(2)}) copy-start(s32[2048]{0:T(1024)} %param.21) | copy-start | bytes 24580
  489.7 25.1 %copy-start.1 = (bf16[512,768]{1,0:T(8,128)(2,1)}, bf16[512,768]{1,0:T(8,128)(2,1)S(1)}, u32[]{:S(2)}) copy-start(bf16[512,768]{1,0:T(8,128)(2,1)S(1)} %get-tuple-element.2514) | copy-start | bytes 2359300
  542.5 189.1 %all-reduce.5.cloned.1.call-start = ((), (), s32[]{:S(2)}) async-start(), calls=%async_computation.2 | async-start | bytes 12582912 | tf_op jit(solution)/shard_map/psum | solution.py:171
Sparse Core Ops, SparseCore 0:
  10.2 49.6 all-gather.1
  542.6 63.7 all-reduce.2
  609.8 121.7 all-reduce.4
where the time goes:
time: 743 us; the launch traced here: 740 us
  blocking collectives  469 us (63%)
  waiting for transfers between devices  152 us (20%)
  matrix products  69.3 us (9%)
  other arithmetic  16.9 us (2%)
  between operations  14.1 us (2%)
  local copies, waits for them, and re-layouts  12.5 us (2%)
    psum x3, blocking collectives, across_row(): totals = lax.psum(totals * jnp.exp(maxima - larger), 'row')  146 us
    pmax x3, blocking collectives, across_row(): larger = lax.pmax(maxima, 'row')  139 us
    psum x1, waiting for transfers between devices, body(): caption_summed = lax.psum(caption_term, 'row')  113 us
    psum x1, blocking collectives, body(): loss = lax.psum(loss_local, ('row', 'col'))  69.6 us
    dot_general x32, matrix products, pair_logits(): lax.dot_general(clip_side, caption_side, (((1,), (1,)), ((), ())), prefer...  59.9 us
    pmax x4, blocking collectives, across_col(): larger = lax.pmax(maxima, 'col')  51.4 us
    psum x4, blocking collectives, across_col(): totals = lax.psum(totals * jnp.exp(maxima - larger), 'col')  49.9 us
    all_gather x1, waiting for transfers between devices, body(): caption_full = lax.all_gather(captions, 'row', axis=1, tiled=True)  37.6 us
  transfers between devices with their start and end apart: 3, of which 2 were waited for; matrix products, arithmetic and copies ran while one was open for 1% of the time, Pallas kernels for 0%

commit v1 on v0

v1 whole, which is shorter than its diff:
```python
import math

import jax
import jax.numpy as jnp
from jax import lax
from jax.experimental import pallas as pl
from jax.experimental.pallas import tpu as pltpu
from jax.sharding import PartitionSpec as P

BOOST = 4.0
HALF_LOG = math.log(0.5)
WIDTH = 768
ROWS = 512
COLS = 2048
LANES = 128
TILES = COLS // LANES
SIDE = 4
CLIP_PIECE = 96
CAPTION_PIECE = 48
EXTRA = 16
PACKED = WIDTH + EXTRA
AWAY = (0, 1, 3, 2)
F32 = jnp.float32
BF16 = jnp.bfloat16

VM = pl.BlockSpec(memory_space=pltpu.VMEM)
SM = pl.BlockSpec(memory_space=pltpu.SMEM)


def call(
    kernel, args, outs, name, scratch=(), smem=0, limit=8, flops=0, moved=0, exps=0, specs=None, grid=()
):
    return pl.pallas_call(
        kernel,
        grid=grid,
        out_shape=outs,
        in_specs=specs or [SM] * smem + [VM] * (len(args) - smem),
        out_specs=[VM] * len(outs),
        scratch_shapes=list(scratch),
        compiler_params=pltpu.CompilerParams(vmem_limit_bytes=limit * 2**20),
        cost_estimate=pl.CostEstimate(flops=flops, bytes_accessed=moved, transcendentals=exps),
        name=name,
    )(*args)


def shape(dims, kind=F32):
    return jax.ShapeDtypeStruct(dims, kind)


def row_shift(value, step_y, step_z):
    pairs = [
        (y * SIDE + z, ((y + step_y) % SIDE) * SIDE + (z + step_z) % SIDE)
        for y in range(SIDE)
        for z in range(SIDE)
    ]
    return lax.ppermute(value, "row", pairs)


def col_shift(value, step_x, flip):
    pairs = [
        (x * 2 + k, ((x + step_x) % SIDE) * 2 + (k ^ flip)) for x in range(SIDE) for k in range(2)
    ]
    return lax.ppermute(value, "col", pairs)


AWAY = (0, 1, 3, 2)


def col_all(copies):
    return lax.all_to_all(copies, "col", 0, 0, tiled=True)


def row_all(copies):
    return lax.all_to_all(copies, "row", 0, 0, tiled=True)


def swap(value, bits):
    return lax.ppermute(value, "col", [(c, c ^ bits) for c in range(8)])


def along_z(values):
    return [values[0]] + [row_shift(v, 0, d) for v, d in zip(values[1:], AWAY[1:])]


def along_y(values):
    return [values[0]] + [row_shift(v, d, 0) for v, d in zip(values[1:], AWAY[1:])]


def down(line):
    return jnp.transpose(jnp.broadcast_to(line, (LANES, line.shape[1])))


def along(block):
    return jnp.sum(jnp.transpose(block), axis=0, keepdims=True)


def copy_out(sums, value):
    for k in range(sums.shape[0]):
        sums[k] = value


def integers(packed):
    return packed.astype(jnp.int32).astype(F32)


def scale_of(steps):
    return jnp.exp2(steps * (1 / 64)) * (1 / 32000)


def steps_of(peak):
    return jnp.ceil(jnp.log2(jnp.maximum(peak, 1e-30)) * 64.0)


def halfwords(numbers):
    return jnp.round(numbers).astype(jnp.int32).astype(jnp.int16)


def widen(packed):
    rows = packed.shape[0] - EXTRA
    tail = integers(packed[rows:])
    share = (tail[2:3] + tail[3:4] * 2.0**-14) * scale_of(tail[1:2])
    return integers(packed[0:rows]) * scale_of(tail[0:1]), share


ZERO = 0.0


def narrow(value, share, out, start):
    rows, lanes = value.shape
    steps = steps_of(jnp.max(jnp.abs(value), axis=0, keepdims=True))
    out[start : start + rows] = halfwords(value * (1.0 / scale_of(steps)))
    share = share + jnp.zeros((1, lanes), F32)
    share_steps = steps_of(jnp.abs(share))
    scaled = share * (1.0 / scale_of(share_steps))
    high = jnp.round(scaled)
    low = (scaled - high) * 2.0**14
    row = lax.broadcasted_iota(jnp.int32, (EXTRA, lanes), 0)
    tail = jnp.where(
        row == 0, steps, jnp.where(row == 1, share_steps, jnp.where(row == 2, high, low))
    )
    out[start + rows : start + rows + EXTRA] = halfwords(tail)


def gathered(parts):
    total = parts[0]
    for k in range(1, parts.shape[0]):
        total += parts[k]
    return total


def joined(lses):
    peak = jnp.max(lses, axis=0, keepdims=True)
    return peak + jnp.log(jnp.sum(jnp.exp(lses - peak), axis=0, keepdims=True))


def tile(t):
    return slice(t * LANES, (t + 1) * LANES)


def row_chunks(step, body):
    def run(i, carry):
        body(pl.ds(pl.multiple_of(i * step, step), step))
        return carry

    lax.fori_loop(0, ROWS // step, run, 0)


def local_kernel(captions, clips, beside, captions_out, clips_out):
    captions_out[...] = captions[...]
    clips_out[0:CLIP_PIECE] = clips[...]
    clips_out[CLIP_PIECE:] = beside[...]


def join_kernel(*refs):
    parts, out = refs[:-1], refs[-1]
    for k, part in enumerate(parts):
        out[:, k * COLS : (k + 1) * COLS] = part[...]


def join(parts):
    dims = (CAPTION_PIECE, len(parts) * COLS)
    return call(join_kernel, parts, [shape(dims, BF16)], "join", moved=2**21)[0]


def pair_kernel(first, second, out):
    rows = first.shape[0]
    out[0:rows] = first[...]
    out[rows:] = second[...]


def pair(first, second):
    dims = (2 * first.shape[0], ROWS)
    return call(pair_kernel, [first, second], [shape(dims, BF16)], "pair", moved=2**20)[0]


def clips_kernel(place, here, there, clips, clips_t):
    x, core = place[2] // 2, place[2] % 2
    near = x + 1 - 2 * (x % 2)
    for k, part in enumerate((here, there)):
        for i, chip in enumerate((x, near, 3 - x, 3 - near)):
            rows = pl.ds(pl.multiple_of((2 * chip + (core + k) % 2) * CLIP_PIECE, 16), CLIP_PIECE)
            clips_t[rows, :] = part[i * CLIP_PIECE : (i + 1) * CLIP_PIECE]
    clips[...] = jnp.transpose(clips_t[...])


def logits_kernel(place, owner, clips, *refs):
    from_z, from_y, outs, (acc0, acc1, peaks) = refs[:4], refs[4:7], refs[7:11], refs[11:]
    captions, plain, raised, stats = outs
    y, z = place[0], place[1]

    def put(i, k, piece):
        block = ((y - AWAY[i] + SIDE) % SIDE) * SIDE + (z - AWAY[k] + SIDE) % SIDE
        rows = pl.ds(pl.multiple_of(block * CAPTION_PIECE, 16), CAPTION_PIECE)
        captions[rows, :] = piece

    for k in range(SIDE):
        for i in range(3):
            put(i, k, from_y[i][:, k * COLS : (k + 1) * COLS])
        put(3, k, from_z[k][...])
    scale = 1.0 / math.sqrt(WIDTH)
    for n in range(4):
        at = slice(n * 512, (n + 1) * 512)
        product = jnp.dot(clips[...], captions[:, at], preferred_element_type=F32) * scale
        plain[:, at] = product
        ids = lax.broadcasted_iota(jnp.int32, (ROWS, 512), 0)
        raised[:, at] = product + BOOST * (ids == owner[:, at]).astype(F32)

    def peak_body(rows):
        best = plain[rows, tile(0)]
        for t in range(1, TILES):
            best = jnp.maximum(best, plain[rows, tile(t)])
        best = jnp.broadcast_to(jnp.max(best, axis=1, keepdims=True), best.shape) + BOOST
        peaks[rows, :] = best
        sum0 = jnp.zeros_like(best)
        sum1 = jnp.zeros_like(best)
        for t in range(TILES):
            value = plain[rows, tile(t)]
            term = jnp.exp(value - best)
            sum0 += term
            sum1 += jnp.where(raised[rows, tile(t)] > value, term * math.exp(BOOST), term)
        acc0[rows, :] = sum0
        acc1[rows, :] = sum1

    row_chunks(32, peak_body)
    best = jnp.max(jnp.transpose(peaks[...]), axis=0, keepdims=True)
    copy_out(stats, best + jnp.log(jnp.concatenate([along(acc1[...]), along(acc0[...])])))


def first_cols_kernel(raised, plain, parts, row_dual, row_lse, stats):
    row_dual[...] = down(-joined(parts[:, 0, :]))
    row_lse[...] = down(joined(parts[:, 1, :]))
    for t in range(TILES):
        block = raised[:, tile(t)] + row_dual[...]
        best = jnp.max(block, axis=0, keepdims=True)
        total = jnp.sum(jnp.exp(block - best), axis=0, keepdims=True)
        block = plain[:, tile(t)]
        best_plain = jnp.max(block, axis=0, keepdims=True)
        total_plain = jnp.sum(jnp.exp(block - best_plain), axis=0, keepdims=True)
        line = jnp.concatenate([best + jnp.log(total), best_plain + jnp.log(total_plain)])
        for k in range(16):
            stats[k, :, tile(t)] = line


def joint_kernel(raised, row_dual, parts, joint, col_lse, sums, line, acc):
    line[...] = jnp.broadcast_to(HALF_LOG - joined(parts[:, 0, :]), line.shape)
    col_lse[...] = joined(parts[:, 1, :])

    def body(rows):
        dual = row_dual[rows, :]
        total = jnp.zeros_like(dual)
        for t in range(TILES):
            value = jnp.exp(raised[rows, tile(t)] + dual + line[0:1, tile(t)])
            joint[rows, tile(t)] = value
            total += value
        acc[rows, :] = total

    row_chunks(32, body)
    copy_out(sums, along(acc[...]))


def col_step_kernel(joint, parts, sums, scale):
    scale[...] = down(1.0 / gathered(parts))
    for t in range(TILES):
        total = jnp.sum(joint[:, tile(t)] * scale[...], axis=0, keepdims=True)
        for k in range(16):
            sums[k, :, tile(t)] = total


def row_step_kernel(joint, parts, sums, line, acc):
    line[...] = jnp.broadcast_to(0.5 / gathered(parts), line.shape)

    def body(rows):
        total = joint[rows, tile(0)] * line[0:1, tile(0)]
        for t in range(1, TILES):
            total += joint[rows, tile(t)] * line[0:1, tile(t)]
        acc[rows, :] = total

    row_chunks(32, body)
    copy_out(sums, along(acc[...]))


def last_col_kernel(joint, plain, col_lse, parts, scale, sums):
    scale[...] = down(1.0 / gathered(parts))
    for t in range(TILES):
        value = joint[:, tile(t)] * scale[...]
        total = jnp.sum(value, axis=0, keepdims=True)
        gap = col_lse[0:1, tile(t)] - plain[:, tile(t)]
        both = jnp.concatenate([total, jnp.sum(value * gap, axis=0, keepdims=True)])
        for k in range(16):
            sums[k, :, tile(t)] = both


def last_row_kernel(joint, plain, row_lse, parts, col_scale, sums, line, acc0, acc1):
    total = gathered(parts)
    factor = 0.5 / total[0:1]
    col_scale[...] = factor
    line[...] = jnp.broadcast_to(factor, line.shape)
    col_terms = jnp.sum(factor * total[1:2], axis=1, keepdims=True)

    def body(rows):
        lse = row_lse[rows, :]
        sum0 = jnp.zeros_like(lse)
        sum1 = jnp.zeros_like(lse)
        for t in range(TILES):
            value = joint[rows, tile(t)] * line[0:1, tile(t)]
            sum0 += value
            sum1 += value * (lse - plain[rows, tile(t)])
        acc0[rows, :] = sum0
        acc1[rows, :] = sum1

    row_chunks(32, body)
    terms = jnp.broadcast_to(col_terms, (1, ROWS))
    copy_out(sums, jnp.concatenate([along(acc0[...]), along(acc1[...]), terms, terms]))


def chunk_pairs(place, slope, clips_t, i):
    y, z = place[0], place[1]

    def columns(k):
        block = ((y + AWAY[i]) % SIDE) * SIDE + (z + AWAY[k]) % SIDE
        return slope[:, pl.ds(pl.multiple_of(block * LANES, LANES), LANES)]

    for k in (0, 2):
        two = jnp.concatenate([columns(k), columns(k + 1)], axis=1)
        product = jnp.dot(clips_t[...], two, preferred_element_type=F32)
        yield k, product[:, 0:LANES]
        yield k + 1, product[:, LANES:]


def slope_kernel(
    place, joint, plain, row_lse, col_lse, row_scale, col_scale, clips_t, parts, *refs
):
    slope, own_share, *to_y = refs[:4]
    both, line = refs[4:]
    total = gathered(parts)
    norm = 1.0 / total[0:1]
    row_terms = jnp.sum(total[1:2] * norm, axis=1, keepdims=True)
    share = jnp.broadcast_to(row_terms + total[2:3, 0:1] / 16.0, (1, LANES)) / 16384.0
    own_share[...] = share
    both[...] = row_scale[...] + down(norm)
    line[...] = jnp.broadcast_to(col_scale[...], line.shape)

    def body(rows):
        scale = both[rows, :]
        lse = row_lse[rows, :]
        for t in range(TILES):
            value = plain[rows, tile(t)]
            soft = jnp.exp(value - lse) + 0.5 * jnp.exp(value - col_lse[0:1, tile(t)])
            target = joint[rows, tile(t)] * line[0:1, tile(t)] * scale
            slope[rows, tile(t)] = (soft - target).astype(BF16)

    row_chunks(32, body)
    for i in (1, 2):
        for k, product in chunk_pairs(place, slope, clips_t, i):
            narrow(product, share, to_y[i - 1], k * PACKED)

def far_kernel(place, slope, clips_t, share, own_z, *to_z):
    for k, product in chunk_pairs(place, slope, clips_t, 3):
        if k == 0:
            own_z[...] = product
        else:
            narrow(product, share[...], to_z[k - 1], 0)


SHARE = ROWS // 8


def near_kernel(place, slope, clips_t, *own_y):
    for k, value in chunk_pairs(place, slope, clips_t, 0):
        own_y[k][...] = value


def clip_kernel(place, slope, captions, kept, sent, product):
    product[...] = lax.dot_general(
        slope[...], captions[...], (((1,), (1,)), ((), ())), preferred_element_type=F32
    )
    x, core = place[2] // 2, place[2] % 2
    near = x + 1 - 2 * (x % 2)

    def rows_for(core):
        return [
            product[pl.ds(pl.multiple_of((chip * 2 + core) * SHARE, SHARE), SHARE), :]
            for chip in (x, 3 - x, near, 3 - near)
        ]

    kept[...] = jnp.concatenate(rows_for(core))
    narrow(jnp.concatenate(rows_for(1 - core)), ZERO, sent, 0)


def halve_kernel(own, came, kept, sent):
    value = own[...] + widen(came[...])[0]
    half = value.shape[0] // 2
    kept[...] = value[0:half]
    narrow(value[half:], ZERO, sent, 0)


def add_kernel(own, came, out):
    out[...] = own[...] + widen(came[...])[0]


def total(own, own_share, parts):
    value, share = own[...], own_share[...]
    for part in parts:
        more, came = widen(part[...])
        value += more
        share += came
    return value, share


def pass_on_kernel(own, own_share, *refs):
    parts, out = refs[:-1], refs[-1]
    value, share = total(own, own_share, parts)
    narrow(value, share, out, 0)


def keep_kernel(own, own_share, *refs):
    parts, (value_out, share_out) = refs[:-2], refs[-2:]
    value_out[...], share_out[...] = total(own, own_share, parts)


def final_kernel(own_share, kept, *refs):
    parts, (caption_grad, loss) = refs[0:4], refs[4:]
    value, loss[...] = total(kept, own_share, parts)
    caption_grad[...] = jnp.transpose(value)


def body(clips, captions, caption_owner):
    row = lax.axis_index("row").astype(jnp.int32)
    col = lax.axis_index("col").astype(jnp.int32)
    place = jnp.stack([row // SIDE, row % SIDE, col, col])
    owner = (caption_owner - row * ROWS).reshape(1, COLS)
    area = ROWS * COLS

    captions_t = captions.T
    far = row_shift(captions_t, 2, 0)
    from_z = along_z([captions_t] * SIDE)
    beside = swap(clips.T, 2)
    from_z[0], two = call(
        local_kernel,
        [captions_t, clips.T, beside],
        [shape((CAPTION_PIECE, COLS), BF16), shape((2 * CLIP_PIECE, ROWS), BF16)],
        "local",
        moved=2**20,
    )
    far, from_z = lax.optimization_barrier((far, from_z))
    joined = join(from_z)
    clips_here = pair(two, swap(two, 6))
    clips_rows, clips_t = call(
        clips_kernel,
        [place, clips_here, swap(clips_here, 1)],
        [pltpu.VMEM((ROWS, WIDTH), BF16), pltpu.VMEM((WIDTH, ROWS), BF16)],
        "clips",
        smem=1,
        moved=2**21,
    )
    from_y = along_y([joined] * 3)
    from_z = along_z([far] * SIDE)

    captions_full, plain, raised, stats = call(
        logits_kernel,
        [place, owner, clips_rows, *from_z, *from_y],
        [
            pltpu.VMEM((WIDTH, COLS), BF16),
            pltpu.VMEM((ROWS, COLS), F32),
            pltpu.VMEM((ROWS, COLS), F32),
            shape((8, 2, ROWS)),
        ],
        "logits",
        [pltpu.VMEM((ROWS, LANES), F32)] * 3,
        smem=1,
        limit=12,
        flops=2 * area * WIDTH,
        moved=20 * 2**20,
        exps=2 * area,
    )
    parts = col_all(stats)
    row_dual, row_lse, stats = call(
        first_cols_kernel,
        [raised, plain, parts],
        [pltpu.VMEM((ROWS, LANES), F32), pltpu.VMEM((ROWS, LANES), F32), shape((16, 2, COLS))],
        "first_cols",
        flops=6 * area,
        moved=4 * area,
        exps=area,
    )
    parts = row_all(stats)
    joint, col_lse, sums = call(
        joint_kernel,
        [raised, row_dual, parts],
        [pltpu.VMEM((ROWS, COLS), F32), shape((1, COLS)), shape((8, 1, ROWS))],
        "joint",
        [pltpu.VMEM((8, COLS), F32), pltpu.VMEM((ROWS, LANES), F32)],
        flops=6 * area,
        moved=8 * area,
        exps=area,
    )
    parts = col_all(sums)
    (sums,) = call(
        col_step_kernel,
        [joint, parts],
        [shape((16, 1, COLS))],
        "col_step",
        [pltpu.VMEM((ROWS, LANES), F32)],
        flops=2 * area,
        moved=4 * area,
    )
    (sums,) = call(
        row_step_kernel,
        [joint, row_all(sums)],
        [shape((8, 1, ROWS))],
        "row_step",
        [pltpu.VMEM((8, COLS), F32), pltpu.VMEM((ROWS, LANES), F32)],
        flops=2 * area,
        moved=4 * area,
    )
    row_scale, sums = call(
        last_col_kernel,
        [joint, plain, col_lse, col_all(sums)],
        [pltpu.VMEM((ROWS, LANES), F32), shape((16, 2, COLS))],
        "last_col",
        flops=4 * area,
        moved=8 * area,
    )
    col_scale, sums = call(
        last_row_kernel,
        [joint, plain, row_lse, row_all(sums)],
        [shape((1, COLS)), shape((8, 4, ROWS))],
        "last_row",
        [pltpu.VMEM((8, COLS), F32)] + [pltpu.VMEM((ROWS, LANES), F32)] * 2,
        flops=4 * area,
        moved=8 * area,
    )
    def packed(chunks):
        return shape((chunks * PACKED, LANES), jnp.int16)

    slope, share, *to_y = call(
        slope_kernel,
        [place, joint, plain, row_lse, col_lse, row_scale, col_scale, clips_t, col_all(sums)],
        [pltpu.VMEM((ROWS, COLS), BF16), shape((1, LANES))] + [packed(SIDE)] * 2,
        "slope",
        [pltpu.VMEM((ROWS, LANES), F32), pltpu.VMEM((8, COLS), F32)],
        smem=1,
        flops=area * WIDTH,
        moved=12 * area,
        exps=2 * area,
    )
    from_y = along_y([None, *to_y])[1:]
    own_z, *to_z = call(
        far_kernel,
        [place, slope, clips_t, share],
        [shape((WIDTH, LANES))] + [packed(1)] * 3,
        "far",
        smem=1,
        flops=area * WIDTH // 2,
        moved=8 * area,
    )
    two_away = row_shift(to_z[2], 0, 2)
    from_z = [row_shift(to_z[0], 0, 1), row_shift(to_z[1], 0, 3), two_away]
    own_z, slope = lax.optimization_barrier((own_z, slope))
    clip_own, sent = call(
        clip_kernel,
        [place, slope, captions_full],
        [shape((4 * SHARE, WIDTH)), shape((4 * SHARE + EXTRA, WIDTH), jnp.int16)],
        "clip_share",
        [pltpu.VMEM((ROWS, WIDTH), F32)],
        smem=1,
        flops=2 * area * WIDTH,
        moved=8 * area,
    )
    came = swap(sent, 1)
    own_y0, own_y1, own_y2, own_y3 = call(
        near_kernel,
        [place, slope, clips_t],
        [shape((WIDTH, LANES))] * 4,
        "near",
        smem=1,
        flops=area * WIDTH // 2,
        moved=4 * area,
    )
    came, own_y0 = lax.optimization_barrier((came, own_y0))
    from_y, came_z = lax.optimization_barrier((from_y, from_z))
    from_z, all_sent = [], []
    for k, own in ((1, own_y1), (2, own_y2), (3, own_y3)):
        chunk = pl.BlockSpec((PACKED, LANES), lambda step, k=k: (k, 0))
        (sent_z,) = call(
            pass_on_kernel,
            [own, share, *from_y],
            [packed(1)],
            "pass_on_z",
            moved=2**21,
            specs=[VM, VM, chunk, chunk],
            grid=(1,),
        )
        all_sent.append(sent_z)
        from_z.append(row_shift(sent_z, 0, AWAY[k]))
    (sent_on,) = call(pass_on_kernel, [own_z, share, *came_z], [packed(1)], "pass_on_y", moved=2**21)
    from_y2 = row_shift(sent_on, 2, 0)
    chunk = pl.BlockSpec((PACKED, LANES), lambda step: (0, 0))
    kept, share = call(
        keep_kernel,
        [own_y0, share, *from_y],
        [shape((WIDTH, LANES)), shape((1, LANES))],
        "keep",
        moved=2**21,
        specs=[VM, VM, chunk, chunk],
        grid=(1,),
    )
    for rows, bits in ((2 * SHARE, 2), (SHARE, 6)):
        clip_own, sent = call(
            halve_kernel,
            [clip_own, came],
            [shape((rows, WIDTH)), shape((rows + EXTRA, WIDTH), jnp.int16)],
            "halve",
            moved=2**21,
        )
        came = swap(sent, bits)
    (clip_grad,) = call(add_kernel, [clip_own, came], [shape((SHARE, WIDTH))], "clip_add")
    clip_grad, kept = lax.optimization_barrier((clip_grad, kept))
    caption_grad, loss = call(
        final_kernel,
        [share, kept, from_y2, *from_z],
        [shape((LANES, WIDTH)), shape((1, LANES))],
        "final",
        flops=area,
        moved=4 * area,
    )
    return loss[0, 0], clip_grad, caption_grad


def solution(mesh):
    in_specs = (P("row", "col"), P("col", "row"), P("col"))
    out_specs = (P(), P(("row", "col"), None), P(("col", "row"), None))
    return jax.shard_map(body, mesh=mesh, in_specs=in_specs, out_specs=out_specs, check_vma=False)
```

time: 743 us -> 160 us (0.22)
  blocking collectives: 469 us -> 68.8 us
  waiting for transfers between devices: 152 us -> 27.8 us
  matrix products: 69.3 us -> 0 us
  starting transfers between devices: 0.12 us -> 33.9 us
  Pallas kernels: 0 us -> 25.9 us
  other arithmetic: 16.9 us -> 0.78 us
  between operations: 14.1 us -> 0.86 us
  local copies, waits for them, and re-layouts: 12.5 us -> 1.82 us
    psum x8 -> x0, blocking collectives: 265 us -> none  [the longest x3 146 us: across_row(): totals = lax.psum(totals * jnp.exp(maxima - larger), 'row')]
    pmax x7 -> x0, blocking collectives: 190 us -> none  [the longest x3 139 us: across_row(): larger = lax.pmax(maxima, 'row')]
    psum x2 -> x0, waiting for transfers between devices: 113 us -> none  [the longest x1 113 us: body(): caption_summed = lax.psum(caption_term, 'row')]
    dot_general x34 -> x0, matrix products: 69.3 us -> none  [the longest x32 59.9 us: pair_logits(): lax.dot_general(clip_side, caption_side, (((1,), (1,)), ((), ())), prefer...]
    all_to_all x0 -> x7, blocking collectives: none -> 68.8 us  [the longest x3 36.8 us: row_all(): return lax.all_to_all(copies, 'row', 0, 0, tiled=True)]
    all_gather x1 -> x0, waiting for transfers between devices: 37.6 us -> none  [body(): caption_full = lax.all_gather(captions, 'row', axis=1, tiled=True)]
    ppermute x0 -> x24, starting transfers between devices: none -> 33.9 us  [the longest x18 27.6 us: row_shift(): return lax.ppermute(value, 'row', pairs)]
    ppermute x0 -> x24, waiting for transfers between devices: none -> 27.8 us  [the longest x18 17.6 us: row_shift(): return lax.ppermute(value, 'row', pairs)]
  transfers between devices with their start and end apart: 3 -> 24, of which waited for: 2 -> 10; matrix products, arithmetic and copies ran while one was open for 1% -> 0% of each run, Pallas kernels for 0% -> 5%
where the time goes in v1:
time: 160 us
  blocking collectives  68.8 us (43%)
  starting transfers between devices  33.9 us (21%)
  waiting for transfers between devices  27.8 us (17%)
  Pallas kernels  25.9 us (16%)
  local copies, waits for them, and re-layouts  1.82 us (1%)
    all_to_all x3, blocking collectives, row_all(): return lax.all_to_all(copies, 'row', 0, 0, tiled=True)  36.8 us
    all_to_all x4, blocking collectives, col_all(): return lax.all_to_all(copies, 'col', 0, 0, tiled=True)  32 us
    ppermute x18, starting transfers between devices, row_shift(): return lax.ppermute(value, 'row', pairs)  27.6 us
    pallas_call x24, Pallas kernels, call(): pl.pallas_call(kernel, grid=grid, out_shape=outs, in_specs=specs or [SM]...  25.9 us
    ppermute x18, waiting for transfers between devices, row_shift(): return lax.ppermute(value, 'row', pairs)  17.6 us
    ppermute x6, waiting for transfers between devices, swap(): return lax.ppermute(value, 'col', [(c, c ^ bits) for c in range(8)])  10.2 us
    ppermute x6, starting transfers between devices, swap(): return lax.ppermute(value, 'col', [(c, c ^ bits) for c in range(8)])  6.31 us
  transfers between devices with their start and end apart: 24, of which 10 were waited for; matrix products, arithmetic and copies ran while one was open for 0% of the time, Pallas kernels for 5%

profile of v1, /device:TPU:8, one launch (start us, length us, event | category | flops | bytes accessed | tf_op | source)
XLA Modules:
  0.0 159.9 jit_solution(9979405622989568980)
XLA Ops:
  0.6 4.0 %collective-permute-start.6 = (bf16[48,2048]{1,0:T(8,128)(2,1)}, bf16[48,2048]{1,0:T(8,128)(2,1)S(1)}, u32[]{:S(2)}, u32[]{:S(2)}) collective-permute-start(bf16[48,2048]{1,0:T(8,128)(2,1)} %bitcast.8), channel_id=1, source_target_pairs={{0,16},{8,24},{16,0},{24,8},{32,48},{40,56},{48,32},{56,40},{64,80... | collective-permute-start | bytes 589832 | tf_op jit(solution)/shard_map/ppermute | solution.py:56
  5.3 1.3 collective-permute-start.4
  6.6 2.3 %collective-permute-start.3 = (bf16[48,2048]{1,0:T(8,128)(2,1)}, bf16[48,2048]{1,0:T(8,128)(2,1)S(1)}, u32[]{:S(2)}, u32[]{:S(2)}) collective-permute-start(bf16[48,2048]{1,0:T(8,128)(2,1)} %bitcast.11), channel_id=1, source_target_pairs={{0,64},{8,72},{16,80},{24,88},{32,96},{40,104},{48,112},{56,120},{... | collective-permute-start | bytes 589832 | tf_op jit(solution)/shard_map/ppermute | solution.py:56
  8.9 1.5 collective-permute-start
  10.4 3.3 %collective-permute-done.beside = bf16[96,512]{1,0:T(8,128)(2,1)S(1)} collective-permute-done((bf16[96,512]{1,0:T(8,128)(2,1)}, bf16[96,512]{1,0:T(8,128)(2,1)S(1)}, u32[]{:S(2)}, u32[]{:S(2)}) %collective-permute-start) | collective-permute-done | bytes 98336 | tf_op jit(solution)/shard_map/ppermute | solution.py:78
  15.6 2.8 %collective-permute-start.1 = (bf16[192,512]{1,0:T(8,128)(2,1)S(1)}, bf16[192,512]{1,0:T(8,128)(2,1)S(1)}, u32[]{:S(2)}, u32[]{:S(2)}) collective-permute-start(bf16[192,512]{1,0:T(8,128)(2,1)S(1)} %get-tuple-element.59.first), channel_id=1, source_target_pairs={{0,6},{1,7},{2,4},{3,5},{4,2},{5,3},{6,0},{7,1},{8,14},{9,15},{10,... | collective-permute-start | bytes 589832 | tf_op jit(solution)/shard_map/ppermute | solution.py:78
  18.5 1.4 collective-permute-start.11
  20.6 1.9 %collective-permute-done.1.second = bf16[192,512]{1,0:T(8,128)(2,1)S(1)} collective-permute-done((bf16[192,512]{1,0:T(8,128)(2,1)S(1)}, bf16[192,512]{1,0:T(8,128)(2,1)S(1)}, u32[]{:S(2)}, u32[]{:S(2)}) %collective-permute-start.1) | collective-permute-done | bytes 196640 | tf_op jit(solution)/shard_map/ppermute | solution.py:78
  23.9 2.6 %collective-permute-start.8 = (bf16[48,2048]{1,0:T(8,128)(2,1)S(1)}, bf16[48,2048]{1,0:T(8,128)(2,1)S(1)}, u32[]{:S(2)}, u32[]{:S(2)}) collective-permute-start(bf16[48,2048]{1,0:T(8,128)(2,1)S(1)} %collective-permute-done.3.refs_0_), channel_id=1, source_target_pairs={{0,24},{8,0},{16,8},{24,16},{32,56},{40,32},{48,40},{56,48},{64,88... | collective-permute-start | bytes 589832 | tf_op jit(solution)/shard_map/ppermute | solution.py:56
  28.1 3.9 %collective-permute-done.9.refs_3_ = bf16[48,2048]{1,0:T(8,128)(2,1)S(1)} collective-permute-done((bf16[48,2048]{1,0:T(8,128)(2,1)S(1)}, bf16[48,2048]{1,0:T(8,128)(2,1)S(1)}, u32[]{:S(2)}, u32[]{:S(2)}) %collective-permute-start.9) | collective-permute-done | bytes 196640 | tf_op jit(solution)/shard_map/ppermute | solution.py:56
  32.0 3.1 %collective-permute-done.8.refs_2_ = bf16[48,2048]{1,0:T(8,128)(2,1)S(1)} collective-permute-done((bf16[48,2048]{1,0:T(8,128)(2,1)S(1)}, bf16[48,2048]{1,0:T(8,128)(2,1)S(1)}, u32[]{:S(2)}, u32[]{:S(2)}) %collective-permute-start.8) | collective-permute-done | bytes 196640 | tf_op jit(solution)/shard_map/ppermute | solution.py:56
  36.7 5.8 %logits.1 = (bf16[768,2048]{1,0:T(8,128)(2,1)S(1)}, f32[512,2048]{1,0:T(8,128)S(1)}, f32[512,2048]{1,0:T(8,128)S(1)}, f32[8,2,512]{2,1,0:T(2,128)S(1)}) custom-call(s32[4]{0:T(128)S(1)} %pad_add_fusion.place, s32[1,2048]{1,0:T(1,128)S(1)} %bitcast.15, bf16[512,768]{1,0:T(8,128)(2,1)S(1)} %get-tuple-element.60.clips, ...), custom_call_target="tpu_custom_call" | custom-call | flops 1610612736 | bytes 20971520 | tf_op jit(solution)/shard_map/logits/pallas_call | solution.py:33
  42.5 8.4 %all_to_all.35.parts = f32[8,2,512]{2,1,0:T(2,128)S(1)} all-to-all(f32[8,2,512]{2,1,0:T(2,128)S(1)} %get-tuple-element.69), channel_id=1, replica_groups=mesh['row'=16,'col'=8] {'col'}, dimensions={0} | all-to-all | bytes 65536 | tf_op jit(solution)/shard_map/all_to_all | solution.py:70
  50.9 2.0 %first_cols.1 = (f32[512,128]{1,0:T(8,128)S(1)}, f32[512,128]{1,0:T(8,128)S(1)}, f32[16,2,2048]{2,1,0:T(2,128)S(1)}) custom-call(f32[512,2048]{1,0:T(8,128)S(1)} %get-tuple-element.67.raised, f32[512,2048]{1,0:T(8,128)S(1)} %get-tuple-element.68.plain, f32[8,2,512]{2,1,0:T(2,128)S(1)} %all_to_all.35.parts), custom_call_target="tpu_custom_call" | custom-call | flops 6291456 | bytes 4194304 | tf_op jit(solution)/shard_map/first_cols/pallas_call | solution.py:33
  52.9 13.6 %all_to_all.36.parts = f32[16,2,2048]{2,1,0:T(2,128)S(1)} all-to-all(f32[16,2,2048]{2,1,0:T(2,128)S(1)} %get-tuple-element.71), channel_id=1, replica_groups=mesh['row'=16,'col'=8] {'row'}, dimensions={0} | all-to-all | bytes 524288 | tf_op jit(solution)/shard_map/all_to_all | solution.py:74
  67.7 7.7 %all_to_all.37.parts = f32[8,1,512]{2,1,0:T(1,128)S(1)} all-to-all(f32[8,1,512]{2,1,0:T(1,128)S(1)} %get-tuple-element.75), channel_id=1, replica_groups=mesh['row'=16,'col'=8] {'col'}, dimensions={0} | all-to-all | bytes 32768 | tf_op jit(solution)/shard_map/all_to_all | solution.py:70
  75.9 11.5 %all_to_all.38.parts = f32[16,1,2048]{2,1,0:T(1,128)S(1)} all-to-all(f32[16,1,2048]{2,1,0:T(1,128)S(1)} %col_step.1), channel_id=1, replica_groups=mesh['row'=16,'col'=8] {'row'}, dimensions={0} | all-to-all | bytes 262144 | tf_op jit(solution)/shard_map/all_to_all | solution.py:74
  88.0 7.7 %all_to_all.39.parts = f32[8,1,512]{2,1,0:T(1,128)S(1)} all-to-all(f32[8,1,512]{2,1,0:T(1,128)S(1)} %row_step.1), channel_id=1, replica_groups=mesh['row'=16,'col'=8] {'col'}, dimensions={0} | all-to-all | bytes 32768 | tf_op jit(solution)/shard_map/all_to_all | solution.py:70
  95.7 1.4 last_col.1
  97.1 11.6 %all_to_all.40.parts = f32[16,2,2048]{2,1,0:T(2,128)S(1)} all-to-all(f32[16,2,2048]{2,1,0:T(2,128)S(1)} %get-tuple-element.77), channel_id=1, replica_groups=mesh['row'=16,'col'=8] {'row'}, dimensions={0} | all-to-all | bytes 524288 | tf_op jit(solution)/shard_map/all_to_all | solution.py:74
  108.7 1.3 last_row.1
  110.0 8.2 %all_to_all.41.parts = f32[8,4,512]{2,1,0:T(4,128)S(1)} all-to-all(f32[8,4,512]{2,1,0:T(4,128)S(1)} %get-tuple-element.80), channel_id=1, replica_groups=mesh['row'=16,'col'=8] {'col'}, dimensions={0} | all-to-all | bytes 131072 | tf_op jit(solution)/shard_map/all_to_all | solution.py:70
  118.2 4.1 %slope.1 = (bf16[512,2048]{1,0:T(8,128)(2,1)S(1)}, f32[1,128]{1,0:T(1,128)S(1)}, s16[3136,128]{1,0:T(8,128)(2,1)S(1)}, s16[3136,128]{1,0:T(8,128)(2,1)S(1)}) custom-call(s32[4]{0:T(128)S(1)} %pad_add_fusion.place, f32[512,2048]{1,0:T(8,128)S(1)} %get-tuple-element.72.joint, f32[512,2048]{1,0:T(8,128)S(1)} %get-tuple-element.68.plain, ...), custom_call_target="tpu_custom_call" | custom-call | flops 805306368 | bytes 12582912 | tf_op jit(solution)/shard_map/slope/pallas_call | solution.py:33
  124.4 1.4 far.1
  125.7 2.6 %clip_share.1 = (f32[256,768]{1,0:T(8,128)S(1)}, s16[272,768]{1,0:T(8,128)(2,1)S(1)}) custom-call(s32[4]{0:T(128)S(1)} %pad_add_fusion.place, bf16[512,2048]{1,0:T(8,128)(2,1)S(1)} %get-tuple-element.84.slope, bf16[768,2048]{1,0:T(8,128)(2,1)S(1)} %get-tuple-element.85.captions), custom_call_target="tpu_custom_call" | custom-call | flops 1610612736 | bytes 8388608 | tf_op jit(solution)/shard_map/clip_share/pallas_call | solution.py:33
  128.9 2.8 %collective-permute-start.16 = (s16[784,128]{1,0:T(8,128)(2,1)S(1)}, s16[784,128]{1,0:T(8,128)(2,1)S(1)}, u32[]{:S(2)}, u32[]{:S(2)}) collective-permute-start(s16[784,128]{1,0:T(8,128)(2,1)S(1)} %get-tuple-element.92), channel_id=1, source_target_pairs={{0,24},{8,0},{16,8},{24,16},{32,56},{40,32},{48,40},{56,48},{64,88... | collective-permute-start | bytes 602120 | tf_op jit(solution)/shard_map/ppermute | solution.py:56
  133.5 7.8 %collective-permute-done.15.refs_0_ = s16[784,128]{1,0:T(8,128)(2,1)S(1)} collective-permute-done((s16[784,128]{1,0:T(8,128)(2,1)S(1)}, s16[784,128]{1,0:T(8,128)(2,1)S(1)}, u32[]{:S(2)}, u32[]{:S(2)}) %collective-permute-start.15) | collective-permute-done | bytes 200736 | tf_op jit(solution)/shard_map/ppermute | solution.py:56
  142.9 4.1 %collective-permute-start.20 = (s16[784,128]{1,0:T(8,128)(2,1)S(1)}, s16[784,128]{1,0:T(8,128)(2,1)S(1)}, u32[]{:S(2)}, u32[]{:S(2)}) collective-permute-start(s16[784,128]{1,0:T(8,128)(2,1)S(1)} %pass_on_y.1), channel_id=1, source_target_pairs={{0,64},{8,72},{16,80},{24,88},{32,96},{40,104},{48,112},{56,120},{... | collective-permute-start | bytes 602120 | tf_op jit(solution)/shard_map/ppermute | solution.py:56
  147.7 1.5 collective-permute-start.23
  149.2 1.7 %collective-permute-start.22 = (s16[784,128]{1,0:T(8,128)(2,1)S(1)}, s16[784,128]{1,0:T(8,128)(2,1)S(1)}, u32[]{:S(2)}, u32[]{:S(2)}) collective-permute-start(s16[784,128]{1,0:T(8,128)(2,1)S(1)} %pass_on_z.4), channel_id=1, source_target_pairs={{0,24},{8,0},{16,8},{24,16},{32,56},{40,32},{48,40},{56,48},{64,88... | collective-permute-start | bytes 602120 | tf_op jit(solution)/shard_map/ppermute | solution.py:56
  151.4 1.2 collective-permute-start.19
  152.6 4.9 %collective-permute-done.19.came = s16[80,768]{1,0:T(8,128)(2,1)S(1)} collective-permute-done((s16[80,768]{1,0:T(8,128)(2,1)S(1)}, s16[80,768]{1,0:T(8,128)(2,1)S(1)}, u32[]{:S(2)}, u32[]{:S(2)}) %collective-permute-start.19) | collective-permute-done | bytes 122912 | tf_op jit(solution)/shard_map/ppermute | solution.py:78
  (53 shorter events, 19.4 us)
Async XLA Ops:
  0.6 17.8 %collective-permute-start.6 = (bf16[48,2048]{1,0:T(8,128)(2,1)}, bf16[48,2048]{1,0:T(8,128)(2,1)S(1)}, u32[]{:S(2)}, u32[]{:S(2)}) collective-permute-start(bf16[48,2048]{1,0:T(8,128)(2,1)} %bitcast.8), channel_id=1, source_target_pairs={{0,16},{8,24},{16,0},{24,8},{32,48},{40,56},{48,32},{56,40},{64,80... | collective-permute-start | bytes 589832 | tf_op jit(solution)/shard_map/ppermute | solution.py:56
  4.6 13.8 %collective-permute-start.5 = (bf16[48,2048]{1,0:T(8,128)(2,1)}, bf16[48,2048]{1,0:T(8,128)(2,1)S(1)}, u32[]{:S(2)}, u32[]{:S(2)}) collective-permute-start(bf16[48,2048]{1,0:T(8,128)(2,1)} %bitcast.9), channel_id=1, source_target_pairs={{0,24},{8,0},{16,8},{24,16},{32,56},{40,32},{48,40},{56,48},{64,88... | collective-permute-start | bytes 589832 | tf_op jit(solution)/shard_map/ppermute | solution.py:56
  5.3 13.1 %collective-permute-start.4 = (bf16[48,2048]{1,0:T(8,128)(2,1)}, bf16[48,2048]{1,0:T(8,128)(2,1)S(1)}, u32[]{:S(2)}, u32[]{:S(2)}) collective-permute-start(bf16[48,2048]{1,0:T(8,128)(2,1)} %bitcast.10), channel_id=1, source_target_pairs={{0,8},{8,16},{16,24},{24,0},{32,40},{40,48},{48,56},{56,32},{64,72... | collective-permute-start | bytes 589832 | tf_op jit(solution)/shard_map/ppermute | solution.py:56
  6.6 11.8 %collective-permute-start.3 = (bf16[48,2048]{1,0:T(8,128)(2,1)}, bf16[48,2048]{1,0:T(8,128)(2,1)S(1)}, u32[]{:S(2)}, u32[]{:S(2)}) collective-permute-start(bf16[48,2048]{1,0:T(8,128)(2,1)} %bitcast.11), channel_id=1, source_target_pairs={{0,64},{8,72},{16,80},{24,88},{32,96},{40,104},{48,112},{56,120},{... | collective-permute-start | bytes 589832 | tf_op jit(solution)/shard_map/ppermute | solution.py:56
  8.9 4.8 %collective-permute-start = (bf16[96,512]{1,0:T(8,128)(2,1)}, bf16[96,512]{1,0:T(8,128)(2,1)S(1)}, u32[]{:S(2)}, u32[]{:S(2)}) collective-permute-start(bf16[96,512]{1,0:T(8,128)(2,1)} %bitcast.13), channel_id=1, source_target_pairs={{0,2},{1,3},{2,0},{3,1},{4,6},{5,7},{6,4},{7,5},{8,10},{9,11},{10,... | collective-permute-start | bytes 294920 | tf_op jit(solution)/shard_map/ppermute | solution.py:78
  13.7 0.9 copy-start
  14.7 0.9 copy-start.1
  15.6 7.0 %collective-permute-start.1 = (bf16[192,512]{1,0:T(8,128)(2,1)S(1)}, bf16[192,512]{1,0:T(8,128)(2,1)S(1)}, u32[]{:S(2)}, u32[]{:S(2)}) collective-permute-start(bf16[192,512]{1,0:T(8,128)(2,1)S(1)} %get-tuple-element.59.first), channel_id=1, source_target_pairs={{0,6},{1,7},{2,4},{3,5},{4,2},{5,3},{6,0},{7,1},{8,14},{9,15},{10,... | collective-permute-start | bytes 589832 | tf_op jit(solution)/shard_map/ppermute | solution.py:78
  18.5 17.3 %collective-permute-start.11 = (bf16[48,8192]{1,0:T(8,128)(2,1)S(1)}, bf16[48,8192]{1,0:T(8,128)(2,1)S(1)}, u32[]{:S(2)}, u32[]{:S(2)}) collective-permute-start(bf16[48,8192]{1,0:T(8,128)(2,1)S(1)} %join.1.refs_4_), channel_id=1, source_target_pairs={{0,96},{8,104},{16,112},{24,120},{32,0},{40,8},{48,16},{56,24},{64... | collective-permute-start | bytes 2359304 | tf_op jit(solution)/shard_map/ppermute | solution.py:56
  19.9 16.7 %collective-permute-start.10 = (bf16[48,8192]{1,0:T(8,128)(2,1)S(1)}, bf16[48,8192]{1,0:T(8,128)(2,1)S(1)}, u32[]{:S(2)}, u32[]{:S(2)}) collective-permute-start(bf16[48,8192]{1,0:T(8,128)(2,1)S(1)} %join.1.refs_4_), channel_id=1, source_target_pairs={{0,32},{8,40},{16,48},{24,56},{32,64},{40,72},{48,80},{56,88},{64,... | collective-permute-start | bytes 2359304 | tf_op jit(solution)/shard_map/ppermute | solution.py:56
  22.6 3.9 %collective-permute-start.2 = (bf16[384,512]{1,0:T(8,128)(2,1)S(1)}, bf16[384,512]{1,0:T(8,128)(2,1)S(1)}, u32[]{:S(2)}, u32[]{:S(2)}) collective-permute-start(bf16[384,512]{1,0:T(8,128)(2,1)S(1)} %pair.1.here), channel_id=1, source_target_pairs={{0,1},{1,0},{2,3},{3,2},{4,5},{5,4},{6,7},{7,6},{8,9},{9,8},{10,11... | collective-permute-start | bytes 1179656 | tf_op jit(solution)/shard_map/ppermute | solution.py:78
  22.8 9.2 %collective-permute-start.9 = (bf16[48,2048]{1,0:T(8,128)(2,1)S(1)}, bf16[48,2048]{1,0:T(8,128)(2,1)S(1)}, u32[]{:S(2)}, u32[]{:S(2)}) collective-permute-start(bf16[48,2048]{1,0:T(8,128)(2,1)S(1)} %collective-permute-done.3.refs_0_), channel_id=1, source_target_pairs={{0,16},{8,24},{16,0},{24,8},{32,48},{40,56},{48,32},{56,40},{64,80... | collective-permute-start | bytes 589832 | tf_op jit(solution)/shard_map/ppermute | solution.py:56
  23.9 11.2 %collective-permute-start.8 = (bf16[48,2048]{1,0:T(8,128)(2,1)S(1)}, bf16[48,2048]{1,0:T(8,128)(2,1)S(1)}, u32[]{:S(2)}, u32[]{:S(2)}) collective-permute-start(bf16[48,2048]{1,0:T(8,128)(2,1)S(1)} %collective-permute-done.3.refs_0_), channel_id=1, source_target_pairs={{0,24},{8,0},{16,8},{24,16},{32,56},{40,32},{48,40},{56,48},{64,88... | collective-permute-start | bytes 589832 | tf_op jit(solution)/shard_map/ppermute | solution.py:56
  26.5 9.3 %collective-permute-start.7 = (bf16[48,2048]{1,0:T(8,128)(2,1)S(1)}, bf16[48,2048]{1,0:T(8,128)(2,1)S(1)}, u32[]{:S(2)}, u32[]{:S(2)}) collective-permute-start(bf16[48,2048]{1,0:T(8,128)(2,1)S(1)} %collective-permute-done.3.refs_0_), channel_id=1, source_target_pairs={{0,8},{8,16},{16,24},{24,0},{32,40},{40,48},{48,56},{56,32},{64,72... | collective-permute-start | bytes 589832 | tf_op jit(solution)/shard_map/ppermute | solution.py:56
  122.3 19.7 %collective-permute-start.13 = (s16[3136,128]{1,0:T(8,128)(2,1)S(1)}, s16[3136,128]{1,0:T(8,128)(2,1)S(1)}, u32[]{:S(2)}, u32[]{:S(2)}) collective-permute-start(s16[3136,128]{1,0:T(8,128)(2,1)S(1)} %get-tuple-element.89), channel_id=1, source_target_pairs={{0,32},{8,40},{16,48},{24,56},{32,64},{40,72},{48,80},{56,88},{64,... | collective-permute-start | bytes 2408456 | tf_op jit(solution)/shard_map/ppermute | solution.py:56
  123.4 19.2 %collective-permute-start.14 = (s16[3136,128]{1,0:T(8,128)(2,1)S(1)}, s16[3136,128]{1,0:T(8,128)(2,1)S(1)}, u32[]{:S(2)}, u32[]{:S(2)}) collective-permute-start(s16[3136,128]{1,0:T(8,128)(2,1)S(1)} %get-tuple-element.90), channel_id=1, source_target_pairs={{0,96},{8,104},{16,112},{24,120},{32,0},{40,8},{48,16},{56,24},{64... | collective-permute-start | bytes 2408456 | tf_op jit(solution)/shard_map/ppermute | solution.py:56
  128.3 3.4 %collective-permute-start.12 = (s16[272,768]{1,0:T(8,128)(2,1)S(1)}, s16[272,768]{1,0:T(8,128)(2,1)S(1)}, u32[]{:S(2)}, u32[]{:S(2)}) collective-permute-start(s16[272,768]{1,0:T(8,128)(2,1)S(1)} %get-tuple-element.86), channel_id=1, source_target_pairs={{0,1},{1,0},{2,3},{3,2},{4,5},{5,4},{6,7},{7,6},{8,9},{9,8},{10,11... | collective-permute-start | bytes 1253384 | tf_op jit(solution)/shard_map/ppermute | solution.py:78
  128.4 12.9 %collective-permute-start.15 = (s16[784,128]{1,0:T(8,128)(2,1)S(1)}, s16[784,128]{1,0:T(8,128)(2,1)S(1)}, u32[]{:S(2)}, u32[]{:S(2)}) collective-permute-start(s16[784,128]{1,0:T(8,128)(2,1)S(1)} %get-tuple-element.91), channel_id=1, source_target_pairs={{0,8},{8,16},{16,24},{24,0},{32,40},{40,48},{48,56},{56,32},{64,72... | collective-permute-start | bytes 602120 | tf_op jit(solution)/shard_map/ppermute | solution.py:56
  128.9 13.0 %collective-permute-start.16 = (s16[784,128]{1,0:T(8,128)(2,1)S(1)}, s16[784,128]{1,0:T(8,128)(2,1)S(1)}, u32[]{:S(2)}, u32[]{:S(2)}) collective-permute-start(s16[784,128]{1,0:T(8,128)(2,1)S(1)} %get-tuple-element.92), channel_id=1, source_target_pairs={{0,24},{8,0},{16,8},{24,16},{32,56},{40,32},{48,40},{56,48},{64,88... | collective-permute-start | bytes 602120 | tf_op jit(solution)/shard_map/ppermute | solution.py:56
  131.7 10.2 %collective-permute-start.17 = (s16[784,128]{1,0:T(8,128)(2,1)S(1)}, s16[784,128]{1,0:T(8,128)(2,1)S(1)}, u32[]{:S(2)}, u32[]{:S(2)}) collective-permute-start(s16[784,128]{1,0:T(8,128)(2,1)S(1)} %get-tuple-element.93), channel_id=1, source_target_pairs={{0,16},{8,24},{16,0},{24,8},{32,48},{40,56},{48,32},{56,40},{64,80... | collective-permute-start | bytes 602120 | tf_op jit(solution)/shard_map/ppermute | solution.py:56
  141.3 9.9 %collective-permute-start.18 = (s16[144,768]{1,0:T(8,128)(2,1)S(1)}, s16[144,768]{1,0:T(8,128)(2,1)S(1)}, u32[]{:S(2)}, u32[]{:S(2)}) collective-permute-start(s16[144,768]{1,0:T(8,128)(2,1)S(1)} %get-tuple-element.100), channel_id=1, source_target_pairs={{0,2},{1,3},{2,0},{3,1},{4,6},{5,7},{6,4},{7,5},{8,10},{9,11},{10,... | collective-permute-start | bytes 663560 | tf_op jit(solution)/shard_map/ppermute | solution.py:78
  142.9 15.5 %collective-permute-start.20 = (s16[784,128]{1,0:T(8,128)(2,1)S(1)}, s16[784,128]{1,0:T(8,128)(2,1)S(1)}, u32[]{:S(2)}, u32[]{:S(2)}) collective-permute-start(s16[784,128]{1,0:T(8,128)(2,1)S(1)} %pass_on_y.1), channel_id=1, source_target_pairs={{0,64},{8,72},{16,80},{24,88},{32,96},{40,104},{48,112},{56,120},{... | collective-permute-start | bytes 602120 | tf_op jit(solution)/shard_map/ppermute | solution.py:56
  147.7 10.7 %collective-permute-start.23 = (s16[784,128]{1,0:T(8,128)(2,1)S(1)}, s16[784,128]{1,0:T(8,128)(2,1)S(1)}, u32[]{:S(2)}, u32[]{:S(2)}) collective-permute-start(s16[784,128]{1,0:T(8,128)(2,1)S(1)} %pass_on_z.5), channel_id=1, source_target_pairs={{0,16},{8,24},{16,0},{24,8},{32,48},{40,56},{48,32},{56,40},{64,80... | collective-permute-start | bytes 602120 | tf_op jit(solution)/shard_map/ppermute | solution.py:56
  149.2 9.2 %collective-permute-start.22 = (s16[784,128]{1,0:T(8,128)(2,1)S(1)}, s16[784,128]{1,0:T(8,128)(2,1)S(1)}, u32[]{:S(2)}, u32[]{:S(2)}) collective-permute-start(s16[784,128]{1,0:T(8,128)(2,1)S(1)} %pass_on_z.4), channel_id=1, source_target_pairs={{0,24},{8,0},{16,8},{24,16},{32,56},{40,32},{48,40},{56,48},{64,88... | collective-permute-start | bytes 602120 | tf_op jit(solution)/shard_map/ppermute | solution.py:56
  150.9 8.0 %collective-permute-start.21 = (s16[784,128]{1,0:T(8,128)(2,1)S(1)}, s16[784,128]{1,0:T(8,128)(2,1)S(1)}, u32[]{:S(2)}, u32[]{:S(2)}) collective-permute-start(s16[784,128]{1,0:T(8,128)(2,1)S(1)} %pass_on_z.3), channel_id=1, source_target_pairs={{0,8},{8,16},{16,24},{24,0},{32,40},{40,48},{48,56},{56,32},{64,72... | collective-permute-start | bytes 602120 | tf_op jit(solution)/shard_map/ppermute | solution.py:56
  151.4 6.2 %collective-permute-start.19 = (s16[80,768]{1,0:T(8,128)(2,1)S(1)}, s16[80,768]{1,0:T(8,128)(2,1)S(1)}, u32[]{:S(2)}, u32[]{:S(2)}) collective-permute-start(s16[80,768]{1,0:T(8,128)(2,1)S(1)} %get-tuple-element.102), channel_id=1, source_target_pairs={{0,6},{1,7},{2,4},{3,5},{4,2},{5,3},{6,0},{7,1},{8,14},{9,15},{10,... | collective-permute-start | bytes 368648 | tf_op jit(solution)/shard_map/ppermute | solution.py:78

commit v2 on v1

--- a/solution.py
+++ b/solution.py
@@ -460,6 +460,7 @@
         [captions_t, clips.T, beside],
         [shape((CAPTION_PIECE, COLS), BF16), shape((2 * CLIP_PIECE, ROWS), BF16)],
         "local",
+        flops=2**33,
         moved=2**20,
     )
     far, from_z = lax.optimization_barrier((far, from_z))

time: 160 us -> 161 us (level)
  blocking collectives: 68.8 us -> 70.5 us
    ppermute x18, waiting for transfers between devices: 17.6 us -> 22.2 us  [row_shift(): return lax.ppermute(value, 'row', pairs)]
    ppermute x6, waiting for transfers between devices: 10.2 us -> 6.13 us  [swap(): return lax.ppermute(value, 'col', [(c, c ^ bits) for c in range(8)])]
  transfers between devices with their start and end apart: 24 -> 24, of which waited for: 10 -> 11; matrix products, arithmetic and copies ran while one was open for 0% -> 0% of each run, Pallas kernels for 5% -> 5%
where the time goes in v2:
time: 161 us
  blocking collectives  70.5 us (44%)
  starting transfers between devices  33.3 us (21%)
  waiting for transfers between devices  28.4 us (18%)
  Pallas kernels  25.9 us (16%)
  local copies, waits for them, and re-layouts  1.85 us (1%)
    all_to_all x3, blocking collectives, row_all(): return lax.all_to_all(copies, 'row', 0, 0, tiled=True)  37.6 us
    all_to_all x4, blocking collectives, col_all(): return lax.all_to_all(copies, 'col', 0, 0, tiled=True)  32.9 us
    ppermute x18, starting transfers between devices, row_shift(): return lax.ppermute(value, 'row', pairs)  27.5 us
    pallas_call x24, Pallas kernels, call(): pl.pallas_call(kernel, grid=grid, out_shape=outs, in_specs=specs or [SM]...  25.9 us
    ppermute x18, waiting for transfers between devices, row_shift(): return lax.ppermute(value, 'row', pairs)  22.2 us
    ppermute x6, waiting for transfers between devices, swap(): return lax.ppermute(value, 'col', [(c, c ^ bits) for c in range(8)])  6.13 us
    ppermute x6, starting transfers between devices, swap(): return lax.ppermute(value, 'col', [(c, c ^ bits) for c in range(8)])  5.73 us
  transfers between devices with their start and end apart: 24, of which 11 were waited for; matrix products, arithmetic and copies ran while one was open for 0% of the time, Pallas kernels for 5%

profile of v2, /device:TPU:8, one launch (start us, length us, event | category | flops | bytes accessed | tf_op | source)
XLA Modules:
  0.0 160.8 jit_solution(11738262371637041580)
XLA Ops:
  0.6 1.6 collective-permute-start
  2.2 3.9 %collective-permute-start.6 = (bf16[48,2048]{1,0:T(8,128)(2,1)}, bf16[48,2048]{1,0:T(8,128)(2,1)S(1)}, u32[]{:S(2)}, u32[]{:S(2)}) collective-permute-start(bf16[48,2048]{1,0:T(8,128)(2,1)} %bitcast.9), channel_id=1, source_target_pairs={{0,16},{8,24},{16,0},{24,8},{32,48},{40,56},{48,32},{56,40},{64,80... | collective-permute-start | bytes 589832 | tf_op jit(solution)/shard_map/ppermute | solution.py:56
  6.8 1.3 collective-permute-start.4
  8.1 2.3 %collective-permute-start.3 = (bf16[48,2048]{1,0:T(8,128)(2,1)}, bf16[48,2048]{1,0:T(8,128)(2,1)S(1)}, u32[]{:S(2)}, u32[]{:S(2)}) collective-permute-start(bf16[48,2048]{1,0:T(8,128)(2,1)} %bitcast.12), channel_id=1, source_target_pairs={{0,64},{8,72},{16,80},{24,88},{32,96},{40,104},{48,112},{56,120},{... | collective-permute-start | bytes 589832 | tf_op jit(solution)/shard_map/ppermute | solution.py:56
  12.3 2.2 %collective-permute-start.1 = (bf16[192,512]{1,0:T(8,128)(2,1)S(1)}, bf16[192,512]{1,0:T(8,128)(2,1)S(1)}, u32[]{:S(2)}, u32[]{:S(2)}) collective-permute-start(bf16[192,512]{1,0:T(8,128)(2,1)S(1)} %get-tuple-element.59.first), channel_id=1, source_target_pairs={{0,6},{1,7},{2,4},{3,5},{4,2},{5,3},{6,0},{7,1},{8,14},{9,15},{10,... | collective-permute-start | bytes 589832 | tf_op jit(solution)/shard_map/ppermute | solution.py:78
  14.5 1.4 collective-permute-done.5.refs_2_
  16.5 1.6 collective-permute-start.10
  19.5 1.3 collective-permute-start.9
  20.8 2.4 %collective-permute-start.8 = (bf16[48,2048]{1,0:T(8,128)(2,1)S(1)}, bf16[48,2048]{1,0:T(8,128)(2,1)S(1)}, u32[]{:S(2)}, u32[]{:S(2)}) collective-permute-start(bf16[48,2048]{1,0:T(8,128)(2,1)S(1)} %collective-permute-done.3.refs_0_), channel_id=1, source_target_pairs={{0,24},{8,0},{16,8},{24,16},{32,56},{40,32},{48,40},{56,48},{64,88... | collective-permute-start | bytes 589832 | tf_op jit(solution)/shard_map/ppermute | solution.py:56
  24.1 4.6 %collective-permute-done.9.refs_3_ = bf16[48,2048]{1,0:T(8,128)(2,1)S(1)} collective-permute-done((bf16[48,2048]{1,0:T(8,128)(2,1)S(1)}, bf16[48,2048]{1,0:T(8,128)(2,1)S(1)}, u32[]{:S(2)}, u32[]{:S(2)}) %collective-permute-start.9) | collective-permute-done | bytes 196640 | tf_op jit(solution)/shard_map/ppermute | solution.py:56
  28.7 3.1 %collective-permute-done.8.refs_2_ = bf16[48,2048]{1,0:T(8,128)(2,1)S(1)} collective-permute-done((bf16[48,2048]{1,0:T(8,128)(2,1)S(1)}, bf16[48,2048]{1,0:T(8,128)(2,1)S(1)}, u32[]{:S(2)}, u32[]{:S(2)}) %collective-permute-start.8) | collective-permute-done | bytes 196640 | tf_op jit(solution)/shard_map/ppermute | solution.py:56
  32.5 2.0 %collective-permute-done.11.refs_6_ = bf16[48,8192]{1,0:T(8,128)(2,1)S(1)} collective-permute-done((bf16[48,8192]{1,0:T(8,128)(2,1)S(1)}, bf16[48,8192]{1,0:T(8,128)(2,1)S(1)}, u32[]{:S(2)}, u32[]{:S(2)}) %collective-permute-start.11) | collective-permute-done | bytes 786464 | tf_op jit(solution)/shard_map/ppermute | solution.py:56
  34.5 1.4 collective-permute-done.10.refs_5_
  35.9 5.8 %logits.1 = (bf16[768,2048]{1,0:T(8,128)(2,1)S(1)}, f32[512,2048]{1,0:T(8,128)S(1)}, f32[512,2048]{1,0:T(8,128)S(1)}, f32[8,2,512]{2,1,0:T(2,128)S(1)}) custom-call(s32[4]{0:T(128)S(1)} %pad_add_fusion.place, s32[1,2048]{1,0:T(1,128)S(1)} %bitcast.8, bf16[512,768]{1,0:T(8,128)(2,1)S(1)} %get-tuple-element.60.clips, ...), custom_call_target="tpu_custom_call" | custom-call | flops 1610612736 | bytes 20971520 | tf_op jit(solution)/shard_map/logits/pallas_call | solution.py:33
  41.8 9.3 %all_to_all.35.parts = f32[8,2,512]{2,1,0:T(2,128)S(1)} all-to-all(f32[8,2,512]{2,1,0:T(2,128)S(1)} %get-tuple-element.69), channel_id=1, replica_groups=mesh['row'=16,'col'=8] {'col'}, dimensions={0} | all-to-all | bytes 65536 | tf_op jit(solution)/shard_map/all_to_all | solution.py:70
  51.0 2.0 %first_cols.1 = (f32[512,128]{1,0:T(8,128)S(1)}, f32[512,128]{1,0:T(8,128)S(1)}, f32[16,2,2048]{2,1,0:T(2,128)S(1)}) custom-call(f32[512,2048]{1,0:T(8,128)S(1)} %get-tuple-element.67.raised, f32[512,2048]{1,0:T(8,128)S(1)} %get-tuple-element.68.plain, f32[8,2,512]{2,1,0:T(2,128)S(1)} %all_to_all.35.parts), custom_call_target="tpu_custom_call" | custom-call | flops 6291456 | bytes 4194304 | tf_op jit(solution)/shard_map/first_cols/pallas_call | solution.py:33
  53.0 14.4 %all_to_all.36.parts = f32[16,2,2048]{2,1,0:T(2,128)S(1)} all-to-all(f32[16,2,2048]{2,1,0:T(2,128)S(1)} %get-tuple-element.71), channel_id=1, replica_groups=mesh['row'=16,'col'=8] {'row'}, dimensions={0} | all-to-all | bytes 524288 | tf_op jit(solution)/shard_map/all_to_all | solution.py:74
  68.6 7.7 %all_to_all.37.parts = f32[8,1,512]{2,1,0:T(1,128)S(1)} all-to-all(f32[8,1,512]{2,1,0:T(1,128)S(1)} %get-tuple-element.75), channel_id=1, replica_groups=mesh['row'=16,'col'=8] {'col'}, dimensions={0} | all-to-all | bytes 32768 | tf_op jit(solution)/shard_map/all_to_all | solution.py:70
  76.8 11.5 %all_to_all.38.parts = f32[16,1,2048]{2,1,0:T(1,128)S(1)} all-to-all(f32[16,1,2048]{2,1,0:T(1,128)S(1)} %col_step.1), channel_id=1, replica_groups=mesh['row'=16,'col'=8] {'row'}, dimensions={0} | all-to-all | bytes 262144 | tf_op jit(solution)/shard_map/all_to_all | solution.py:74
  88.9 7.7 %all_to_all.39.parts = f32[8,1,512]{2,1,0:T(1,128)S(1)} all-to-all(f32[8,1,512]{2,1,0:T(1,128)S(1)} %row_step.1), channel_id=1, replica_groups=mesh['row'=16,'col'=8] {'col'}, dimensions={0} | all-to-all | bytes 32768 | tf_op jit(solution)/shard_map/all_to_all | solution.py:70
  96.7 1.4 last_col.1
  98.0 11.6 %all_to_all.40.parts = f32[16,2,2048]{2,1,0:T(2,128)S(1)} all-to-all(f32[16,2,2048]{2,1,0:T(2,128)S(1)} %get-tuple-element.77), channel_id=1, replica_groups=mesh['row'=16,'col'=8] {'row'}, dimensions={0} | all-to-all | bytes 524288 | tf_op jit(solution)/shard_map/all_to_all | solution.py:74
  110.9 8.2 %all_to_all.41.parts = f32[8,4,512]{2,1,0:T(4,128)S(1)} all-to-all(f32[8,4,512]{2,1,0:T(4,128)S(1)} %get-tuple-element.80), channel_id=1, replica_groups=mesh['row'=16,'col'=8] {'col'}, dimensions={0} | all-to-all | bytes 131072 | tf_op jit(solution)/shard_map/all_to_all | solution.py:70
  119.1 4.1 %slope.1 = (bf16[512,2048]{1,0:T(8,128)(2,1)S(1)}, f32[1,128]{1,0:T(1,128)S(1)}, s16[3136,128]{1,0:T(8,128)(2,1)S(1)}, s16[3136,128]{1,0:T(8,128)(2,1)S(1)}) custom-call(s32[4]{0:T(128)S(1)} %pad_add_fusion.place, f32[512,2048]{1,0:T(8,128)S(1)} %get-tuple-element.72.joint, f32[512,2048]{1,0:T(8,128)S(1)} %get-tuple-element.68.plain, ...), custom_call_target="tpu_custom_call" | custom-call | flops 805306368 | bytes 12582912 | tf_op jit(solution)/shard_map/slope/pallas_call | solution.py:33
  125.3 1.4 far.1
  126.7 2.6 %clip_share.1 = (f32[256,768]{1,0:T(8,128)S(1)}, s16[272,768]{1,0:T(8,128)(2,1)S(1)}) custom-call(s32[4]{0:T(128)S(1)} %pad_add_fusion.place, bf16[512,2048]{1,0:T(8,128)(2,1)S(1)} %get-tuple-element.84.slope, bf16[768,2048]{1,0:T(8,128)(2,1)S(1)} %get-tuple-element.85.captions), custom_call_target="tpu_custom_call" | custom-call | flops 1610612736 | bytes 8388608 | tf_op jit(solution)/shard_map/clip_share/pallas_call | solution.py:33
  129.8 2.8 %collective-permute-start.16 = (s16[784,128]{1,0:T(8,128)(2,1)S(1)}, s16[784,128]{1,0:T(8,128)(2,1)S(1)}, u32[]{:S(2)}, u32[]{:S(2)}) collective-permute-start(s16[784,128]{1,0:T(8,128)(2,1)S(1)} %get-tuple-element.92), channel_id=1, source_target_pairs={{0,24},{8,0},{16,8},{24,16},{32,56},{40,32},{48,40},{56,48},{64,88... | collective-permute-start | bytes 602120 | tf_op jit(solution)/shard_map/ppermute | solution.py:56
  134.5 7.8 %collective-permute-done.15.refs_0_ = s16[784,128]{1,0:T(8,128)(2,1)S(1)} collective-permute-done((s16[784,128]{1,0:T(8,128)(2,1)S(1)}, s16[784,128]{1,0:T(8,128)(2,1)S(1)}, u32[]{:S(2)}, u32[]{:S(2)}) %collective-permute-start.15) | collective-permute-done | bytes 200736 | tf_op jit(solution)/shard_map/ppermute | solution.py:56
  143.8 4.1 %collective-permute-start.20 = (s16[784,128]{1,0:T(8,128)(2,1)S(1)}, s16[784,128]{1,0:T(8,128)(2,1)S(1)}, u32[]{:S(2)}, u32[]{:S(2)}) collective-permute-start(s16[784,128]{1,0:T(8,128)(2,1)S(1)} %pass_on_y.1), channel_id=1, source_target_pairs={{0,64},{8,72},{16,80},{24,88},{32,96},{40,104},{48,112},{56,120},{... | collective-permute-start | bytes 602120 | tf_op jit(solution)/shard_map/ppermute | solution.py:56
  148.6 1.5 collective-permute-start.23
  150.1 1.7 %collective-permute-start.22 = (s16[784,128]{1,0:T(8,128)(2,1)S(1)}, s16[784,128]{1,0:T(8,128)(2,1)S(1)}, u32[]{:S(2)}, u32[]{:S(2)}) collective-permute-start(s16[784,128]{1,0:T(8,128)(2,1)S(1)} %pass_on_z.4), channel_id=1, source_target_pairs={{0,24},{8,0},{16,8},{24,16},{32,56},{40,32},{48,40},{56,48},{64,88... | collective-permute-start | bytes 602120 | tf_op jit(solution)/shard_map/ppermute | solution.py:56
  153.5 4.9 %collective-permute-done.19.came = s16[80,768]{1,0:T(8,128)(2,1)S(1)} collective-permute-done((s16[80,768]{1,0:T(8,128)(2,1)S(1)}, s16[80,768]{1,0:T(8,128)(2,1)S(1)}, u32[]{:S(2)}, u32[]{:S(2)}) %collective-permute-start.19) | collective-permute-done | bytes 122912 | tf_op jit(solution)/shard_map/ppermute | solution.py:78
  (55 shorter events, 20.3 us)
Async XLA Ops:
  0.6 9.8 %collective-permute-start = (bf16[96,512]{1,0:T(8,128)(2,1)}, bf16[96,512]{1,0:T(8,128)(2,1)S(1)}, u32[]{:S(2)}, u32[]{:S(2)}) collective-permute-start(bf16[96,512]{1,0:T(8,128)(2,1)} %bitcast.14), channel_id=1, source_target_pairs={{0,2},{1,3},{2,0},{3,1},{4,6},{5,7},{6,4},{7,5},{8,10},{9,11},{10,... | collective-permute-start | bytes 294920 | tf_op jit(solution)/shard_map/ppermute | solution.py:78
  2.2 12.3 %collective-permute-start.6 = (bf16[48,2048]{1,0:T(8,128)(2,1)}, bf16[48,2048]{1,0:T(8,128)(2,1)S(1)}, u32[]{:S(2)}, u32[]{:S(2)}) collective-permute-start(bf16[48,2048]{1,0:T(8,128)(2,1)} %bitcast.9), channel_id=1, source_target_pairs={{0,16},{8,24},{16,0},{24,8},{32,48},{40,56},{48,32},{56,40},{64,80... | collective-permute-start | bytes 589832 | tf_op jit(solution)/shard_map/ppermute | solution.py:56
  6.1 9.8 %collective-permute-start.5 = (bf16[48,2048]{1,0:T(8,128)(2,1)}, bf16[48,2048]{1,0:T(8,128)(2,1)S(1)}, u32[]{:S(2)}, u32[]{:S(2)}) collective-permute-start(bf16[48,2048]{1,0:T(8,128)(2,1)} %bitcast.10), channel_id=1, source_target_pairs={{0,24},{8,0},{16,8},{24,16},{32,56},{40,32},{48,40},{56,48},{64,88... | collective-permute-start | bytes 589832 | tf_op jit(solution)/shard_map/ppermute | solution.py:56
  6.8 9.1 %collective-permute-start.4 = (bf16[48,2048]{1,0:T(8,128)(2,1)}, bf16[48,2048]{1,0:T(8,128)(2,1)S(1)}, u32[]{:S(2)}, u32[]{:S(2)}) collective-permute-start(bf16[48,2048]{1,0:T(8,128)(2,1)} %bitcast.11), channel_id=1, source_target_pairs={{0,8},{8,16},{16,24},{24,0},{32,40},{40,48},{48,56},{56,32},{64,72... | collective-permute-start | bytes 589832 | tf_op jit(solution)/shard_map/ppermute | solution.py:56
  8.1 7.8 %collective-permute-start.3 = (bf16[48,2048]{1,0:T(8,128)(2,1)}, bf16[48,2048]{1,0:T(8,128)(2,1)S(1)}, u32[]{:S(2)}, u32[]{:S(2)}) collective-permute-start(bf16[48,2048]{1,0:T(8,128)(2,1)} %bitcast.12), channel_id=1, source_target_pairs={{0,64},{8,72},{16,80},{24,88},{32,96},{40,104},{48,112},{56,120},{... | collective-permute-start | bytes 589832 | tf_op jit(solution)/shard_map/ppermute | solution.py:56
  10.4 1.0 copy-start
  11.4 0.9 copy-start.1
  12.3 10.9 %copy-start.2 = (s32[2048]{0:T(1024)S(1)}, s32[2048]{0:T(1024)}, u32[]{:S(2)}) copy-start(s32[2048]{0:T(1024)} %param.5) | copy-start | bytes 24580
  12.3 7.0 %collective-permute-start.1 = (bf16[192,512]{1,0:T(8,128)(2,1)S(1)}, bf16[192,512]{1,0:T(8,128)(2,1)S(1)}, u32[]{:S(2)}, u32[]{:S(2)}) collective-permute-start(bf16[192,512]{1,0:T(8,128)(2,1)S(1)} %get-tuple-element.59.first), channel_id=1, source_target_pairs={{0,6},{1,7},{2,4},{3,5},{4,2},{5,3},{6,0},{7,1},{8,14},{9,15},{10,... | collective-permute-start | bytes 589832 | tf_op jit(solution)/shard_map/ppermute | solution.py:78
  16.0 18.5 %collective-permute-start.11 = (bf16[48,8192]{1,0:T(8,128)(2,1)S(1)}, bf16[48,8192]{1,0:T(8,128)(2,1)S(1)}, u32[]{:S(2)}, u32[]{:S(2)}) collective-permute-start(bf16[48,8192]{1,0:T(8,128)(2,1)S(1)} %join.1.refs_4_), channel_id=1, source_target_pairs={{0,96},{8,104},{16,112},{24,120},{32,0},{40,8},{48,16},{56,24},{64... | collective-permute-start | bytes 2359304 | tf_op jit(solution)/shard_map/ppermute | solution.py:56
  16.5 19.5 %collective-permute-start.10 = (bf16[48,8192]{1,0:T(8,128)(2,1)S(1)}, bf16[48,8192]{1,0:T(8,128)(2,1)S(1)}, u32[]{:S(2)}, u32[]{:S(2)}) collective-permute-start(bf16[48,8192]{1,0:T(8,128)(2,1)S(1)} %join.1.refs_4_), channel_id=1, source_target_pairs={{0,32},{8,40},{16,48},{24,56},{32,64},{40,72},{48,80},{56,88},{64,... | collective-permute-start | bytes 2359304 | tf_op jit(solution)/shard_map/ppermute | solution.py:56
  19.3 3.9 %collective-permute-start.2 = (bf16[384,512]{1,0:T(8,128)(2,1)S(1)}, bf16[384,512]{1,0:T(8,128)(2,1)S(1)}, u32[]{:S(2)}, u32[]{:S(2)}) collective-permute-start(bf16[384,512]{1,0:T(8,128)(2,1)S(1)} %pair.1.here), channel_id=1, source_target_pairs={{0,1},{1,0},{2,3},{3,2},{4,5},{5,4},{6,7},{7,6},{8,9},{9,8},{10,11... | collective-permute-start | bytes 1179656 | tf_op jit(solution)/shard_map/ppermute | solution.py:78
  19.5 9.2 %collective-permute-start.9 = (bf16[48,2048]{1,0:T(8,128)(2,1)S(1)}, bf16[48,2048]{1,0:T(8,128)(2,1)S(1)}, u32[]{:S(2)}, u32[]{:S(2)}) collective-permute-start(bf16[48,2048]{1,0:T(8,128)(2,1)S(1)} %collective-permute-done.3.refs_0_), channel_id=1, source_target_pairs={{0,16},{8,24},{16,0},{24,8},{32,48},{40,56},{48,32},{56,40},{64,80... | collective-permute-start | bytes 589832 | tf_op jit(solution)/shard_map/ppermute | solution.py:56
  20.8 11.0 %collective-permute-start.8 = (bf16[48,2048]{1,0:T(8,128)(2,1)S(1)}, bf16[48,2048]{1,0:T(8,128)(2,1)S(1)}, u32[]{:S(2)}, u32[]{:S(2)}) collective-permute-start(bf16[48,2048]{1,0:T(8,128)(2,1)S(1)} %collective-permute-done.3.refs_0_), channel_id=1, source_target_pairs={{0,24},{8,0},{16,8},{24,16},{32,56},{40,32},{48,40},{56,48},{64,88... | collective-permute-start | bytes 589832 | tf_op jit(solution)/shard_map/ppermute | solution.py:56
  23.2 9.3 %collective-permute-start.7 = (bf16[48,2048]{1,0:T(8,128)(2,1)S(1)}, bf16[48,2048]{1,0:T(8,128)(2,1)S(1)}, u32[]{:S(2)}, u32[]{:S(2)}) collective-permute-start(bf16[48,2048]{1,0:T(8,128)(2,1)S(1)} %collective-permute-done.3.refs_0_), channel_id=1, source_target_pairs={{0,8},{8,16},{16,24},{24,0},{32,40},{40,48},{48,56},{56,32},{64,72... | collective-permute-start | bytes 589832 | tf_op jit(solution)/shard_map/ppermute | solution.py:56
  123.2 19.7 %collective-permute-start.13 = (s16[3136,128]{1,0:T(8,128)(2,1)S(1)}, s16[3136,128]{1,0:T(8,128)(2,1)S(1)}, u32[]{:S(2)}, u32[]{:S(2)}) collective-permute-start(s16[3136,128]{1,0:T(8,128)(2,1)S(1)} %get-tuple-element.89), channel_id=1, source_target_pairs={{0,32},{8,40},{16,48},{24,56},{32,64},{40,72},{48,80},{56,88},{64,... | collective-permute-start | bytes 2408456 | tf_op jit(solution)/shard_map/ppermute | solution.py:56
  124.3 19.2 %collective-permute-start.14 = (s16[3136,128]{1,0:T(8,128)(2,1)S(1)}, s16[3136,128]{1,0:T(8,128)(2,1)S(1)}, u32[]{:S(2)}, u32[]{:S(2)}) collective-permute-start(s16[3136,128]{1,0:T(8,128)(2,1)S(1)} %get-tuple-element.90), channel_id=1, source_target_pairs={{0,96},{8,104},{16,112},{24,120},{32,0},{40,8},{48,16},{56,24},{64... | collective-permute-start | bytes 2408456 | tf_op jit(solution)/shard_map/ppermute | solution.py:56
  129.2 3.4 %collective-permute-start.12 = (s16[272,768]{1,0:T(8,128)(2,1)S(1)}, s16[272,768]{1,0:T(8,128)(2,1)S(1)}, u32[]{:S(2)}, u32[]{:S(2)}) collective-permute-start(s16[272,768]{1,0:T(8,128)(2,1)S(1)} %get-tuple-element.86), channel_id=1, source_target_pairs={{0,1},{1,0},{2,3},{3,2},{4,5},{5,4},{6,7},{7,6},{8,9},{9,8},{10,11... | collective-permute-start | bytes 1253384 | tf_op jit(solution)/shard_map/ppermute | solution.py:78
  129.3 12.9 %collective-permute-start.15 = (s16[784,128]{1,0:T(8,128)(2,1)S(1)}, s16[784,128]{1,0:T(8,128)(2,1)S(1)}, u32[]{:S(2)}, u32[]{:S(2)}) collective-permute-start(s16[784,128]{1,0:T(8,128)(2,1)S(1)} %get-tuple-element.91), channel_id=1, source_target_pairs={{0,8},{8,16},{16,24},{24,0},{32,40},{40,48},{48,56},{56,32},{64,72... | collective-permute-start | bytes 602120 | tf_op jit(solution)/shard_map/ppermute | solution.py:56
  129.8 13.0 %collective-permute-start.16 = (s16[784,128]{1,0:T(8,128)(2,1)S(1)}, s16[784,128]{1,0:T(8,128)(2,1)S(1)}, u32[]{:S(2)}, u32[]{:S(2)}) collective-permute-start(s16[784,128]{1,0:T(8,128)(2,1)S(1)} %get-tuple-element.92), channel_id=1, source_target_pairs={{0,24},{8,0},{16,8},{24,16},{32,56},{40,32},{48,40},{56,48},{64,88... | collective-permute-start | bytes 602120 | tf_op jit(solution)/shard_map/ppermute | solution.py:56
  132.6 10.2 %collective-permute-start.17 = (s16[784,128]{1,0:T(8,128)(2,1)S(1)}, s16[784,128]{1,0:T(8,128)(2,1)S(1)}, u32[]{:S(2)}, u32[]{:S(2)}) collective-permute-start(s16[784,128]{1,0:T(8,128)(2,1)S(1)} %get-tuple-element.93), channel_id=1, source_target_pairs={{0,16},{8,24},{16,0},{24,8},{32,48},{40,56},{48,32},{56,40},{64,80... | collective-permute-start | bytes 602120 | tf_op jit(solution)/shard_map/ppermute | solution.py:56
  142.2 9.9 %collective-permute-start.18 = (s16[144,768]{1,0:T(8,128)(2,1)S(1)}, s16[144,768]{1,0:T(8,128)(2,1)S(1)}, u32[]{:S(2)}, u32[]{:S(2)}) collective-permute-start(s16[144,768]{1,0:T(8,128)(2,1)S(1)} %get-tuple-element.100), channel_id=1, source_target_pairs={{0,2},{1,3},{2,0},{3,1},{4,6},{5,7},{6,4},{7,5},{8,10},{9,11},{10,... | collective-permute-start | bytes 663560 | tf_op jit(solution)/shard_map/ppermute | solution.py:78
  143.8 15.5 %collective-permute-start.20 = (s16[784,128]{1,0:T(8,128)(2,1)S(1)}, s16[784,128]{1,0:T(8,128)(2,1)S(1)}, u32[]{:S(2)}, u32[]{:S(2)}) collective-permute-start(s16[784,128]{1,0:T(8,128)(2,1)S(1)} %pass_on_y.1), channel_id=1, source_target_pairs={{0,64},{8,72},{16,80},{24,88},{32,96},{40,104},{48,112},{56,120},{... | collective-permute-start | bytes 602120 | tf_op jit(solution)/shard_map/ppermute | solution.py:56
  148.6 10.7 %collective-permute-start.23 = (s16[784,128]{1,0:T(8,128)(2,1)S(1)}, s16[784,128]{1,0:T(8,128)(2,1)S(1)}, u32[]{:S(2)}, u32[]{:S(2)}) collective-permute-start(s16[784,128]{1,0:T(8,128)(2,1)S(1)} %pass_on_z.5), channel_id=1, source_target_pairs={{0,16},{8,24},{16,0},{24,8},{32,48},{40,56},{48,32},{56,40},{64,80... | collective-permute-start | bytes 602120 | tf_op jit(solution)/shard_map/ppermute | solution.py:56
  150.1 9.2 %collective-permute-start.22 = (s16[784,128]{1,0:T(8,128)(2,1)S(1)}, s16[784,128]{1,0:T(8,128)(2,1)S(1)}, u32[]{:S(2)}, u32[]{:S(2)}) collective-permute-start(s16[784,128]{1,0:T(8,128)(2,1)S(1)} %pass_on_z.4), channel_id=1, source_target_pairs={{0,24},{8,0},{16,8},{24,16},{32,56},{40,32},{48,40},{56,48},{64,88... | collective-permute-start | bytes 602120 | tf_op jit(solution)/shard_map/ppermute | solution.py:56
  151.8 7.9 %collective-permute-start.21 = (s16[784,128]{1,0:T(8,128)(2,1)S(1)}, s16[784,128]{1,0:T(8,128)(2,1)S(1)}, u32[]{:S(2)}, u32[]{:S(2)}) collective-permute-start(s16[784,128]{1,0:T(8,128)(2,1)S(1)} %pass_on_z.3), channel_id=1, source_target_pairs={{0,8},{8,16},{16,24},{24,0},{32,40},{40,48},{48,56},{56,32},{64,72... | collective-permute-start | bytes 602120 | tf_op jit(solution)/shard_map/ppermute | solution.py:56
  152.3 6.2 %collective-permute-start.19 = (s16[80,768]{1,0:T(8,128)(2,1)S(1)}, s16[80,768]{1,0:T(8,128)(2,1)S(1)}, u32[]{:S(2)}, u32[]{:S(2)}) collective-permute-start(s16[80,768]{1,0:T(8,128)(2,1)S(1)} %get-tuple-element.102), channel_id=1, source_target_pairs={{0,6},{1,7},{2,4},{3,5},{4,2},{5,3},{6,0},{7,1},{8,14},{9,15},{10,... | collective-permute-start | bytes 368648 | tf_op jit(solution)/shard_map/ppermute | solution.py:78

commit v3 on v2

--- a/solution.py
+++ b/solution.py
@@ -299,36 +299,38 @@
     copy_out(sums, along(acc[...]))
 
 
-def last_col_kernel(joint, plain, col_lse, parts, scale, sums):
+def last_col_kernel(joint, parts, scale, sums):
     scale[...] = down(1.0 / gathered(parts))
     for t in range(TILES):
-        value = joint[:, tile(t)] * scale[...]
-        total = jnp.sum(value, axis=0, keepdims=True)
-        gap = col_lse[0:1, tile(t)] - plain[:, tile(t)]
-        both = jnp.concatenate([total, jnp.sum(value * gap, axis=0, keepdims=True)])
+        total = jnp.sum(joint[:, tile(t)] * scale[...], axis=0, keepdims=True)
         for k in range(16):
-            sums[k, :, tile(t)] = both
-
-
-def last_row_kernel(joint, plain, row_lse, parts, col_scale, sums, line, acc0, acc1):
-    total = gathered(parts)
-    factor = 0.5 / total[0:1]
+            sums[k, :, tile(t)] = total
+
+
+def last_row_kernel(
+    joint, plain, row_lse, col_lse, row_scale, parts, col_scale, sums, line, acc0, acc1, acc2
+):
+    factor = 0.5 / gathered(parts)
     col_scale[...] = factor
     line[...] = jnp.broadcast_to(factor, line.shape)
-    col_terms = jnp.sum(factor * total[1:2], axis=1, keepdims=True)
 
     def body(rows):
         lse = row_lse[rows, :]
         sum0 = jnp.zeros_like(lse)
         sum1 = jnp.zeros_like(lse)
+        sum2 = jnp.zeros_like(lse)
         for t in range(TILES):
+            logit = plain[rows, tile(t)]
             value = joint[rows, tile(t)] * line[0:1, tile(t)]
             sum0 += value
-            sum1 += value * (lse - plain[rows, tile(t)])
+            sum1 += value * (lse - logit)
+            sum2 += value * (col_lse[0:1, tile(t)] - logit)
         acc0[rows, :] = sum0
         acc1[rows, :] = sum1
+        acc2[rows, :] = sum2 * row_scale[rows, :]
 
     row_chunks(32, body)
+    col_terms = jnp.sum(jnp.sum(acc2[...], axis=0, keepdims=True), axis=1, keepdims=True)
     terms = jnp.broadcast_to(col_terms, (1, ROWS))
     copy_out(sums, jnp.concatenate([along(acc0[...]), along(acc1[...]), terms, terms]))
 
@@ -355,7 +357,7 @@
     total = gathered(parts)
     norm = 1.0 / total[0:1]
     row_terms = jnp.sum(total[1:2] * norm, axis=1, keepdims=True)
-    share = jnp.broadcast_to(row_terms + total[2:3, 0:1] / 16.0, (1, LANES)) / 16384.0
+    share = jnp.broadcast_to(row_terms + total[2:3, 0:1], (1, LANES)) / 16384.0
     own_share[...] = share
     both[...] = row_scale[...] + down(norm)
     line[...] = jnp.broadcast_to(col_scale[...], line.shape)
@@ -536,21 +538,22 @@
     )
     row_scale, sums = call(
         last_col_kernel,
-        [joint, plain, col_lse, col_all(sums)],
-        [pltpu.VMEM((ROWS, LANES), F32), shape((16, 2, COLS))],
+        [joint, col_all(sums)],
+        [pltpu.VMEM((ROWS, LANES), F32), shape((16, 1, COLS))],
         "last_col",
-        flops=4 * area,
-        moved=8 * area,
+        flops=2 * area,
+        moved=4 * area,
     )
     col_scale, sums = call(
         last_row_kernel,
-        [joint, plain, row_lse, row_all(sums)],
+        [joint, plain, row_lse, col_lse, row_scale, row_all(sums)],
         [shape((1, COLS)), shape((8, 4, ROWS))],
         "last_row",
-        [pltpu.VMEM((8, COLS), F32)] + [pltpu.VMEM((ROWS, LANES), F32)] * 2,
-        flops=4 * area,
+        [pltpu.VMEM((8, COLS), F32)] + [pltpu.VMEM((ROWS, LANES), F32)] * 3,
+        flops=8 * area,
         moved=8 * area,
     )
+
     def packed(chunks):
         return shape((chunks * PACKED, LANES), jnp.int16)
 

time: 161 us -> 160 us (level)
  no operation moved by 1% of the time
where the time goes in v3:
time: 160 us
  blocking collectives  69.9 us (44%)
  starting transfers between devices  33.2 us (21%)
  waiting for transfers between devices  28.2 us (18%)
  Pallas kernels  25.6 us (16%)
  local copies, waits for them, and re-layouts  1.85 us (1%)
    all_to_all x3, blocking collectives, row_all(): return lax.all_to_all(copies, 'row', 0, 0, tiled=True)  37.2 us
    all_to_all x4, blocking collectives, col_all(): return lax.all_to_all(copies, 'col', 0, 0, tiled=True)  32.7 us
    ppermute x18, starting transfers between devices, row_shift(): return lax.ppermute(value, 'row', pairs)  27.5 us
    pallas_call x24, Pallas kernels, call(): pl.pallas_call(kernel, grid=grid, out_shape=outs, in_specs=specs or [SM]...  25.6 us
    ppermute x18, waiting for transfers between devices, row_shift(): return lax.ppermute(value, 'row', pairs)  22 us
    ppermute x6, waiting for transfers between devices, swap(): return lax.ppermute(value, 'col', [(c, c ^ bits) for c in range(8)])  6.13 us
    ppermute x6, starting transfers between devices, swap(): return lax.ppermute(value, 'col', [(c, c ^ bits) for c in range(8)])  5.73 us
  transfers between devices with their start and end apart: 24, of which 11 were waited for; matrix products, arithmetic and copies ran while one was open for 0% of the time, Pallas kernels for 5%

profile of v3, /device:TPU:8, one launch (start us, length us, event | category | flops | bytes accessed | tf_op | source)
XLA Modules:
  0.0 159.7 jit_solution(4893830981879867728)
XLA Ops:
  0.6 1.6 collective-permute-start
  2.2 3.9 %collective-permute-start.6 = (bf16[48,2048]{1,0:T(8,128)(2,1)}, bf16[48,2048]{1,0:T(8,128)(2,1)S(1)}, u32[]{:S(2)}, u32[]{:S(2)}) collective-permute-start(bf16[48,2048]{1,0:T(8,128)(2,1)} %bitcast.9), channel_id=1, source_target_pairs={{0,16},{8,24},{16,0},{24,8},{32,48},{40,56},{48,32},{56,40},{64,80... | collective-permute-start | bytes 589832 | tf_op jit(solution)/shard_map/ppermute | solution.py:56
  6.8 1.3 collective-permute-start.4
  8.1 2.3 %collective-permute-start.3 = (bf16[48,2048]{1,0:T(8,128)(2,1)}, bf16[48,2048]{1,0:T(8,128)(2,1)S(1)}, u32[]{:S(2)}, u32[]{:S(2)}) collective-permute-start(bf16[48,2048]{1,0:T(8,128)(2,1)} %bitcast.12), channel_id=1, source_target_pairs={{0,64},{8,72},{16,80},{24,88},{32,96},{40,104},{48,112},{56,120},{... | collective-permute-start | bytes 589832 | tf_op jit(solution)/shard_map/ppermute | solution.py:56
  12.3 2.2 %collective-permute-start.1 = (bf16[192,512]{1,0:T(8,128)(2,1)S(1)}, bf16[192,512]{1,0:T(8,128)(2,1)S(1)}, u32[]{:S(2)}, u32[]{:S(2)}) collective-permute-start(bf16[192,512]{1,0:T(8,128)(2,1)S(1)} %get-tuple-element.59.first), channel_id=1, source_target_pairs={{0,6},{1,7},{2,4},{3,5},{4,2},{5,3},{6,0},{7,1},{8,14},{9,15},{10,... | collective-permute-start | bytes 589832 | tf_op jit(solution)/shard_map/ppermute | solution.py:78
  14.5 1.4 collective-permute-done.5.refs_2_
  16.5 1.6 collective-permute-start.10
  19.5 1.3 collective-permute-start.9
  20.8 2.4 %collective-permute-start.8 = (bf16[48,2048]{1,0:T(8,128)(2,1)S(1)}, bf16[48,2048]{1,0:T(8,128)(2,1)S(1)}, u32[]{:S(2)}, u32[]{:S(2)}) collective-permute-start(bf16[48,2048]{1,0:T(8,128)(2,1)S(1)} %collective-permute-done.3.refs_0_), channel_id=1, source_target_pairs={{0,24},{8,0},{16,8},{24,16},{32,56},{40,32},{48,40},{56,48},{64,88... | collective-permute-start | bytes 589832 | tf_op jit(solution)/shard_map/ppermute | solution.py:56
  24.1 4.6 %collective-permute-done.9.refs_3_ = bf16[48,2048]{1,0:T(8,128)(2,1)S(1)} collective-permute-done((bf16[48,2048]{1,0:T(8,128)(2,1)S(1)}, bf16[48,2048]{1,0:T(8,128)(2,1)S(1)}, u32[]{:S(2)}, u32[]{:S(2)}) %collective-permute-start.9) | collective-permute-done | bytes 196640 | tf_op jit(solution)/shard_map/ppermute | solution.py:56
  28.7 3.1 %collective-permute-done.8.refs_2_ = bf16[48,2048]{1,0:T(8,128)(2,1)S(1)} collective-permute-done((bf16[48,2048]{1,0:T(8,128)(2,1)S(1)}, bf16[48,2048]{1,0:T(8,128)(2,1)S(1)}, u32[]{:S(2)}, u32[]{:S(2)}) %collective-permute-start.8) | collective-permute-done | bytes 196640 | tf_op jit(solution)/shard_map/ppermute | solution.py:56
  32.5 2.0 %collective-permute-done.11.refs_6_ = bf16[48,8192]{1,0:T(8,128)(2,1)S(1)} collective-permute-done((bf16[48,8192]{1,0:T(8,128)(2,1)S(1)}, bf16[48,8192]{1,0:T(8,128)(2,1)S(1)}, u32[]{:S(2)}, u32[]{:S(2)}) %collective-permute-start.11) | collective-permute-done | bytes 786464 | tf_op jit(solution)/shard_map/ppermute | solution.py:56
  34.5 1.4 collective-permute-done.10.refs_5_
  35.9 5.8 %logits.1 = (bf16[768,2048]{1,0:T(8,128)(2,1)S(1)}, f32[512,2048]{1,0:T(8,128)S(1)}, f32[512,2048]{1,0:T(8,128)S(1)}, f32[8,2,512]{2,1,0:T(2,128)S(1)}) custom-call(s32[4]{0:T(128)S(1)} %pad_add_fusion.place, s32[1,2048]{1,0:T(1,128)S(1)} %bitcast.8, bf16[512,768]{1,0:T(8,128)(2,1)S(1)} %get-tuple-element.60.clips, ...), custom_call_target="tpu_custom_call" | custom-call | flops 1610612736 | bytes 20971520 | tf_op jit(solution)/shard_map/logits/pallas_call | solution.py:33
  41.8 9.3 %all_to_all.35.parts = f32[8,2,512]{2,1,0:T(2,128)S(1)} all-to-all(f32[8,2,512]{2,1,0:T(2,128)S(1)} %get-tuple-element.69), channel_id=1, replica_groups=mesh['row'=16,'col'=8] {'col'}, dimensions={0} | all-to-all | bytes 65536 | tf_op jit(solution)/shard_map/all_to_all | solution.py:70
  51.0 2.0 %first_cols.1 = (f32[512,128]{1,0:T(8,128)S(1)}, f32[512,128]{1,0:T(8,128)S(1)}, f32[16,2,2048]{2,1,0:T(2,128)S(1)}) custom-call(f32[512,2048]{1,0:T(8,128)S(1)} %get-tuple-element.67.raised, f32[512,2048]{1,0:T(8,128)S(1)} %get-tuple-element.68.plain, f32[8,2,512]{2,1,0:T(2,128)S(1)} %all_to_all.35.parts), custom_call_target="tpu_custom_call" | custom-call | flops 6291456 | bytes 4194304 | tf_op jit(solution)/shard_map/first_cols/pallas_call | solution.py:33
  53.0 14.4 %all_to_all.36.parts = f32[16,2,2048]{2,1,0:T(2,128)S(1)} all-to-all(f32[16,2,2048]{2,1,0:T(2,128)S(1)} %get-tuple-element.71), channel_id=1, replica_groups=mesh['row'=16,'col'=8] {'row'}, dimensions={0} | all-to-all | bytes 524288 | tf_op jit(solution)/shard_map/all_to_all | solution.py:74
  68.6 7.7 %all_to_all.37.parts = f32[8,1,512]{2,1,0:T(1,128)S(1)} all-to-all(f32[8,1,512]{2,1,0:T(1,128)S(1)} %get-tuple-element.75), channel_id=1, replica_groups=mesh['row'=16,'col'=8] {'col'}, dimensions={0} | all-to-all | bytes 32768 | tf_op jit(solution)/shard_map/all_to_all | solution.py:70
  76.8 11.5 %all_to_all.38.parts = f32[16,1,2048]{2,1,0:T(1,128)S(1)} all-to-all(f32[16,1,2048]{2,1,0:T(1,128)S(1)} %col_step.1), channel_id=1, replica_groups=mesh['row'=16,'col'=8] {'row'}, dimensions={0} | all-to-all | bytes 262144 | tf_op jit(solution)/shard_map/all_to_all | solution.py:74
  88.9 7.7 %all_to_all.39.parts = f32[8,1,512]{2,1,0:T(1,128)S(1)} all-to-all(f32[8,1,512]{2,1,0:T(1,128)S(1)} %row_step.1), channel_id=1, replica_groups=mesh['row'=16,'col'=8] {'col'}, dimensions={0} | all-to-all | bytes 32768 | tf_op jit(solution)/shard_map/all_to_all | solution.py:70
  97.2 11.2 %all_to_all.40.parts = f32[16,1,2048]{2,1,0:T(1,128)S(1)} all-to-all(f32[16,1,2048]{2,1,0:T(1,128)S(1)} %get-tuple-element.77), channel_id=1, replica_groups=mesh['row'=16,'col'=8] {'row'}, dimensions={0} | all-to-all | bytes 262144 | tf_op jit(solution)/shard_map/all_to_all | solution.py:74
  108.4 1.9 %last_row.1 = (f32[1,2048]{1,0:T(1,128)S(1)}, f32[8,4,512]{2,1,0:T(4,128)S(1)}) custom-call(f32[512,2048]{1,0:T(8,128)S(1)} %get-tuple-element.72.joint, f32[512,2048]{1,0:T(8,128)S(1)} %get-tuple-element.68.plain, f32[512,128]{1,0:T(8,128)S(1)} %get-tuple-element.73.row_lse, f32[1,2048]{1,0:T(1,128)S(1)} %get-tuple-element.74.col_lse, ...), custom_call_target="tpu_custom_call" | custom-call | flops 8388608 | bytes 8388608 | tf_op jit(solution)/shard_map/last_row/pallas_call | solution.py:33
  110.3 8.0 %all_to_all.41.parts = f32[8,4,512]{2,1,0:T(4,128)S(1)} all-to-all(f32[8,4,512]{2,1,0:T(4,128)S(1)} %get-tuple-element.80), channel_id=1, replica_groups=mesh['row'=16,'col'=8] {'col'}, dimensions={0} | all-to-all | bytes 131072 | tf_op jit(solution)/shard_map/all_to_all | solution.py:70
  118.3 4.1 %slope.1 = (bf16[512,2048]{1,0:T(8,128)(2,1)S(1)}, f32[1,128]{1,0:T(1,128)S(1)}, s16[3136,128]{1,0:T(8,128)(2,1)S(1)}, s16[3136,128]{1,0:T(8,128)(2,1)S(1)}) custom-call(s32[4]{0:T(128)S(1)} %pad_add_fusion.place, f32[512,2048]{1,0:T(8,128)S(1)} %get-tuple-element.72.joint, f32[512,2048]{1,0:T(8,128)S(1)} %get-tuple-element.68.plain, ...), custom_call_target="tpu_custom_call" | custom-call | flops 805306368 | bytes 12582912 | tf_op jit(solution)/shard_map/slope/pallas_call | solution.py:33
  124.5 1.4 far.1
  125.8 2.6 %clip_share.1 = (f32[256,768]{1,0:T(8,128)S(1)}, s16[272,768]{1,0:T(8,128)(2,1)S(1)}) custom-call(s32[4]{0:T(128)S(1)} %pad_add_fusion.place, bf16[512,2048]{1,0:T(8,128)(2,1)S(1)} %get-tuple-element.84.slope, bf16[768,2048]{1,0:T(8,128)(2,1)S(1)} %get-tuple-element.85.captions), custom_call_target="tpu_custom_call" | custom-call | flops 1610612736 | bytes 8388608 | tf_op jit(solution)/shard_map/clip_share/pallas_call | solution.py:33
  129.0 2.8 %collective-permute-start.16 = (s16[784,128]{1,0:T(8,128)(2,1)S(1)}, s16[784,128]{1,0:T(8,128)(2,1)S(1)}, u32[]{:S(2)}, u32[]{:S(2)}) collective-permute-start(s16[784,128]{1,0:T(8,128)(2,1)S(1)} %get-tuple-element.92), channel_id=1, source_target_pairs={{0,24},{8,0},{16,8},{24,16},{32,56},{40,32},{48,40},{56,48},{64,88... | collective-permute-start | bytes 602120 | tf_op jit(solution)/shard_map/ppermute | solution.py:56
  133.5 7.9 %collective-permute-done.15.refs_0_ = s16[784,128]{1,0:T(8,128)(2,1)S(1)} collective-permute-done((s16[784,128]{1,0:T(8,128)(2,1)S(1)}, s16[784,128]{1,0:T(8,128)(2,1)S(1)}, u32[]{:S(2)}, u32[]{:S(2)}) %collective-permute-start.15) | collective-permute-done | bytes 200736 | tf_op jit(solution)/shard_map/ppermute | solution.py:56
  142.7 4.2 %collective-permute-start.20 = (s16[784,128]{1,0:T(8,128)(2,1)S(1)}, s16[784,128]{1,0:T(8,128)(2,1)S(1)}, u32[]{:S(2)}, u32[]{:S(2)}) collective-permute-start(s16[784,128]{1,0:T(8,128)(2,1)S(1)} %pass_on_y.1), channel_id=1, source_target_pairs={{0,64},{8,72},{16,80},{24,88},{32,96},{40,104},{48,112},{56,120},{... | collective-permute-start | bytes 602120 | tf_op jit(solution)/shard_map/ppermute | solution.py:56
  147.5 1.6 %collective-permute-start.23 = (s16[784,128]{1,0:T(8,128)(2,1)S(1)}, s16[784,128]{1,0:T(8,128)(2,1)S(1)}, u32[]{:S(2)}, u32[]{:S(2)}) collective-permute-start(s16[784,128]{1,0:T(8,128)(2,1)S(1)} %pass_on_z.5), channel_id=1, source_target_pairs={{0,16},{8,24},{16,0},{24,8},{32,48},{40,56},{48,32},{56,40},{64,80... | collective-permute-start | bytes 602120 | tf_op jit(solution)/shard_map/ppermute | solution.py:56
  149.1 1.6 %collective-permute-start.22 = (s16[784,128]{1,0:T(8,128)(2,1)S(1)}, s16[784,128]{1,0:T(8,128)(2,1)S(1)}, u32[]{:S(2)}, u32[]{:S(2)}) collective-permute-start(s16[784,128]{1,0:T(8,128)(2,1)S(1)} %pass_on_z.4), channel_id=1, source_target_pairs={{0,24},{8,0},{16,8},{24,16},{32,56},{40,32},{48,40},{56,48},{64,88... | collective-permute-start | bytes 602120 | tf_op jit(solution)/shard_map/ppermute | solution.py:56
  152.5 4.9 %collective-permute-done.19.came = s16[80,768]{1,0:T(8,128)(2,1)S(1)} collective-permute-done((s16[80,768]{1,0:T(8,128)(2,1)S(1)}, s16[80,768]{1,0:T(8,128)(2,1)S(1)}, u32[]{:S(2)}, u32[]{:S(2)}) %collective-permute-start.19) | collective-permute-done | bytes 122912 | tf_op jit(solution)/shard_map/ppermute | solution.py:78
  (55 shorter events, 19.1 us)
Async XLA Ops:
  0.6 9.8 %collective-permute-start = (bf16[96,512]{1,0:T(8,128)(2,1)}, bf16[96,512]{1,0:T(8,128)(2,1)S(1)}, u32[]{:S(2)}, u32[]{:S(2)}) collective-permute-start(bf16[96,512]{1,0:T(8,128)(2,1)} %bitcast.14), channel_id=1, source_target_pairs={{0,2},{1,3},{2,0},{3,1},{4,6},{5,7},{6,4},{7,5},{8,10},{9,11},{10,... | collective-permute-start | bytes 294920 | tf_op jit(solution)/shard_map/ppermute | solution.py:78
  2.2 12.3 %collective-permute-start.6 = (bf16[48,2048]{1,0:T(8,128)(2,1)}, bf16[48,2048]{1,0:T(8,128)(2,1)S(1)}, u32[]{:S(2)}, u32[]{:S(2)}) collective-permute-start(bf16[48,2048]{1,0:T(8,128)(2,1)} %bitcast.9), channel_id=1, source_target_pairs={{0,16},{8,24},{16,0},{24,8},{32,48},{40,56},{48,32},{56,40},{64,80... | collective-permute-start | bytes 589832 | tf_op jit(solution)/shard_map/ppermute | solution.py:56
  6.1 9.8 %collective-permute-start.5 = (bf16[48,2048]{1,0:T(8,128)(2,1)}, bf16[48,2048]{1,0:T(8,128)(2,1)S(1)}, u32[]{:S(2)}, u32[]{:S(2)}) collective-permute-start(bf16[48,2048]{1,0:T(8,128)(2,1)} %bitcast.10), channel_id=1, source_target_pairs={{0,24},{8,0},{16,8},{24,16},{32,56},{40,32},{48,40},{56,48},{64,88... | collective-permute-start | bytes 589832 | tf_op jit(solution)/shard_map/ppermute | solution.py:56
  6.8 9.1 %collective-permute-start.4 = (bf16[48,2048]{1,0:T(8,128)(2,1)}, bf16[48,2048]{1,0:T(8,128)(2,1)S(1)}, u32[]{:S(2)}, u32[]{:S(2)}) collective-permute-start(bf16[48,2048]{1,0:T(8,128)(2,1)} %bitcast.11), channel_id=1, source_target_pairs={{0,8},{8,16},{16,24},{24,0},{32,40},{40,48},{48,56},{56,32},{64,72... | collective-permute-start | bytes 589832 | tf_op jit(solution)/shard_map/ppermute | solution.py:56
  8.1 7.8 %collective-permute-start.3 = (bf16[48,2048]{1,0:T(8,128)(2,1)}, bf16[48,2048]{1,0:T(8,128)(2,1)S(1)}, u32[]{:S(2)}, u32[]{:S(2)}) collective-permute-start(bf16[48,2048]{1,0:T(8,128)(2,1)} %bitcast.12), channel_id=1, source_target_pairs={{0,64},{8,72},{16,80},{24,88},{32,96},{40,104},{48,112},{56,120},{... | collective-permute-start | bytes 589832 | tf_op jit(solution)/shard_map/ppermute | solution.py:56
  10.4 1.0 copy-start
  11.4 0.9 copy-start.1
  12.3 10.9 %copy-start.2 = (s32[2048]{0:T(1024)S(1)}, s32[2048]{0:T(1024)}, u32[]{:S(2)}) copy-start(s32[2048]{0:T(1024)} %param.5) | copy-start | bytes 24580
  12.3 7.0 %collective-permute-start.1 = (bf16[192,512]{1,0:T(8,128)(2,1)S(1)}, bf16[192,512]{1,0:T(8,128)(2,1)S(1)}, u32[]{:S(2)}, u32[]{:S(2)}) collective-permute-start(bf16[192,512]{1,0:T(8,128)(2,1)S(1)} %get-tuple-element.59.first), channel_id=1, source_target_pairs={{0,6},{1,7},{2,4},{3,5},{4,2},{5,3},{6,0},{7,1},{8,14},{9,15},{10,... | collective-permute-start | bytes 589832 | tf_op jit(solution)/shard_map/ppermute | solution.py:78
  16.0 18.5 %collective-permute-start.11 = (bf16[48,8192]{1,0:T(8,128)(2,1)S(1)}, bf16[48,8192]{1,0:T(8,128)(2,1)S(1)}, u32[]{:S(2)}, u32[]{:S(2)}) collective-permute-start(bf16[48,8192]{1,0:T(8,128)(2,1)S(1)} %join.1.refs_4_), channel_id=1, source_target_pairs={{0,96},{8,104},{16,112},{24,120},{32,0},{40,8},{48,16},{56,24},{64... | collective-permute-start | bytes 2359304 | tf_op jit(solution)/shard_map/ppermute | solution.py:56
  16.5 19.5 %collective-permute-start.10 = (bf16[48,8192]{1,0:T(8,128)(2,1)S(1)}, bf16[48,8192]{1,0:T(8,128)(2,1)S(1)}, u32[]{:S(2)}, u32[]{:S(2)}) collective-permute-start(bf16[48,8192]{1,0:T(8,128)(2,1)S(1)} %join.1.refs_4_), channel_id=1, source_target_pairs={{0,32},{8,40},{16,48},{24,56},{32,64},{40,72},{48,80},{56,88},{64,... | collective-permute-start | bytes 2359304 | tf_op jit(solution)/shard_map/ppermute | solution.py:56
  19.3 3.9 %collective-permute-start.2 = (bf16[384,512]{1,0:T(8,128)(2,1)S(1)}, bf16[384,512]{1,0:T(8,128)(2,1)S(1)}, u32[]{:S(2)}, u32[]{:S(2)}) collective-permute-start(bf16[384,512]{1,0:T(8,128)(2,1)S(1)} %pair.1.here), channel_id=1, source_target_pairs={{0,1},{1,0},{2,3},{3,2},{4,5},{5,4},{6,7},{7,6},{8,9},{9,8},{10,11... | collective-permute-start | bytes 1179656 | tf_op jit(solution)/shard_map/ppermute | solution.py:78
  19.5 9.2 %collective-permute-start.9 = (bf16[48,2048]{1,0:T(8,128)(2,1)S(1)}, bf16[48,2048]{1,0:T(8,128)(2,1)S(1)}, u32[]{:S(2)}, u32[]{:S(2)}) collective-permute-start(bf16[48,2048]{1,0:T(8,128)(2,1)S(1)} %collective-permute-done.3.refs_0_), channel_id=1, source_target_pairs={{0,16},{8,24},{16,0},{24,8},{32,48},{40,56},{48,32},{56,40},{64,80... | collective-permute-start | bytes 589832 | tf_op jit(solution)/shard_map/ppermute | solution.py:56
  20.8 11.0 %collective-permute-start.8 = (bf16[48,2048]{1,0:T(8,128)(2,1)S(1)}, bf16[48,2048]{1,0:T(8,128)(2,1)S(1)}, u32[]{:S(2)}, u32[]{:S(2)}) collective-permute-start(bf16[48,2048]{1,0:T(8,128)(2,1)S(1)} %collective-permute-done.3.refs_0_), channel_id=1, source_target_pairs={{0,24},{8,0},{16,8},{24,16},{32,56},{40,32},{48,40},{56,48},{64,88... | collective-permute-start | bytes 589832 | tf_op jit(solution)/shard_map/ppermute | solution.py:56
  23.2 9.3 %collective-permute-start.7 = (bf16[48,2048]{1,0:T(8,128)(2,1)S(1)}, bf16[48,2048]{1,0:T(8,128)(2,1)S(1)}, u32[]{:S(2)}, u32[]{:S(2)}) collective-permute-start(bf16[48,2048]{1,0:T(8,128)(2,1)S(1)} %collective-permute-done.3.refs_0_), channel_id=1, source_target_pairs={{0,8},{8,16},{16,24},{24,0},{32,40},{40,48},{48,56},{56,32},{64,72... | collective-permute-start | bytes 589832 | tf_op jit(solution)/shard_map/ppermute | solution.py:56
  122.4 19.6 %collective-permute-start.13 = (s16[3136,128]{1,0:T(8,128)(2,1)S(1)}, s16[3136,128]{1,0:T(8,128)(2,1)S(1)}, u32[]{:S(2)}, u32[]{:S(2)}) collective-permute-start(s16[3136,128]{1,0:T(8,128)(2,1)S(1)} %get-tuple-element.89), channel_id=1, source_target_pairs={{0,32},{8,40},{16,48},{24,56},{32,64},{40,72},{48,80},{56,88},{64,... | collective-permute-start | bytes 2408456 | tf_op jit(solution)/shard_map/ppermute | solution.py:56
  123.2 19.2 %collective-permute-start.14 = (s16[3136,128]{1,0:T(8,128)(2,1)S(1)}, s16[3136,128]{1,0:T(8,128)(2,1)S(1)}, u32[]{:S(2)}, u32[]{:S(2)}) collective-permute-start(s16[3136,128]{1,0:T(8,128)(2,1)S(1)} %get-tuple-element.90), channel_id=1, source_target_pairs={{0,96},{8,104},{16,112},{24,120},{32,0},{40,8},{48,16},{56,24},{64... | collective-permute-start | bytes 2408456 | tf_op jit(solution)/shard_map/ppermute | solution.py:56
  128.4 3.4 %collective-permute-start.12 = (s16[272,768]{1,0:T(8,128)(2,1)S(1)}, s16[272,768]{1,0:T(8,128)(2,1)S(1)}, u32[]{:S(2)}, u32[]{:S(2)}) collective-permute-start(s16[272,768]{1,0:T(8,128)(2,1)S(1)} %get-tuple-element.86), channel_id=1, source_target_pairs={{0,1},{1,0},{2,3},{3,2},{4,5},{5,4},{6,7},{7,6},{8,9},{9,8},{10,11... | collective-permute-start | bytes 1253384 | tf_op jit(solution)/shard_map/ppermute | solution.py:78
  128.5 12.9 %collective-permute-start.15 = (s16[784,128]{1,0:T(8,128)(2,1)S(1)}, s16[784,128]{1,0:T(8,128)(2,1)S(1)}, u32[]{:S(2)}, u32[]{:S(2)}) collective-permute-start(s16[784,128]{1,0:T(8,128)(2,1)S(1)} %get-tuple-element.91), channel_id=1, source_target_pairs={{0,8},{8,16},{16,24},{24,0},{32,40},{40,48},{48,56},{56,32},{64,72... | collective-permute-start | bytes 602120 | tf_op jit(solution)/shard_map/ppermute | solution.py:56
  129.0 12.9 %collective-permute-start.16 = (s16[784,128]{1,0:T(8,128)(2,1)S(1)}, s16[784,128]{1,0:T(8,128)(2,1)S(1)}, u32[]{:S(2)}, u32[]{:S(2)}) collective-permute-start(s16[784,128]{1,0:T(8,128)(2,1)S(1)} %get-tuple-element.92), channel_id=1, source_target_pairs={{0,24},{8,0},{16,8},{24,16},{32,56},{40,32},{48,40},{56,48},{64,88... | collective-permute-start | bytes 602120 | tf_op jit(solution)/shard_map/ppermute | solution.py:56
  131.8 10.2 %collective-permute-start.17 = (s16[784,128]{1,0:T(8,128)(2,1)S(1)}, s16[784,128]{1,0:T(8,128)(2,1)S(1)}, u32[]{:S(2)}, u32[]{:S(2)}) collective-permute-start(s16[784,128]{1,0:T(8,128)(2,1)S(1)} %get-tuple-element.93), channel_id=1, source_target_pairs={{0,16},{8,24},{16,0},{24,8},{32,48},{40,56},{48,32},{56,40},{64,80... | collective-permute-start | bytes 602120 | tf_op jit(solution)/shard_map/ppermute | solution.py:56
  141.4 9.7 %collective-permute-start.18 = (s16[144,768]{1,0:T(8,128)(2,1)S(1)}, s16[144,768]{1,0:T(8,128)(2,1)S(1)}, u32[]{:S(2)}, u32[]{:S(2)}) collective-permute-start(s16[144,768]{1,0:T(8,128)(2,1)S(1)} %get-tuple-element.100), channel_id=1, source_target_pairs={{0,2},{1,3},{2,0},{3,1},{4,6},{5,7},{6,4},{7,5},{8,10},{9,11},{10,... | collective-permute-start | bytes 663560 | tf_op jit(solution)/shard_map/ppermute | solution.py:78
  142.7 15.5 %collective-permute-start.20 = (s16[784,128]{1,0:T(8,128)(2,1)S(1)}, s16[784,128]{1,0:T(8,128)(2,1)S(1)}, u32[]{:S(2)}, u32[]{:S(2)}) collective-permute-start(s16[784,128]{1,0:T(8,128)(2,1)S(1)} %pass_on_y.1), channel_id=1, source_target_pairs={{0,64},{8,72},{16,80},{24,88},{32,96},{40,104},{48,112},{56,120},{... | collective-permute-start | bytes 602120 | tf_op jit(solution)/shard_map/ppermute | solution.py:56
  147.5 10.8 %collective-permute-start.23 = (s16[784,128]{1,0:T(8,128)(2,1)S(1)}, s16[784,128]{1,0:T(8,128)(2,1)S(1)}, u32[]{:S(2)}, u32[]{:S(2)}) collective-permute-start(s16[784,128]{1,0:T(8,128)(2,1)S(1)} %pass_on_z.5), channel_id=1, source_target_pairs={{0,16},{8,24},{16,0},{24,8},{32,48},{40,56},{48,32},{56,40},{64,80... | collective-permute-start | bytes 602120 | tf_op jit(solution)/shard_map/ppermute | solution.py:56
  149.1 9.2 %collective-permute-start.22 = (s16[784,128]{1,0:T(8,128)(2,1)S(1)}, s16[784,128]{1,0:T(8,128)(2,1)S(1)}, u32[]{:S(2)}, u32[]{:S(2)}) collective-permute-start(s16[784,128]{1,0:T(8,128)(2,1)S(1)} %pass_on_z.4), channel_id=1, source_target_pairs={{0,24},{8,0},{16,8},{24,16},{32,56},{40,32},{48,40},{56,48},{64,88... | collective-permute-start | bytes 602120 | tf_op jit(solution)/shard_map/ppermute | solution.py:56
  150.7 7.9 %collective-permute-start.21 = (s16[784,128]{1,0:T(8,128)(2,1)S(1)}, s16[784,128]{1,0:T(8,128)(2,1)S(1)}, u32[]{:S(2)}, u32[]{:S(2)}) collective-permute-start(s16[784,128]{1,0:T(8,128)(2,1)S(1)} %pass_on_z.3), channel_id=1, source_target_pairs={{0,8},{8,16},{16,24},{24,0},{32,40},{40,48},{48,56},{56,32},{64,72... | collective-permute-start | bytes 602120 | tf_op jit(solution)/shard_map/ppermute | solution.py:56
  151.2 6.2 %collective-permute-start.19 = (s16[80,768]{1,0:T(8,128)(2,1)S(1)}, s16[80,768]{1,0:T(8,128)(2,1)S(1)}, u32[]{:S(2)}, u32[]{:S(2)}) collective-permute-start(s16[80,768]{1,0:T(8,128)(2,1)S(1)} %get-tuple-element.102), channel_id=1, source_target_pairs={{0,6},{1,7},{2,4},{3,5},{4,2},{5,3},{6,0},{7,1},{8,14},{9,15},{10,... | collective-permute-start | bytes 368648 | tf_op jit(solution)/shard_map/ppermute | solution.py:78

commit v4 on v3

--- a/solution.py
+++ b/solution.py
@@ -162,7 +162,7 @@
         body(pl.ds(pl.multiple_of(i * step, step), step))
         return carry
 
-    lax.fori_loop(0, ROWS // step, run, 0)
+    lax.fori_loop(0, ROWS // step, run, 0, unroll=4)
 
 
 def local_kernel(captions, clips, beside, captions_out, clips_out):

time: 160 us -> 159 us (level)
  no operation moved by 1% of the time
where the time goes in v4:
time: 159 us; the launch traced here: 158 us
  blocking collectives  69.9 us (44%)
  starting transfers between devices  33.2 us (21%)
  waiting for transfers between devices  28.2 us (18%)
  Pallas kernels  24.3 us (15%)
  local copies, waits for them, and re-layouts  1.85 us (1%)
    all_to_all x3, blocking collectives, row_all(): return lax.all_to_all(copies, 'row', 0, 0, tiled=True)  37.2 us
    all_to_all x4, blocking collectives, col_all(): return lax.all_to_all(copies, 'col', 0, 0, tiled=True)  32.7 us
    ppermute x18, starting transfers between devices, row_shift(): return lax.ppermute(value, 'row', pairs)  27.5 us
    pallas_call x24, Pallas kernels, call(): pl.pallas_call(kernel, grid=grid, out_shape=outs, in_specs=specs or [SM]...  24.3 us
    ppermute x18, waiting for transfers between devices, row_shift(): return lax.ppermute(value, 'row', pairs)  22 us
    ppermute x6, waiting for transfers between devices, swap(): return lax.ppermute(value, 'col', [(c, c ^ bits) for c in range(8)])  6.13 us
    ppermute x6, starting transfers between devices, swap(): return lax.ppermute(value, 'col', [(c, c ^ bits) for c in range(8)])  5.73 us
  transfers between devices with their start and end apart: 24, of which 11 were waited for; matrix products, arithmetic and copies ran while one was open for 0% of the time, Pallas kernels for 5%

profile of v4, /device:TPU:8, one launch (start us, length us, event | category | flops | bytes accessed | tf_op | source)
XLA Modules:
  0.0 158.4 jit_solution(4378543532234014144)
XLA Ops:
  0.6 1.6 collective-permute-start
  2.2 3.9 %collective-permute-start.6 = (bf16[48,2048]{1,0:T(8,128)(2,1)}, bf16[48,2048]{1,0:T(8,128)(2,1)S(1)}, u32[]{:S(2)}, u32[]{:S(2)}) collective-permute-start(bf16[48,2048]{1,0:T(8,128)(2,1)} %bitcast.9), channel_id=1, source_target_pairs={{0,16},{8,24},{16,0},{24,8},{32,48},{40,56},{48,32},{56,40},{64,80... | collective-permute-start | bytes 589832 | tf_op jit(solution)/shard_map/ppermute | solution.py:56
  6.8 1.3 collective-permute-start.4
  8.1 2.3 %collective-permute-start.3 = (bf16[48,2048]{1,0:T(8,128)(2,1)}, bf16[48,2048]{1,0:T(8,128)(2,1)S(1)}, u32[]{:S(2)}, u32[]{:S(2)}) collective-permute-start(bf16[48,2048]{1,0:T(8,128)(2,1)} %bitcast.12), channel_id=1, source_target_pairs={{0,64},{8,72},{16,80},{24,88},{32,96},{40,104},{48,112},{56,120},{... | collective-permute-start | bytes 589832 | tf_op jit(solution)/shard_map/ppermute | solution.py:56
  12.3 2.2 %collective-permute-start.1 = (bf16[192,512]{1,0:T(8,128)(2,1)S(1)}, bf16[192,512]{1,0:T(8,128)(2,1)S(1)}, u32[]{:S(2)}, u32[]{:S(2)}) collective-permute-start(bf16[192,512]{1,0:T(8,128)(2,1)S(1)} %get-tuple-element.59.first), channel_id=1, source_target_pairs={{0,6},{1,7},{2,4},{3,5},{4,2},{5,3},{6,0},{7,1},{8,14},{9,15},{10,... | collective-permute-start | bytes 589832 | tf_op jit(solution)/shard_map/ppermute | solution.py:78
  14.5 1.4 collective-permute-done.5.refs_2_
  16.5 1.6 collective-permute-start.10
  19.5 1.3 collective-permute-start.9
  20.8 2.4 %collective-permute-start.8 = (bf16[48,2048]{1,0:T(8,128)(2,1)S(1)}, bf16[48,2048]{1,0:T(8,128)(2,1)S(1)}, u32[]{:S(2)}, u32[]{:S(2)}) collective-permute-start(bf16[48,2048]{1,0:T(8,128)(2,1)S(1)} %collective-permute-done.3.refs_0_), channel_id=1, source_target_pairs={{0,24},{8,0},{16,8},{24,16},{32,56},{40,32},{48,40},{56,48},{64,88... | collective-permute-start | bytes 589832 | tf_op jit(solution)/shard_map/ppermute | solution.py:56
  24.1 4.6 %collective-permute-done.9.refs_3_ = bf16[48,2048]{1,0:T(8,128)(2,1)S(1)} collective-permute-done((bf16[48,2048]{1,0:T(8,128)(2,1)S(1)}, bf16[48,2048]{1,0:T(8,128)(2,1)S(1)}, u32[]{:S(2)}, u32[]{:S(2)}) %collective-permute-start.9) | collective-permute-done | bytes 196640 | tf_op jit(solution)/shard_map/ppermute | solution.py:56
  28.7 3.1 %collective-permute-done.8.refs_2_ = bf16[48,2048]{1,0:T(8,128)(2,1)S(1)} collective-permute-done((bf16[48,2048]{1,0:T(8,128)(2,1)S(1)}, bf16[48,2048]{1,0:T(8,128)(2,1)S(1)}, u32[]{:S(2)}, u32[]{:S(2)}) %collective-permute-start.8) | collective-permute-done | bytes 196640 | tf_op jit(solution)/shard_map/ppermute | solution.py:56
  32.5 2.0 %collective-permute-done.11.refs_6_ = bf16[48,8192]{1,0:T(8,128)(2,1)S(1)} collective-permute-done((bf16[48,8192]{1,0:T(8,128)(2,1)S(1)}, bf16[48,8192]{1,0:T(8,128)(2,1)S(1)}, u32[]{:S(2)}, u32[]{:S(2)}) %collective-permute-start.11) | collective-permute-done | bytes 786464 | tf_op jit(solution)/shard_map/ppermute | solution.py:56
  34.5 1.4 collective-permute-done.10.refs_5_
  35.9 4.6 %logits.1 = (bf16[768,2048]{1,0:T(8,128)(2,1)S(1)}, f32[512,2048]{1,0:T(8,128)S(1)}, f32[512,2048]{1,0:T(8,128)S(1)}, f32[8,2,512]{2,1,0:T(2,128)S(1)}) custom-call(s32[4]{0:T(128)S(1)} %pad_add_fusion.place, s32[1,2048]{1,0:T(1,128)S(1)} %bitcast.8, bf16[512,768]{1,0:T(8,128)(2,1)S(1)} %get-tuple-element.60.clips, ...), custom_call_target="tpu_custom_call" | custom-call | flops 1610612736 | bytes 20971520 | tf_op jit(solution)/shard_map/logits/pallas_call | solution.py:33
  40.5 9.3 %all_to_all.35.parts = f32[8,2,512]{2,1,0:T(2,128)S(1)} all-to-all(f32[8,2,512]{2,1,0:T(2,128)S(1)} %get-tuple-element.69), channel_id=1, replica_groups=mesh['row'=16,'col'=8] {'col'}, dimensions={0} | all-to-all | bytes 65536 | tf_op jit(solution)/shard_map/all_to_all | solution.py:70
  49.8 2.0 %first_cols.1 = (f32[512,128]{1,0:T(8,128)S(1)}, f32[512,128]{1,0:T(8,128)S(1)}, f32[16,2,2048]{2,1,0:T(2,128)S(1)}) custom-call(f32[512,2048]{1,0:T(8,128)S(1)} %get-tuple-element.67.raised, f32[512,2048]{1,0:T(8,128)S(1)} %get-tuple-element.68.plain, f32[8,2,512]{2,1,0:T(2,128)S(1)} %all_to_all.35.parts), custom_call_target="tpu_custom_call" | custom-call | flops 6291456 | bytes 4194304 | tf_op jit(solution)/shard_map/first_cols/pallas_call | solution.py:33
  51.8 14.4 %all_to_all.36.parts = f32[16,2,2048]{2,1,0:T(2,128)S(1)} all-to-all(f32[16,2,2048]{2,1,0:T(2,128)S(1)} %get-tuple-element.71), channel_id=1, replica_groups=mesh['row'=16,'col'=8] {'row'}, dimensions={0} | all-to-all | bytes 524288 | tf_op jit(solution)/shard_map/all_to_all | solution.py:74
  67.5 7.7 %all_to_all.37.parts = f32[8,1,512]{2,1,0:T(1,128)S(1)} all-to-all(f32[8,1,512]{2,1,0:T(1,128)S(1)} %get-tuple-element.75), channel_id=1, replica_groups=mesh['row'=16,'col'=8] {'col'}, dimensions={0} | all-to-all | bytes 32768 | tf_op jit(solution)/shard_map/all_to_all | solution.py:70
  75.7 11.5 %all_to_all.38.parts = f32[16,1,2048]{2,1,0:T(1,128)S(1)} all-to-all(f32[16,1,2048]{2,1,0:T(1,128)S(1)} %col_step.1), channel_id=1, replica_groups=mesh['row'=16,'col'=8] {'row'}, dimensions={0} | all-to-all | bytes 262144 | tf_op jit(solution)/shard_map/all_to_all | solution.py:74
  87.8 7.7 %all_to_all.39.parts = f32[8,1,512]{2,1,0:T(1,128)S(1)} all-to-all(f32[8,1,512]{2,1,0:T(1,128)S(1)} %row_step.1), channel_id=1, replica_groups=mesh['row'=16,'col'=8] {'col'}, dimensions={0} | all-to-all | bytes 32768 | tf_op jit(solution)/shard_map/all_to_all | solution.py:70
  96.0 11.2 %all_to_all.40.parts = f32[16,1,2048]{2,1,0:T(1,128)S(1)} all-to-all(f32[16,1,2048]{2,1,0:T(1,128)S(1)} %get-tuple-element.77), channel_id=1, replica_groups=mesh['row'=16,'col'=8] {'row'}, dimensions={0} | all-to-all | bytes 262144 | tf_op jit(solution)/shard_map/all_to_all | solution.py:74
  107.2 1.7 %last_row.1 = (f32[1,2048]{1,0:T(1,128)S(1)}, f32[8,4,512]{2,1,0:T(4,128)S(1)}) custom-call(f32[512,2048]{1,0:T(8,128)S(1)} %get-tuple-element.72.joint, f32[512,2048]{1,0:T(8,128)S(1)} %get-tuple-element.68.plain, f32[512,128]{1,0:T(8,128)S(1)} %get-tuple-element.73.row_lse, f32[1,2048]{1,0:T(1,128)S(1)} %get-tuple-element.74.col_lse, ...), custom_call_target="tpu_custom_call" | custom-call | flops 8388608 | bytes 8388608 | tf_op jit(solution)/shard_map/last_row/pallas_call | solution.py:33
  108.9 8.0 %all_to_all.41.parts = f32[8,4,512]{2,1,0:T(4,128)S(1)} all-to-all(f32[8,4,512]{2,1,0:T(4,128)S(1)} %get-tuple-element.80), channel_id=1, replica_groups=mesh['row'=16,'col'=8] {'col'}, dimensions={0} | all-to-all | bytes 131072 | tf_op jit(solution)/shard_map/all_to_all | solution.py:70
  116.9 4.1 %slope.1 = (bf16[512,2048]{1,0:T(8,128)(2,1)S(1)}, f32[1,128]{1,0:T(1,128)S(1)}, s16[3136,128]{1,0:T(8,128)(2,1)S(1)}, s16[3136,128]{1,0:T(8,128)(2,1)S(1)}) custom-call(s32[4]{0:T(128)S(1)} %pad_add_fusion.place, f32[512,2048]{1,0:T(8,128)S(1)} %get-tuple-element.72.joint, f32[512,2048]{1,0:T(8,128)S(1)} %get-tuple-element.68.plain, ...), custom_call_target="tpu_custom_call" | custom-call | flops 805306368 | bytes 12582912 | tf_op jit(solution)/shard_map/slope/pallas_call | solution.py:33
  123.1 1.4 far.1
  124.5 2.6 %clip_share.1 = (f32[256,768]{1,0:T(8,128)S(1)}, s16[272,768]{1,0:T(8,128)(2,1)S(1)}) custom-call(s32[4]{0:T(128)S(1)} %pad_add_fusion.place, bf16[512,2048]{1,0:T(8,128)(2,1)S(1)} %get-tuple-element.84.slope, bf16[768,2048]{1,0:T(8,128)(2,1)S(1)} %get-tuple-element.85.captions), custom_call_target="tpu_custom_call" | custom-call | flops 1610612736 | bytes 8388608 | tf_op jit(solution)/shard_map/clip_share/pallas_call | solution.py:33
  127.7 2.8 %collective-permute-start.16 = (s16[784,128]{1,0:T(8,128)(2,1)S(1)}, s16[784,128]{1,0:T(8,128)(2,1)S(1)}, u32[]{:S(2)}, u32[]{:S(2)}) collective-permute-start(s16[784,128]{1,0:T(8,128)(2,1)S(1)} %get-tuple-element.92), channel_id=1, source_target_pairs={{0,24},{8,0},{16,8},{24,16},{32,56},{40,32},{48,40},{56,48},{64,88... | collective-permute-start | bytes 602120 | tf_op jit(solution)/shard_map/ppermute | solution.py:56
  132.2 7.9 %collective-permute-done.15.refs_0_ = s16[784,128]{1,0:T(8,128)(2,1)S(1)} collective-permute-done((s16[784,128]{1,0:T(8,128)(2,1)S(1)}, s16[784,128]{1,0:T(8,128)(2,1)S(1)}, u32[]{:S(2)}, u32[]{:S(2)}) %collective-permute-start.15) | collective-permute-done | bytes 200736 | tf_op jit(solution)/shard_map/ppermute | solution.py:56
  141.4 4.2 %collective-permute-start.20 = (s16[784,128]{1,0:T(8,128)(2,1)S(1)}, s16[784,128]{1,0:T(8,128)(2,1)S(1)}, u32[]{:S(2)}, u32[]{:S(2)}) collective-permute-start(s16[784,128]{1,0:T(8,128)(2,1)S(1)} %pass_on_y.1), channel_id=1, source_target_pairs={{0,64},{8,72},{16,80},{24,88},{32,96},{40,104},{48,112},{56,120},{... | collective-permute-start | bytes 602120 | tf_op jit(solution)/shard_map/ppermute | solution.py:56
  146.2 1.6 %collective-permute-start.23 = (s16[784,128]{1,0:T(8,128)(2,1)S(1)}, s16[784,128]{1,0:T(8,128)(2,1)S(1)}, u32[]{:S(2)}, u32[]{:S(2)}) collective-permute-start(s16[784,128]{1,0:T(8,128)(2,1)S(1)} %pass_on_z.5), channel_id=1, source_target_pairs={{0,16},{8,24},{16,0},{24,8},{32,48},{40,56},{48,32},{56,40},{64,80... | collective-permute-start | bytes 602120 | tf_op jit(solution)/shard_map/ppermute | solution.py:56
  147.8 1.6 %collective-permute-start.22 = (s16[784,128]{1,0:T(8,128)(2,1)S(1)}, s16[784,128]{1,0:T(8,128)(2,1)S(1)}, u32[]{:S(2)}, u32[]{:S(2)}) collective-permute-start(s16[784,128]{1,0:T(8,128)(2,1)S(1)} %pass_on_z.4), channel_id=1, source_target_pairs={{0,24},{8,0},{16,8},{24,16},{32,56},{40,32},{48,40},{56,48},{64,88... | collective-permute-start | bytes 602120 | tf_op jit(solution)/shard_map/ppermute | solution.py:56
  151.1 4.9 %collective-permute-done.19.came = s16[80,768]{1,0:T(8,128)(2,1)S(1)} collective-permute-done((s16[80,768]{1,0:T(8,128)(2,1)S(1)}, s16[80,768]{1,0:T(8,128)(2,1)S(1)}, u32[]{:S(2)}, u32[]{:S(2)}) %collective-permute-start.19) | collective-permute-done | bytes 122912 | tf_op jit(solution)/shard_map/ppermute | solution.py:78
  (55 shorter events, 19.2 us)
Async XLA Ops:
  0.6 9.8 %collective-permute-start = (bf16[96,512]{1,0:T(8,128)(2,1)}, bf16[96,512]{1,0:T(8,128)(2,1)S(1)}, u32[]{:S(2)}, u32[]{:S(2)}) collective-permute-start(bf16[96,512]{1,0:T(8,128)(2,1)} %bitcast.14), channel_id=1, source_target_pairs={{0,2},{1,3},{2,0},{3,1},{4,6},{5,7},{6,4},{7,5},{8,10},{9,11},{10,... | collective-permute-start | bytes 294920 | tf_op jit(solution)/shard_map/ppermute | solution.py:78
  2.2 12.3 %collective-permute-start.6 = (bf16[48,2048]{1,0:T(8,128)(2,1)}, bf16[48,2048]{1,0:T(8,128)(2,1)S(1)}, u32[]{:S(2)}, u32[]{:S(2)}) collective-permute-start(bf16[48,2048]{1,0:T(8,128)(2,1)} %bitcast.9), channel_id=1, source_target_pairs={{0,16},{8,24},{16,0},{24,8},{32,48},{40,56},{48,32},{56,40},{64,80... | collective-permute-start | bytes 589832 | tf_op jit(solution)/shard_map/ppermute | solution.py:56
  6.1 9.8 %collective-permute-start.5 = (bf16[48,2048]{1,0:T(8,128)(2,1)}, bf16[48,2048]{1,0:T(8,128)(2,1)S(1)}, u32[]{:S(2)}, u32[]{:S(2)}) collective-permute-start(bf16[48,2048]{1,0:T(8,128)(2,1)} %bitcast.10), channel_id=1, source_target_pairs={{0,24},{8,0},{16,8},{24,16},{32,56},{40,32},{48,40},{56,48},{64,88... | collective-permute-start | bytes 589832 | tf_op jit(solution)/shard_map/ppermute | solution.py:56
  6.8 9.1 %collective-permute-start.4 = (bf16[48,2048]{1,0:T(8,128)(2,1)}, bf16[48,2048]{1,0:T(8,128)(2,1)S(1)}, u32[]{:S(2)}, u32[]{:S(2)}) collective-permute-start(bf16[48,2048]{1,0:T(8,128)(2,1)} %bitcast.11), channel_id=1, source_target_pairs={{0,8},{8,16},{16,24},{24,0},{32,40},{40,48},{48,56},{56,32},{64,72... | collective-permute-start | bytes 589832 | tf_op jit(solution)/shard_map/ppermute | solution.py:56
  8.1 7.8 %collective-permute-start.3 = (bf16[48,2048]{1,0:T(8,128)(2,1)}, bf16[48,2048]{1,0:T(8,128)(2,1)S(1)}, u32[]{:S(2)}, u32[]{:S(2)}) collective-permute-start(bf16[48,2048]{1,0:T(8,128)(2,1)} %bitcast.12), channel_id=1, source_target_pairs={{0,64},{8,72},{16,80},{24,88},{32,96},{40,104},{48,112},{56,120},{... | collective-permute-start | bytes 589832 | tf_op jit(solution)/shard_map/ppermute | solution.py:56
  10.4 1.0 copy-start
  11.4 0.9 copy-start.1
  12.3 10.9 %copy-start.2 = (s32[2048]{0:T(1024)S(1)}, s32[2048]{0:T(1024)}, u32[]{:S(2)}) copy-start(s32[2048]{0:T(1024)} %param.5) | copy-start | bytes 24580
  12.3 7.0 %collective-permute-start.1 = (bf16[192,512]{1,0:T(8,128)(2,1)S(1)}, bf16[192,512]{1,0:T(8,128)(2,1)S(1)}, u32[]{:S(2)}, u32[]{:S(2)}) collective-permute-start(bf16[192,512]{1,0:T(8,128)(2,1)S(1)} %get-tuple-element.59.first), channel_id=1, source_target_pairs={{0,6},{1,7},{2,4},{3,5},{4,2},{5,3},{6,0},{7,1},{8,14},{9,15},{10,... | collective-permute-start | bytes 589832 | tf_op jit(solution)/shard_map/ppermute | solution.py:78
  16.0 18.5 %collective-permute-start.11 = (bf16[48,8192]{1,0:T(8,128)(2,1)S(1)}, bf16[48,8192]{1,0:T(8,128)(2,1)S(1)}, u32[]{:S(2)}, u32[]{:S(2)}) collective-permute-start(bf16[48,8192]{1,0:T(8,128)(2,1)S(1)} %join.1.refs_4_), channel_id=1, source_target_pairs={{0,96},{8,104},{16,112},{24,120},{32,0},{40,8},{48,16},{56,24},{64... | collective-permute-start | bytes 2359304 | tf_op jit(solution)/shard_map/ppermute | solution.py:56
  16.5 19.5 %collective-permute-start.10 = (bf16[48,8192]{1,0:T(8,128)(2,1)S(1)}, bf16[48,8192]{1,0:T(8,128)(2,1)S(1)}, u32[]{:S(2)}, u32[]{:S(2)}) collective-permute-start(bf16[48,8192]{1,0:T(8,128)(2,1)S(1)} %join.1.refs_4_), channel_id=1, source_target_pairs={{0,32},{8,40},{16,48},{24,56},{32,64},{40,72},{48,80},{56,88},{64,... | collective-permute-start | bytes 2359304 | tf_op jit(solution)/shard_map/ppermute | solution.py:56
  19.3 3.9 %collective-permute-start.2 = (bf16[384,512]{1,0:T(8,128)(2,1)S(1)}, bf16[384,512]{1,0:T(8,128)(2,1)S(1)}, u32[]{:S(2)}, u32[]{:S(2)}) collective-permute-start(bf16[384,512]{1,0:T(8,128)(2,1)S(1)} %pair.1.here), channel_id=1, source_target_pairs={{0,1},{1,0},{2,3},{3,2},{4,5},{5,4},{6,7},{7,6},{8,9},{9,8},{10,11... | collective-permute-start | bytes 1179656 | tf_op jit(solution)/shard_map/ppermute | solution.py:78
  19.5 9.2 %collective-permute-start.9 = (bf16[48,2048]{1,0:T(8,128)(2,1)S(1)}, bf16[48,2048]{1,0:T(8,128)(2,1)S(1)}, u32[]{:S(2)}, u32[]{:S(2)}) collective-permute-start(bf16[48,2048]{1,0:T(8,128)(2,1)S(1)} %collective-permute-done.3.refs_0_), channel_id=1, source_target_pairs={{0,16},{8,24},{16,0},{24,8},{32,48},{40,56},{48,32},{56,40},{64,80... | collective-permute-start | bytes 589832 | tf_op jit(solution)/shard_map/ppermute | solution.py:56
  20.8 11.0 %collective-permute-start.8 = (bf16[48,2048]{1,0:T(8,128)(2,1)S(1)}, bf16[48,2048]{1,0:T(8,128)(2,1)S(1)}, u32[]{:S(2)}, u32[]{:S(2)}) collective-permute-start(bf16[48,2048]{1,0:T(8,128)(2,1)S(1)} %collective-permute-done.3.refs_0_), channel_id=1, source_target_pairs={{0,24},{8,0},{16,8},{24,16},{32,56},{40,32},{48,40},{56,48},{64,88... | collective-permute-start | bytes 589832 | tf_op jit(solution)/shard_map/ppermute | solution.py:56
  23.2 9.3 %collective-permute-start.7 = (bf16[48,2048]{1,0:T(8,128)(2,1)S(1)}, bf16[48,2048]{1,0:T(8,128)(2,1)S(1)}, u32[]{:S(2)}, u32[]{:S(2)}) collective-permute-start(bf16[48,2048]{1,0:T(8,128)(2,1)S(1)} %collective-permute-done.3.refs_0_), channel_id=1, source_target_pairs={{0,8},{8,16},{16,24},{24,0},{32,40},{40,48},{48,56},{56,32},{64,72... | collective-permute-start | bytes 589832 | tf_op jit(solution)/shard_map/ppermute | solution.py:56
  121.0 19.6 %collective-permute-start.13 = (s16[3136,128]{1,0:T(8,128)(2,1)S(1)}, s16[3136,128]{1,0:T(8,128)(2,1)S(1)}, u32[]{:S(2)}, u32[]{:S(2)}) collective-permute-start(s16[3136,128]{1,0:T(8,128)(2,1)S(1)} %get-tuple-element.89), channel_id=1, source_target_pairs={{0,32},{8,40},{16,48},{24,56},{32,64},{40,72},{48,80},{56,88},{64,... | collective-permute-start | bytes 2408456 | tf_op jit(solution)/shard_map/ppermute | solution.py:56
  121.9 19.2 %collective-permute-start.14 = (s16[3136,128]{1,0:T(8,128)(2,1)S(1)}, s16[3136,128]{1,0:T(8,128)(2,1)S(1)}, u32[]{:S(2)}, u32[]{:S(2)}) collective-permute-start(s16[3136,128]{1,0:T(8,128)(2,1)S(1)} %get-tuple-element.90), channel_id=1, source_target_pairs={{0,96},{8,104},{16,112},{24,120},{32,0},{40,8},{48,16},{56,24},{64... | collective-permute-start | bytes 2408456 | tf_op jit(solution)/shard_map/ppermute | solution.py:56
  127.1 3.4 %collective-permute-start.12 = (s16[272,768]{1,0:T(8,128)(2,1)S(1)}, s16[272,768]{1,0:T(8,128)(2,1)S(1)}, u32[]{:S(2)}, u32[]{:S(2)}) collective-permute-start(s16[272,768]{1,0:T(8,128)(2,1)S(1)} %get-tuple-element.86), channel_id=1, source_target_pairs={{0,1},{1,0},{2,3},{3,2},{4,5},{5,4},{6,7},{7,6},{8,9},{9,8},{10,11... | collective-permute-start | bytes 1253384 | tf_op jit(solution)/shard_map/ppermute | solution.py:78
  127.2 12.9 %collective-permute-start.15 = (s16[784,128]{1,0:T(8,128)(2,1)S(1)}, s16[784,128]{1,0:T(8,128)(2,1)S(1)}, u32[]{:S(2)}, u32[]{:S(2)}) collective-permute-start(s16[784,128]{1,0:T(8,128)(2,1)S(1)} %get-tuple-element.91), channel_id=1, source_target_pairs={{0,8},{8,16},{16,24},{24,0},{32,40},{40,48},{48,56},{56,32},{64,72... | collective-permute-start | bytes 602120 | tf_op jit(solution)/shard_map/ppermute | solution.py:56
  127.7 13.0 %collective-permute-start.16 = (s16[784,128]{1,0:T(8,128)(2,1)S(1)}, s16[784,128]{1,0:T(8,128)(2,1)S(1)}, u32[]{:S(2)}, u32[]{:S(2)}) collective-permute-start(s16[784,128]{1,0:T(8,128)(2,1)S(1)} %get-tuple-element.92), channel_id=1, source_target_pairs={{0,24},{8,0},{16,8},{24,16},{32,56},{40,32},{48,40},{56,48},{64,88... | collective-permute-start | bytes 602120 | tf_op jit(solution)/shard_map/ppermute | solution.py:56
  130.5 10.2 %collective-permute-start.17 = (s16[784,128]{1,0:T(8,128)(2,1)S(1)}, s16[784,128]{1,0:T(8,128)(2,1)S(1)}, u32[]{:S(2)}, u32[]{:S(2)}) collective-permute-start(s16[784,128]{1,0:T(8,128)(2,1)S(1)} %get-tuple-element.93), channel_id=1, source_target_pairs={{0,16},{8,24},{16,0},{24,8},{32,48},{40,56},{48,32},{56,40},{64,80... | collective-permute-start | bytes 602120 | tf_op jit(solution)/shard_map/ppermute | solution.py:56
  140.1 9.7 %collective-permute-start.18 = (s16[144,768]{1,0:T(8,128)(2,1)S(1)}, s16[144,768]{1,0:T(8,128)(2,1)S(1)}, u32[]{:S(2)}, u32[]{:S(2)}) collective-permute-start(s16[144,768]{1,0:T(8,128)(2,1)S(1)} %get-tuple-element.100), channel_id=1, source_target_pairs={{0,2},{1,3},{2,0},{3,1},{4,6},{5,7},{6,4},{7,5},{8,10},{9,11},{10,... | collective-permute-start | bytes 663560 | tf_op jit(solution)/shard_map/ppermute | solution.py:78
  141.4 15.5 %collective-permute-start.20 = (s16[784,128]{1,0:T(8,128)(2,1)S(1)}, s16[784,128]{1,0:T(8,128)(2,1)S(1)}, u32[]{:S(2)}, u32[]{:S(2)}) collective-permute-start(s16[784,128]{1,0:T(8,128)(2,1)S(1)} %pass_on_y.1), channel_id=1, source_target_pairs={{0,64},{8,72},{16,80},{24,88},{32,96},{40,104},{48,112},{56,120},{... | collective-permute-start | bytes 602120 | tf_op jit(solution)/shard_map/ppermute | solution.py:56
  146.2 10.8 %collective-permute-start.23 = (s16[784,128]{1,0:T(8,128)(2,1)S(1)}, s16[784,128]{1,0:T(8,128)(2,1)S(1)}, u32[]{:S(2)}, u32[]{:S(2)}) collective-permute-start(s16[784,128]{1,0:T(8,128)(2,1)S(1)} %pass_on_z.5), channel_id=1, source_target_pairs={{0,16},{8,24},{16,0},{24,8},{32,48},{40,56},{48,32},{56,40},{64,80... | collective-permute-start | bytes 602120 | tf_op jit(solution)/shard_map/ppermute | solution.py:56
  147.8 9.2 %collective-permute-start.22 = (s16[784,128]{1,0:T(8,128)(2,1)S(1)}, s16[784,128]{1,0:T(8,128)(2,1)S(1)}, u32[]{:S(2)}, u32[]{:S(2)}) collective-permute-start(s16[784,128]{1,0:T(8,128)(2,1)S(1)} %pass_on_z.4), channel_id=1, source_target_pairs={{0,24},{8,0},{16,8},{24,16},{32,56},{40,32},{48,40},{56,48},{64,88... | collective-permute-start | bytes 602120 | tf_op jit(solution)/shard_map/ppermute | solution.py:56
  149.4 7.9 %collective-permute-start.21 = (s16[784,128]{1,0:T(8,128)(2,1)S(1)}, s16[784,128]{1,0:T(8,128)(2,1)S(1)}, u32[]{:S(2)}, u32[]{:S(2)}) collective-permute-start(s16[784,128]{1,0:T(8,128)(2,1)S(1)} %pass_on_z.3), channel_id=1, source_target_pairs={{0,8},{8,16},{16,24},{24,0},{32,40},{40,48},{48,56},{56,32},{64,72... | collective-permute-start | bytes 602120 | tf_op jit(solution)/shard_map/ppermute | solution.py:56
  149.9 6.2 %collective-permute-start.19 = (s16[80,768]{1,0:T(8,128)(2,1)S(1)}, s16[80,768]{1,0:T(8,128)(2,1)S(1)}, u32[]{:S(2)}, u32[]{:S(2)}) collective-permute-start(s16[80,768]{1,0:T(8,128)(2,1)S(1)} %get-tuple-element.102), channel_id=1, source_target_pairs={{0,6},{1,7},{2,4},{3,5},{4,2},{5,3},{6,0},{7,1},{8,14},{9,15},{10,... | collective-permute-start | bytes 368648 | tf_op jit(solution)/shard_map/ppermute | solution.py:78

commit v5 on v4

--- a/solution.py
+++ b/solution.py
@@ -162,7 +162,7 @@
         body(pl.ds(pl.multiple_of(i * step, step), step))
         return carry
 
-    lax.fori_loop(0, ROWS // step, run, 0, unroll=4)
+    lax.fori_loop(0, ROWS // step, run, 0, unroll=8)
 
 
 def local_kernel(captions, clips, beside, captions_out, clips_out):

time: 159 us -> 158 us (level)
  no operation moved by 1% of the time
where the time goes in v5:
time: 158 us
  blocking collectives  69.9 us (44%)
  starting transfers between devices  33.2 us (21%)
  waiting for transfers between devices  28.1 us (18%)
  Pallas kernels  23.6 us (15%)
  local copies, waits for them, and re-layouts  1.85 us (1%)
    all_to_all x3, blocking collectives, row_all(): return lax.all_to_all(copies, 'row', 0, 0, tiled=True)  37.2 us
    all_to_all x4, blocking collectives, col_all(): return lax.all_to_all(copies, 'col', 0, 0, tiled=True)  32.7 us
    ppermute x18, starting transfers between devices, row_shift(): return lax.ppermute(value, 'row', pairs)  27.5 us
    pallas_call x24, Pallas kernels, call(): pl.pallas_call(kernel, grid=grid, out_shape=outs, in_specs=specs or [SM]...  23.6 us
    ppermute x18, waiting for transfers between devices, row_shift(): return lax.ppermute(value, 'row', pairs)  22 us
    ppermute x6, waiting for transfers between devices, swap(): return lax.ppermute(value, 'col', [(c, c ^ bits) for c in range(8)])  6.12 us
    ppermute x6, starting transfers between devices, swap(): return lax.ppermute(value, 'col', [(c, c ^ bits) for c in range(8)])  5.73 us
  transfers between devices with their start and end apart: 24, of which 11 were waited for; matrix products, arithmetic and copies ran while one was open for 0% of the time, Pallas kernels for 5%

profile of v5, /device:TPU:8, one launch (start us, length us, event | category | flops | bytes accessed | tf_op | source)
XLA Modules:
  0.0 157.7 jit_solution(6917513755276667506)
XLA Ops:
  0.6 1.6 collective-permute-start
  2.2 3.9 %collective-permute-start.6 = (bf16[48,2048]{1,0:T(8,128)(2,1)}, bf16[48,2048]{1,0:T(8,128)(2,1)S(1)}, u32[]{:S(2)}, u32[]{:S(2)}) collective-permute-start(bf16[48,2048]{1,0:T(8,128)(2,1)} %bitcast.9), channel_id=1, source_target_pairs={{0,16},{8,24},{16,0},{24,8},{32,48},{40,56},{48,32},{56,40},{64,80... | collective-permute-start | bytes 589832 | tf_op jit(solution)/shard_map/ppermute | solution.py:56
  6.8 1.3 collective-permute-start.4
  8.1 2.3 %collective-permute-start.3 = (bf16[48,2048]{1,0:T(8,128)(2,1)}, bf16[48,2048]{1,0:T(8,128)(2,1)S(1)}, u32[]{:S(2)}, u32[]{:S(2)}) collective-permute-start(bf16[48,2048]{1,0:T(8,128)(2,1)} %bitcast.12), channel_id=1, source_target_pairs={{0,64},{8,72},{16,80},{24,88},{32,96},{40,104},{48,112},{56,120},{... | collective-permute-start | bytes 589832 | tf_op jit(solution)/shard_map/ppermute | solution.py:56
  12.3 2.2 %collective-permute-start.1 = (bf16[192,512]{1,0:T(8,128)(2,1)S(1)}, bf16[192,512]{1,0:T(8,128)(2,1)S(1)}, u32[]{:S(2)}, u32[]{:S(2)}) collective-permute-start(bf16[192,512]{1,0:T(8,128)(2,1)S(1)} %get-tuple-element.59.first), channel_id=1, source_target_pairs={{0,6},{1,7},{2,4},{3,5},{4,2},{5,3},{6,0},{7,1},{8,14},{9,15},{10,... | collective-permute-start | bytes 589832 | tf_op jit(solution)/shard_map/ppermute | solution.py:78
  14.5 1.4 collective-permute-done.5.refs_2_
  16.5 1.6 collective-permute-start.10
  19.5 1.3 collective-permute-start.9
  20.8 2.4 %collective-permute-start.8 = (bf16[48,2048]{1,0:T(8,128)(2,1)S(1)}, bf16[48,2048]{1,0:T(8,128)(2,1)S(1)}, u32[]{:S(2)}, u32[]{:S(2)}) collective-permute-start(bf16[48,2048]{1,0:T(8,128)(2,1)S(1)} %collective-permute-done.3.refs_0_), channel_id=1, source_target_pairs={{0,24},{8,0},{16,8},{24,16},{32,56},{40,32},{48,40},{56,48},{64,88... | collective-permute-start | bytes 589832 | tf_op jit(solution)/shard_map/ppermute | solution.py:56
  24.1 4.6 %collective-permute-done.9.refs_3_ = bf16[48,2048]{1,0:T(8,128)(2,1)S(1)} collective-permute-done((bf16[48,2048]{1,0:T(8,128)(2,1)S(1)}, bf16[48,2048]{1,0:T(8,128)(2,1)S(1)}, u32[]{:S(2)}, u32[]{:S(2)}) %collective-permute-start.9) | collective-permute-done | bytes 196640 | tf_op jit(solution)/shard_map/ppermute | solution.py:56
  28.7 3.1 %collective-permute-done.8.refs_2_ = bf16[48,2048]{1,0:T(8,128)(2,1)S(1)} collective-permute-done((bf16[48,2048]{1,0:T(8,128)(2,1)S(1)}, bf16[48,2048]{1,0:T(8,128)(2,1)S(1)}, u32[]{:S(2)}, u32[]{:S(2)}) %collective-permute-start.8) | collective-permute-done | bytes 196640 | tf_op jit(solution)/shard_map/ppermute | solution.py:56
  32.5 2.0 %collective-permute-done.11.refs_6_ = bf16[48,8192]{1,0:T(8,128)(2,1)S(1)} collective-permute-done((bf16[48,8192]{1,0:T(8,128)(2,1)S(1)}, bf16[48,8192]{1,0:T(8,128)(2,1)S(1)}, u32[]{:S(2)}, u32[]{:S(2)}) %collective-permute-start.11) | collective-permute-done | bytes 786464 | tf_op jit(solution)/shard_map/ppermute | solution.py:56
  34.5 1.4 collective-permute-done.10.refs_5_
  35.9 4.4 %logits.1 = (bf16[768,2048]{1,0:T(8,128)(2,1)S(1)}, f32[512,2048]{1,0:T(8,128)S(1)}, f32[512,2048]{1,0:T(8,128)S(1)}, f32[8,2,512]{2,1,0:T(2,128)S(1)}) custom-call(s32[4]{0:T(128)S(1)} %pad_add_fusion.place, s32[1,2048]{1,0:T(1,128)S(1)} %bitcast.8, bf16[512,768]{1,0:T(8,128)(2,1)S(1)} %get-tuple-element.60.clips, ...), custom_call_target="tpu_custom_call" | custom-call | flops 1610612736 | bytes 20971520 | tf_op jit(solution)/shard_map/logits/pallas_call | solution.py:33
  40.3 9.3 %all_to_all.35.parts = f32[8,2,512]{2,1,0:T(2,128)S(1)} all-to-all(f32[8,2,512]{2,1,0:T(2,128)S(1)} %get-tuple-element.69), channel_id=1, replica_groups=mesh['row'=16,'col'=8] {'col'}, dimensions={0} | all-to-all | bytes 65536 | tf_op jit(solution)/shard_map/all_to_all | solution.py:70
  49.6 2.0 %first_cols.1 = (f32[512,128]{1,0:T(8,128)S(1)}, f32[512,128]{1,0:T(8,128)S(1)}, f32[16,2,2048]{2,1,0:T(2,128)S(1)}) custom-call(f32[512,2048]{1,0:T(8,128)S(1)} %get-tuple-element.67.raised, f32[512,2048]{1,0:T(8,128)S(1)} %get-tuple-element.68.plain, f32[8,2,512]{2,1,0:T(2,128)S(1)} %all_to_all.35.parts), custom_call_target="tpu_custom_call" | custom-call | flops 6291456 | bytes 4194304 | tf_op jit(solution)/shard_map/first_cols/pallas_call | solution.py:33
  51.6 14.4 %all_to_all.36.parts = f32[16,2,2048]{2,1,0:T(2,128)S(1)} all-to-all(f32[16,2,2048]{2,1,0:T(2,128)S(1)} %get-tuple-element.71), channel_id=1, replica_groups=mesh['row'=16,'col'=8] {'row'}, dimensions={0} | all-to-all | bytes 524288 | tf_op jit(solution)/shard_map/all_to_all | solution.py:74
  67.1 7.7 %all_to_all.37.parts = f32[8,1,512]{2,1,0:T(1,128)S(1)} all-to-all(f32[8,1,512]{2,1,0:T(1,128)S(1)} %get-tuple-element.75), channel_id=1, replica_groups=mesh['row'=16,'col'=8] {'col'}, dimensions={0} | all-to-all | bytes 32768 | tf_op jit(solution)/shard_map/all_to_all | solution.py:70
  75.2 11.5 %all_to_all.38.parts = f32[16,1,2048]{2,1,0:T(1,128)S(1)} all-to-all(f32[16,1,2048]{2,1,0:T(1,128)S(1)} %col_step.1), channel_id=1, replica_groups=mesh['row'=16,'col'=8] {'row'}, dimensions={0} | all-to-all | bytes 262144 | tf_op jit(solution)/shard_map/all_to_all | solution.py:74
  87.3 7.7 %all_to_all.39.parts = f32[8,1,512]{2,1,0:T(1,128)S(1)} all-to-all(f32[8,1,512]{2,1,0:T(1,128)S(1)} %row_step.1), channel_id=1, replica_groups=mesh['row'=16,'col'=8] {'col'}, dimensions={0} | all-to-all | bytes 32768 | tf_op jit(solution)/shard_map/all_to_all | solution.py:70
  95.5 11.2 %all_to_all.40.parts = f32[16,1,2048]{2,1,0:T(1,128)S(1)} all-to-all(f32[16,1,2048]{2,1,0:T(1,128)S(1)} %get-tuple-element.77), channel_id=1, replica_groups=mesh['row'=16,'col'=8] {'row'}, dimensions={0} | all-to-all | bytes 262144 | tf_op jit(solution)/shard_map/all_to_all | solution.py:74
  106.7 1.7 %last_row.1 = (f32[1,2048]{1,0:T(1,128)S(1)}, f32[8,4,512]{2,1,0:T(4,128)S(1)}) custom-call(f32[512,2048]{1,0:T(8,128)S(1)} %get-tuple-element.72.joint, f32[512,2048]{1,0:T(8,128)S(1)} %get-tuple-element.68.plain, f32[512,128]{1,0:T(8,128)S(1)} %get-tuple-element.73.row_lse, f32[1,2048]{1,0:T(1,128)S(1)} %get-tuple-element.74.col_lse, ...), custom_call_target="tpu_custom_call" | custom-call | flops 8388608 | bytes 8388608 | tf_op jit(solution)/shard_map/last_row/pallas_call | solution.py:33
  108.4 8.0 %all_to_all.41.parts = f32[8,4,512]{2,1,0:T(4,128)S(1)} all-to-all(f32[8,4,512]{2,1,0:T(4,128)S(1)} %get-tuple-element.80), channel_id=1, replica_groups=mesh['row'=16,'col'=8] {'col'}, dimensions={0} | all-to-all | bytes 131072 | tf_op jit(solution)/shard_map/all_to_all | solution.py:70
  116.4 3.9 %slope.1 = (bf16[512,2048]{1,0:T(8,128)(2,1)S(1)}, f32[1,128]{1,0:T(1,128)S(1)}, s16[3136,128]{1,0:T(8,128)(2,1)S(1)}, s16[3136,128]{1,0:T(8,128)(2,1)S(1)}) custom-call(s32[4]{0:T(128)S(1)} %pad_add_fusion.place, f32[512,2048]{1,0:T(8,128)S(1)} %get-tuple-element.72.joint, f32[512,2048]{1,0:T(8,128)S(1)} %get-tuple-element.68.plain, ...), custom_call_target="tpu_custom_call" | custom-call | flops 805306368 | bytes 12582912 | tf_op jit(solution)/shard_map/slope/pallas_call | solution.py:33
  122.5 1.4 far.1
  123.8 2.6 %clip_share.1 = (f32[256,768]{1,0:T(8,128)S(1)}, s16[272,768]{1,0:T(8,128)(2,1)S(1)}) custom-call(s32[4]{0:T(128)S(1)} %pad_add_fusion.place, bf16[512,2048]{1,0:T(8,128)(2,1)S(1)} %get-tuple-element.84.slope, bf16[768,2048]{1,0:T(8,128)(2,1)S(1)} %get-tuple-element.85.captions), custom_call_target="tpu_custom_call" | custom-call | flops 1610612736 | bytes 8388608 | tf_op jit(solution)/shard_map/clip_share/pallas_call | solution.py:33
  127.1 2.8 %collective-permute-start.16 = (s16[784,128]{1,0:T(8,128)(2,1)S(1)}, s16[784,128]{1,0:T(8,128)(2,1)S(1)}, u32[]{:S(2)}, u32[]{:S(2)}) collective-permute-start(s16[784,128]{1,0:T(8,128)(2,1)S(1)} %get-tuple-element.92), channel_id=1, source_target_pairs={{0,24},{8,0},{16,8},{24,16},{32,56},{40,32},{48,40},{56,48},{64,88... | collective-permute-start | bytes 602120 | tf_op jit(solution)/shard_map/ppermute | solution.py:56
  131.5 7.9 %collective-permute-done.15.refs_0_ = s16[784,128]{1,0:T(8,128)(2,1)S(1)} collective-permute-done((s16[784,128]{1,0:T(8,128)(2,1)S(1)}, s16[784,128]{1,0:T(8,128)(2,1)S(1)}, u32[]{:S(2)}, u32[]{:S(2)}) %collective-permute-start.15) | collective-permute-done | bytes 200736 | tf_op jit(solution)/shard_map/ppermute | solution.py:56
  140.7 4.2 %collective-permute-start.20 = (s16[784,128]{1,0:T(8,128)(2,1)S(1)}, s16[784,128]{1,0:T(8,128)(2,1)S(1)}, u32[]{:S(2)}, u32[]{:S(2)}) collective-permute-start(s16[784,128]{1,0:T(8,128)(2,1)S(1)} %pass_on_y.1), channel_id=1, source_target_pairs={{0,64},{8,72},{16,80},{24,88},{32,96},{40,104},{48,112},{56,120},{... | collective-permute-start | bytes 602120 | tf_op jit(solution)/shard_map/ppermute | solution.py:56
  145.5 1.6 %collective-permute-start.23 = (s16[784,128]{1,0:T(8,128)(2,1)S(1)}, s16[784,128]{1,0:T(8,128)(2,1)S(1)}, u32[]{:S(2)}, u32[]{:S(2)}) collective-permute-start(s16[784,128]{1,0:T(8,128)(2,1)S(1)} %pass_on_z.5), channel_id=1, source_target_pairs={{0,16},{8,24},{16,0},{24,8},{32,48},{40,56},{48,32},{56,40},{64,80... | collective-permute-start | bytes 602120 | tf_op jit(solution)/shard_map/ppermute | solution.py:56
  147.1 1.6 %collective-permute-start.22 = (s16[784,128]{1,0:T(8,128)(2,1)S(1)}, s16[784,128]{1,0:T(8,128)(2,1)S(1)}, u32[]{:S(2)}, u32[]{:S(2)}) collective-permute-start(s16[784,128]{1,0:T(8,128)(2,1)S(1)} %pass_on_z.4), channel_id=1, source_target_pairs={{0,24},{8,0},{16,8},{24,16},{32,56},{40,32},{48,40},{56,48},{64,88... | collective-permute-start | bytes 602120 | tf_op jit(solution)/shard_map/ppermute | solution.py:56
  150.5 4.9 %collective-permute-done.19.came = s16[80,768]{1,0:T(8,128)(2,1)S(1)} collective-permute-done((s16[80,768]{1,0:T(8,128)(2,1)S(1)}, s16[80,768]{1,0:T(8,128)(2,1)S(1)}, u32[]{:S(2)}, u32[]{:S(2)}) %collective-permute-start.19) | collective-permute-done | bytes 122912 | tf_op jit(solution)/shard_map/ppermute | solution.py:78
  (55 shorter events, 19.0 us)
Async XLA Ops:
  0.6 9.8 %collective-permute-start = (bf16[96,512]{1,0:T(8,128)(2,1)}, bf16[96,512]{1,0:T(8,128)(2,1)S(1)}, u32[]{:S(2)}, u32[]{:S(2)}) collective-permute-start(bf16[96,512]{1,0:T(8,128)(2,1)} %bitcast.14), channel_id=1, source_target_pairs={{0,2},{1,3},{2,0},{3,1},{4,6},{5,7},{6,4},{7,5},{8,10},{9,11},{10,... | collective-permute-start | bytes 294920 | tf_op jit(solution)/shard_map/ppermute | solution.py:78
  2.2 12.3 %collective-permute-start.6 = (bf16[48,2048]{1,0:T(8,128)(2,1)}, bf16[48,2048]{1,0:T(8,128)(2,1)S(1)}, u32[]{:S(2)}, u32[]{:S(2)}) collective-permute-start(bf16[48,2048]{1,0:T(8,128)(2,1)} %bitcast.9), channel_id=1, source_target_pairs={{0,16},{8,24},{16,0},{24,8},{32,48},{40,56},{48,32},{56,40},{64,80... | collective-permute-start | bytes 589832 | tf_op jit(solution)/shard_map/ppermute | solution.py:56
  6.1 9.8 %collective-permute-start.5 = (bf16[48,2048]{1,0:T(8,128)(2,1)}, bf16[48,2048]{1,0:T(8,128)(2,1)S(1)}, u32[]{:S(2)}, u32[]{:S(2)}) collective-permute-start(bf16[48,2048]{1,0:T(8,128)(2,1)} %bitcast.10), channel_id=1, source_target_pairs={{0,24},{8,0},{16,8},{24,16},{32,56},{40,32},{48,40},{56,48},{64,88... | collective-permute-start | bytes 589832 | tf_op jit(solution)/shard_map/ppermute | solution.py:56
  6.8 9.1 %collective-permute-start.4 = (bf16[48,2048]{1,0:T(8,128)(2,1)}, bf16[48,2048]{1,0:T(8,128)(2,1)S(1)}, u32[]{:S(2)}, u32[]{:S(2)}) collective-permute-start(bf16[48,2048]{1,0:T(8,128)(2,1)} %bitcast.11), channel_id=1, source_target_pairs={{0,8},{8,16},{16,24},{24,0},{32,40},{40,48},{48,56},{56,32},{64,72... | collective-permute-start | bytes 589832 | tf_op jit(solution)/shard_map/ppermute | solution.py:56
  8.1 7.8 %collective-permute-start.3 = (bf16[48,2048]{1,0:T(8,128)(2,1)}, bf16[48,2048]{1,0:T(8,128)(2,1)S(1)}, u32[]{:S(2)}, u32[]{:S(2)}) collective-permute-start(bf16[48,2048]{1,0:T(8,128)(2,1)} %bitcast.12), channel_id=1, source_target_pairs={{0,64},{8,72},{16,80},{24,88},{32,96},{40,104},{48,112},{56,120},{... | collective-permute-start | bytes 589832 | tf_op jit(solution)/shard_map/ppermute | solution.py:56
  10.4 1.0 copy-start
  11.4 0.9 copy-start.1
  12.3 10.9 %copy-start.2 = (s32[2048]{0:T(1024)S(1)}, s32[2048]{0:T(1024)}, u32[]{:S(2)}) copy-start(s32[2048]{0:T(1024)} %param.5) | copy-start | bytes 24580
  12.3 7.0 %collective-permute-start.1 = (bf16[192,512]{1,0:T(8,128)(2,1)S(1)}, bf16[192,512]{1,0:T(8,128)(2,1)S(1)}, u32[]{:S(2)}, u32[]{:S(2)}) collective-permute-start(bf16[192,512]{1,0:T(8,128)(2,1)S(1)} %get-tuple-element.59.first), channel_id=1, source_target_pairs={{0,6},{1,7},{2,4},{3,5},{4,2},{5,3},{6,0},{7,1},{8,14},{9,15},{10,... | collective-permute-start | bytes 589832 | tf_op jit(solution)/shard_map/ppermute | solution.py:78
  16.0 18.5 %collective-permute-start.11 = (bf16[48,8192]{1,0:T(8,128)(2,1)S(1)}, bf16[48,8192]{1,0:T(8,128)(2,1)S(1)}, u32[]{:S(2)}, u32[]{:S(2)}) collective-permute-start(bf16[48,8192]{1,0:T(8,128)(2,1)S(1)} %join.1.refs_4_), channel_id=1, source_target_pairs={{0,96},{8,104},{16,112},{24,120},{32,0},{40,8},{48,16},{56,24},{64... | collective-permute-start | bytes 2359304 | tf_op jit(solution)/shard_map/ppermute | solution.py:56
  16.5 19.5 %collective-permute-start.10 = (bf16[48,8192]{1,0:T(8,128)(2,1)S(1)}, bf16[48,8192]{1,0:T(8,128)(2,1)S(1)}, u32[]{:S(2)}, u32[]{:S(2)}) collective-permute-start(bf16[48,8192]{1,0:T(8,128)(2,1)S(1)} %join.1.refs_4_), channel_id=1, source_target_pairs={{0,32},{8,40},{16,48},{24,56},{32,64},{40,72},{48,80},{56,88},{64,... | collective-permute-start | bytes 2359304 | tf_op jit(solution)/shard_map/ppermute | solution.py:56
  19.3 3.9 %collective-permute-start.2 = (bf16[384,512]{1,0:T(8,128)(2,1)S(1)}, bf16[384,512]{1,0:T(8,128)(2,1)S(1)}, u32[]{:S(2)}, u32[]{:S(2)}) collective-permute-start(bf16[384,512]{1,0:T(8,128)(2,1)S(1)} %pair.1.here), channel_id=1, source_target_pairs={{0,1},{1,0},{2,3},{3,2},{4,5},{5,4},{6,7},{7,6},{8,9},{9,8},{10,11... | collective-permute-start | bytes 1179656 | tf_op jit(solution)/shard_map/ppermute | solution.py:78
  19.5 9.2 %collective-permute-start.9 = (bf16[48,2048]{1,0:T(8,128)(2,1)S(1)}, bf16[48,2048]{1,0:T(8,128)(2,1)S(1)}, u32[]{:S(2)}, u32[]{:S(2)}) collective-permute-start(bf16[48,2048]{1,0:T(8,128)(2,1)S(1)} %collective-permute-done.3.refs_0_), channel_id=1, source_target_pairs={{0,16},{8,24},{16,0},{24,8},{32,48},{40,56},{48,32},{56,40},{64,80... | collective-permute-start | bytes 589832 | tf_op jit(solution)/shard_map/ppermute | solution.py:56
  20.8 11.0 %collective-permute-start.8 = (bf16[48,2048]{1,0:T(8,128)(2,1)S(1)}, bf16[48,2048]{1,0:T(8,128)(2,1)S(1)}, u32[]{:S(2)}, u32[]{:S(2)}) collective-permute-start(bf16[48,2048]{1,0:T(8,128)(2,1)S(1)} %collective-permute-done.3.refs_0_), channel_id=1, source_target_pairs={{0,24},{8,0},{16,8},{24,16},{32,56},{40,32},{48,40},{56,48},{64,88... | collective-permute-start | bytes 589832 | tf_op jit(solution)/shard_map/ppermute | solution.py:56
  23.2 9.3 %collective-permute-start.7 = (bf16[48,2048]{1,0:T(8,128)(2,1)S(1)}, bf16[48,2048]{1,0:T(8,128)(2,1)S(1)}, u32[]{:S(2)}, u32[]{:S(2)}) collective-permute-start(bf16[48,2048]{1,0:T(8,128)(2,1)S(1)} %collective-permute-done.3.refs_0_), channel_id=1, source_target_pairs={{0,8},{8,16},{16,24},{24,0},{32,40},{40,48},{48,56},{56,32},{64,72... | collective-permute-start | bytes 589832 | tf_op jit(solution)/shard_map/ppermute | solution.py:56
  120.4 19.6 %collective-permute-start.13 = (s16[3136,128]{1,0:T(8,128)(2,1)S(1)}, s16[3136,128]{1,0:T(8,128)(2,1)S(1)}, u32[]{:S(2)}, u32[]{:S(2)}) collective-permute-start(s16[3136,128]{1,0:T(8,128)(2,1)S(1)} %get-tuple-element.89), channel_id=1, source_target_pairs={{0,32},{8,40},{16,48},{24,56},{32,64},{40,72},{48,80},{56,88},{64,... | collective-permute-start | bytes 2408456 | tf_op jit(solution)/shard_map/ppermute | solution.py:56
  121.2 19.2 %collective-permute-start.14 = (s16[3136,128]{1,0:T(8,128)(2,1)S(1)}, s16[3136,128]{1,0:T(8,128)(2,1)S(1)}, u32[]{:S(2)}, u32[]{:S(2)}) collective-permute-start(s16[3136,128]{1,0:T(8,128)(2,1)S(1)} %get-tuple-element.90), channel_id=1, source_target_pairs={{0,96},{8,104},{16,112},{24,120},{32,0},{40,8},{48,16},{56,24},{64... | collective-permute-start | bytes 2408456 | tf_op jit(solution)/shard_map/ppermute | solution.py:56
  126.4 3.4 %collective-permute-start.12 = (s16[272,768]{1,0:T(8,128)(2,1)S(1)}, s16[272,768]{1,0:T(8,128)(2,1)S(1)}, u32[]{:S(2)}, u32[]{:S(2)}) collective-permute-start(s16[272,768]{1,0:T(8,128)(2,1)S(1)} %get-tuple-element.86), channel_id=1, source_target_pairs={{0,1},{1,0},{2,3},{3,2},{4,5},{5,4},{6,7},{7,6},{8,9},{9,8},{10,11... | collective-permute-start | bytes 1253384 | tf_op jit(solution)/shard_map/ppermute | solution.py:78
  126.5 12.9 %collective-permute-start.15 = (s16[784,128]{1,0:T(8,128)(2,1)S(1)}, s16[784,128]{1,0:T(8,128)(2,1)S(1)}, u32[]{:S(2)}, u32[]{:S(2)}) collective-permute-start(s16[784,128]{1,0:T(8,128)(2,1)S(1)} %get-tuple-element.91), channel_id=1, source_target_pairs={{0,8},{8,16},{16,24},{24,0},{32,40},{40,48},{48,56},{56,32},{64,72... | collective-permute-start | bytes 602120 | tf_op jit(solution)/shard_map/ppermute | solution.py:56
  127.1 12.9 %collective-permute-start.16 = (s16[784,128]{1,0:T(8,128)(2,1)S(1)}, s16[784,128]{1,0:T(8,128)(2,1)S(1)}, u32[]{:S(2)}, u32[]{:S(2)}) collective-permute-start(s16[784,128]{1,0:T(8,128)(2,1)S(1)} %get-tuple-element.92), channel_id=1, source_target_pairs={{0,24},{8,0},{16,8},{24,16},{32,56},{40,32},{48,40},{56,48},{64,88... | collective-permute-start | bytes 602120 | tf_op jit(solution)/shard_map/ppermute | solution.py:56
  129.8 10.2 %collective-permute-start.17 = (s16[784,128]{1,0:T(8,128)(2,1)S(1)}, s16[784,128]{1,0:T(8,128)(2,1)S(1)}, u32[]{:S(2)}, u32[]{:S(2)}) collective-permute-start(s16[784,128]{1,0:T(8,128)(2,1)S(1)} %get-tuple-element.93), channel_id=1, source_target_pairs={{0,16},{8,24},{16,0},{24,8},{32,48},{40,56},{48,32},{56,40},{64,80... | collective-permute-start | bytes 602120 | tf_op jit(solution)/shard_map/ppermute | solution.py:56
  139.4 9.7 %collective-permute-start.18 = (s16[144,768]{1,0:T(8,128)(2,1)S(1)}, s16[144,768]{1,0:T(8,128)(2,1)S(1)}, u32[]{:S(2)}, u32[]{:S(2)}) collective-permute-start(s16[144,768]{1,0:T(8,128)(2,1)S(1)} %get-tuple-element.100), channel_id=1, source_target_pairs={{0,2},{1,3},{2,0},{3,1},{4,6},{5,7},{6,4},{7,5},{8,10},{9,11},{10,... | collective-permute-start | bytes 663560 | tf_op jit(solution)/shard_map/ppermute | solution.py:78
  140.7 15.5 %collective-permute-start.20 = (s16[784,128]{1,0:T(8,128)(2,1)S(1)}, s16[784,128]{1,0:T(8,128)(2,1)S(1)}, u32[]{:S(2)}, u32[]{:S(2)}) collective-permute-start(s16[784,128]{1,0:T(8,128)(2,1)S(1)} %pass_on_y.1), channel_id=1, source_target_pairs={{0,64},{8,72},{16,80},{24,88},{32,96},{40,104},{48,112},{56,120},{... | collective-permute-start | bytes 602120 | tf_op jit(solution)/shard_map/ppermute | solution.py:56
  145.5 10.8 %collective-permute-start.23 = (s16[784,128]{1,0:T(8,128)(2,1)S(1)}, s16[784,128]{1,0:T(8,128)(2,1)S(1)}, u32[]{:S(2)}, u32[]{:S(2)}) collective-permute-start(s16[784,128]{1,0:T(8,128)(2,1)S(1)} %pass_on_z.5), channel_id=1, source_target_pairs={{0,16},{8,24},{16,0},{24,8},{32,48},{40,56},{48,32},{56,40},{64,80... | collective-permute-start | bytes 602120 | tf_op jit(solution)/shard_map/ppermute | solution.py:56
  147.1 9.2 %collective-permute-start.22 = (s16[784,128]{1,0:T(8,128)(2,1)S(1)}, s16[784,128]{1,0:T(8,128)(2,1)S(1)}, u32[]{:S(2)}, u32[]{:S(2)}) collective-permute-start(s16[784,128]{1,0:T(8,128)(2,1)S(1)} %pass_on_z.4), channel_id=1, source_target_pairs={{0,24},{8,0},{16,8},{24,16},{32,56},{40,32},{48,40},{56,48},{64,88... | collective-permute-start | bytes 602120 | tf_op jit(solution)/shard_map/ppermute | solution.py:56
  148.7 7.9 %collective-permute-start.21 = (s16[784,128]{1,0:T(8,128)(2,1)S(1)}, s16[784,128]{1,0:T(8,128)(2,1)S(1)}, u32[]{:S(2)}, u32[]{:S(2)}) collective-permute-start(s16[784,128]{1,0:T(8,128)(2,1)S(1)} %pass_on_z.3), channel_id=1, source_target_pairs={{0,8},{8,16},{16,24},{24,0},{32,40},{40,48},{48,56},{56,32},{64,72... | collective-permute-start | bytes 602120 | tf_op jit(solution)/shard_map/ppermute | solution.py:56
  149.2 6.2 %collective-permute-start.19 = (s16[80,768]{1,0:T(8,128)(2,1)S(1)}, s16[80,768]{1,0:T(8,128)(2,1)S(1)}, u32[]{:S(2)}, u32[]{:S(2)}) collective-permute-start(s16[80,768]{1,0:T(8,128)(2,1)S(1)} %get-tuple-element.102), channel_id=1, source_target_pairs={{0,6},{1,7},{2,4},{3,5},{4,2},{5,3},{6,0},{7,1},{8,14},{9,15},{10,... | collective-permute-start | bytes 368648 | tf_op jit(solution)/shard_map/ppermute | solution.py:78
